TPU v7x, 32 devices: a whole 2x2x4 slice. The times are simulated.
32 devices in a mesh: grp: 2 (over y), seq: 16 (over z, x, core).
Axes of the slice: x: 2, y: 2, z: 4, core: 2. Of those that a mesh axis runs over, the one named last changes fastest.
Arguments:
- values: bfloat16 [524288, 768], P(('grp', 'seq')), parts along dimension 0, may hold values from -6 to 6
- gate_in: bfloat16 [1024, 16, 768], P(('grp', 'seq')), parts along dimension 0, may hold values from -6 to 6
- cotangent: bfloat16 [1024, 16, 768], P(('grp', 'seq')), parts along dimension 0, may hold values from -1.1953125 to 1.1953125
- first_factor: bfloat16 [512, 16, 512], P('seq'), may hold values from -0.25 to 0.25
- second_factor: bfloat16 [16, 512, 512], P('seq'), may hold values from -0.25 to 0.25
Outputs:
- mixed: bfloat16 [1024, 16, 768], P(('grp', 'seq')), parts along dimension 0
- values_grad: bfloat16 [524288, 768], P(('grp', 'seq')), parts along dimension 0
- gate_grad: bfloat16 [1024, 16, 768], P(('grp', 'seq')), parts along dimension 0
- first_grad: bfloat16 [1024, 16, 512], P(('grp', 'seq')), parts along dimension 0
- second_grad: bfloat16 [32, 512, 512], P(('grp', 'seq')), parts along dimension 0
There are 2 independent parts, one for each index of `grp`. A program takes and returns all parts, laid end to end along the dimension named above; an argument that names none is the same for every part. Nothing has to cross between parts.
All inputs are finite; a program needn't handle non-finite values.
Results may differ from a plain program's by a relative error of at most 0.0058.
Values may be sent and summed in bfloat16 or wider, within the bound.
No kernel may reach another device: no remote copies, remote signals or barrier semaphores. Data moves between devices by JAX's collectives and lax.ppermute only.
A program may use at most 128 MiB of HBM per device.

v0:
```python
import jax
import jax.numpy as jnp
from jax import lax
from jax.sharding import PartitionSpec as P


def on_device(values, gate_in, cotangent, first_factor, second_factor):
    wide = jnp.float32
    narrow = jnp.bfloat16
    block_len = first_factor.shape[2]
    channels = values.shape[1]
    blocks_x = values.reshape(-1, block_len, channels)
    inner = jnp.einsum("aqp,apc->aqc", first_factor, blocks_x, preferred_element_type=wide).astype(
        narrow
    )
    gated = (gate_in.astype(wide) * cotangent.astype(wide)).astype(narrow)
    inner_t = lax.all_to_all(inner, "seq", split_axis=1, concat_axis=0, tiled=True)
    outer_t = jnp.einsum(
        "qxa,aqc->xqc", second_factor, inner_t, preferred_element_type=wide
    ).astype(narrow)
    outer = lax.all_to_all(outer_t, "seq", split_axis=0, concat_axis=1, tiled=True)
    gated_t = lax.all_to_all(gated, "seq", split_axis=1, concat_axis=0, tiled=True)
    second_grad = jnp.einsum("xqc,aqc->qxa", gated_t, inner_t, preferred_element_type=wide).astype(
        narrow
    )
    back_t = jnp.einsum("qxa,xqc->aqc", second_factor, gated_t, preferred_element_type=wide).astype(
        narrow
    )
    back_inner = lax.all_to_all(back_t, "seq", split_axis=0, concat_axis=1, tiled=True)
    outer_f = outer.astype(wide)
    mixed = (gate_in.astype(wide) * outer_f).astype(narrow)
    gate_grad = (cotangent.astype(wide) * outer_f).astype(narrow)
    first_grad = jnp.einsum(
        "aqc,apc->aqp", back_inner, blocks_x, preferred_element_type=wide
    ).astype(narrow)
    values_grad = (
        jnp.einsum("aqp,aqc->apc", first_factor, back_inner, preferred_element_type=wide)
        .astype(narrow)
        .reshape(-1, channels)
    )
    return (mixed, values_grad, gate_grad, first_grad, second_grad)


def solution(mesh):
    return jax.shard_map(
        on_device,
        mesh=mesh,
        in_specs=(
            P(("grp", "seq"), None),
            P(("grp", "seq"), None, None),
            P(("grp", "seq"), None, None),
            P("seq", None, None),
            P("seq", None, None),
        ),
        out_specs=(
            P(("grp", "seq"), None, None),
            P(("grp", "seq"), None),
            P(("grp", "seq"), None, None),
            P(("grp", "seq"), None, None),
            P(("grp", "seq"), None, None),
        ),
        check_vma=False,
    )
```

profile of v0, /device:TPU:11, one launch (start us, length us, event | category | flops | bytes accessed | tf_op | source)
XLA Modules:
  0.0 154.7 jit_solution(17738439180204688661)
XLA Ops:
  0.6 0.0 copy-start
  0.6 1.0 copy-done
  1.7 10.0 %convolution_convert_fusion.3 = bf16[32,16,768]{2,1,0:T(8,128)(2,1)S(1)} fusion(bf16[32,16,512]{2,1,0:T(8,128)(2,1)S(1)} %copy-done, bf16[32,512,768]{2,1,0:T(8,128)(2,1)} %bitcast.52), kind=kOutput, calls=%fused_computation.9 | convolution fusion | flops 403046400 | bytes 26476544 | tf_op jit(solution)/shard_map/aqp,apc->aqc/dot_general | solution.py:13
  11.7 0.2 copy.21
  11.9 25.6 %all_to_all.57 = bf16[32,16,768]{2,0,1:T(8,128)(2,1)S(1)} all-to-all(bf16[32,16,768]{2,0,1:T(8,128)(2,1)S(1)} %copy.21), channel_id=1, replica_groups=mesh['grp'=2,'seq'=16] {'seq'}, dimensions={1} | all-to-all | bytes 1572864 | tf_op jit(solution)/shard_map/all_to_all | solution.py:17
  37.5 0.9 copy-done.3
  38.4 0.6 fusion.3
  39.0 0.5 broadcast
  39.5 1.2 reduce
  40.8 0.3 copy.42
  41.0 0.2 reshape.49
  41.2 24.0 %all_to_all.58 = bf16[16,2,12288]{2,1,0:T(2,128)(2,1)S(1)} all-to-all(bf16[16,2,12288]{2,1,0:T(2,128)(2,1)S(1)} %reshape.49), channel_id=1, replica_groups=mesh['grp'=2,'seq'=16] {'seq'}, dimensions={0} | all-to-all | bytes 1572864 | tf_op jit(solution)/shard_map/all_to_all | solution.py:21
  65.2 0.7 reshape.50
  66.0 0.1 copy.23
  66.1 1.0 copy-done.1
  67.1 0.2 copy-done.2
  67.3 0.7 fusion.2
  68.1 24.0 %all_to_all.59 = bf16[32,16,768]{2,0,1:T(8,128)(2,1)S(1)} all-to-all(bf16[32,16,768]{2,0,1:T(8,128)(2,1)S(1)} %get-tuple-element.16), channel_id=1, replica_groups=mesh['grp'=2,'seq'=16] {'seq'}, dimensions={1} | all-to-all | bytes 1572864 | tf_op jit(solution)/shard_map/all_to_all | solution.py:22
  92.1 0.9 copy-done.5
  93.0 1.5 fusion.4
  94.4 2.4 %reduce.1 = bf16[512,768]{0,1:T(8,128)(2,1)S(1)} reduce(bf16[512,1,768]{0,2,1:T(8,128)(2,1)} %fusion.4, bf16[]{:T(256)} %broadcast), dimensions={1}, to_apply=%copy.25.reduce_sub_computation | reduce | bytes 1572866 | tf_op jit(solution)/shard_map/convert_element_type | solution.py:26
  96.8 1.2 copy.43
  98.0 2.9 %reshape.51 = bf16[16,2,12288]{2,1,0:T(2,128)(2,1)} reshape(bf16[512,768]{1,0:T(8,128)(2,1)} %copy.43) | data formatting | bytes 1572864
  100.9 5.2 %all-to-all-start.3 = ((bf16[16,2,12288]{2,1,0:T(2,128)(2,1)}), bf16[16,2,12288]{2,1,0:T(2,128)(2,1)}, u32[]{:S(2)}, u32[]{:S(2)}) async-start(bf16[16,2,12288]{2,1,0:T(2,128)(2,1)} %reshape.51), calls=%async_computation.3 | async-start | bytes 1572864 | tf_op jit(solution)/shard_map/all_to_all | solution.py:29
  106.1 1.3 copy.28
  107.5 1.3 copy.27
  108.8 1.4 fusion.5
  110.2 15.3 %all-to-all-done.3 = bf16[16,2,12288]{2,1,0:T(2,128)(2,1)} async-done(((bf16[16,2,12288]{2,1,0:T(2,128)(2,1)}), bf16[16,2,12288]{2,1,0:T(2,128)(2,1)}, u32[]{:S(2)}, u32[]{:S(2)}) %all-to-all-start.3) | async-done | bytes 786464 | tf_op jit(solution)/shard_map/all_to_all | solution.py:29
  125.5 4.4 %reshape.52 = bf16[512,1,768]{2,1,0:T(2,128)(2,1)S(1)} reshape(bf16[16,2,12288]{2,1,0:T(2,128)(2,1)} %all-to-all-done.3) | data formatting | bytes 1572864
  129.9 0.1 copy.29
  130.0 12.4 %convolution_convert_fusion.5 = bf16[32,16,512]{2,1,0:T(8,128)(2,1)} fusion(bf16[32,512,768]{2,1,0:T(8,128)(2,1)} %bitcast.53, bf16[16,32,1,768]{3,1,0,2:T(8,128)(2,1)S(1)} %bitcast.55), kind=kOutput, calls=%fused_computation.13 | convolution fusion | flops 402915328 | bytes 26476544 | tf_op jit(solution)/shard_map/aqc,apc->aqp/dot_general | solution.py:33
  142.3 12.4 %convolution_convert_fusion = bf16[32,768,512]{1,2,0:T(8,128)(2,1)} fusion(bf16[32,16,512]{2,1,0:T(8,128)(2,1)S(1)} %copy-done, bf16[16,32,1,768]{3,1,0,2:T(8,128)(2,1)S(1)} %bitcast.56), kind=kOutput, calls=%fused_computation | convolution fusion | flops 415236096 | bytes 26476544 | tf_op jit(solution)/shard_map/aqp,aqc->apc/dot_general | solution.py:37
  (10 shorter events, 0.0 us)
Async XLA Ops:
  0.6 1.0 copy-start
  11.7 26.7 %copy-start.7 = (bf16[1,512,512]{2,1,0:T(8,128)(2,1)S(1)}, bf16[1,512,512]{2,1,0:T(8,128)(2,1)}, u32[]{:S(2)}) copy-start(bf16[1,512,512]{2,1,0:T(8,128)(2,1)} %param.9) | copy-start | bytes 1572868
  37.5 0.9 copy-start.3
  66.0 1.1 copy-start.1
  66.0 1.4 copy-start.2
  92.1 0.9 copy-start.5
  100.9 24.6 %all-to-all-start.3 = ((bf16[16,2,12288]{2,1,0:T(2,128)(2,1)}), bf16[16,2,12288]{2,1,0:T(2,128)(2,1)}, u32[]{:S(2)}, u32[]{:S(2)}) async-start(bf16[16,2,12288]{2,1,0:T(2,128)(2,1)} %reshape.51), calls=%async_computation.3 | async-start | bytes 1572864 | tf_op jit(solution)/shard_map/all_to_all | solution.py:29
  106.1 2.6 %copy-start.4 = (bf16[32,16,768]{2,0,1:T(8,128)(2,1)S(1)}, bf16[32,16,768]{2,0,1:T(8,128)(2,1)}, u32[]{:S(2)}) copy-start(bf16[32,16,768]{2,0,1:T(8,128)(2,1)} %copy-done.3) | copy-start | bytes 2359300
  106.1 2.6 %copy-start.6 = (bf16[32,16,768]{2,0,1:T(8,128)(2,1)S(1)}, bf16[32,16,768]{2,0,1:T(8,128)(2,1)}, u32[]{:S(2)}) copy-start(bf16[32,16,768]{2,0,1:T(8,128)(2,1)} %copy-done.5) | copy-start | bytes 2359300
where the time goes:
time: 156 us; the launch traced here: 155 us
  blocking collectives  73.5 us (47%)
  matrix products  38.2 us (24%)
  local copies, waits for them, and re-layouts  17.3 us (11%)
  waiting for transfers between devices  15.3 us (10%)
  starting transfers between devices  5.21 us (3%)
  other arithmetic  4.34 us (3%)
    all_to_all x1, blocking collectives, on_device(): lax.all_to_all(inner, 'seq', split_axis=1, concat_axis=0, tiled=True)  25.6 us
    all_to_all x1, blocking collectives, on_device(): lax.all_to_all(outer_t, 'seq', split_axis=0, concat_axis=1, tiled=True)  24 us
    all_to_all x1, blocking collectives, on_device(): lax.all_to_all(gated, 'seq', split_axis=1, concat_axis=0, tiled=True)  24 us
    unnamed x25, local copies, waits for them, and re-layouts  16.5 us
    all_to_all x1, waiting for transfers between devices, on_device(): lax.all_to_all(back_t, 'seq', split_axis=0, concat_axis=1, tiled=True)  15.3 us
    dot_general x1, matrix products, on_device(): jnp.einsum('aqp,aqc->apc', first_factor, back_inner, preferred_element_ty...  12.4 us
    dot_general x1, matrix products, on_device(): jnp.einsum('aqc,apc->aqp', back_inner, blocks_x, preferred_element_type=w...  12.4 us
    dot_general x1, matrix products, on_device(): jnp.einsum('aqp,apc->aqc', first_factor, blocks_x, preferred_element_type...  9.99 us
  transfers between devices with their start and end apart: 1, of which 1 were waited for; matrix products, arithmetic and copies ran while one was open for 3% of the time, Pallas kernels for 0%

commit v1 on v0

v1 whole, which is shorter than its diff:
```python
import functools

import jax
import jax.numpy as jnp
from jax import lax
from jax.experimental import pallas as pl
from jax.experimental.pallas import tpu as pltpu
from jax.sharding import PartitionSpec as P

WIDE = jnp.float32
NARROW = jnp.bfloat16
MIB = 1 << 20
VMEM = pltpu.VMEM
ANY = pl.ANY


def params(mib):
    return pltpu.CompilerParams(vmem_limit_bytes=mib * MIB)


def cost(flops, nbytes):
    return pl.CostEstimate(flops=flops, bytes_accessed=nbytes, transcendentals=0)


def split_matrix(rank, rows, n, order):
    total = rows * n
    shape = (total, total)
    i = lax.broadcasted_iota(jnp.int32, shape, 0)
    j = lax.broadcasted_iota(jnp.int32, shape, 1)
    slab, block = i // rows, i % rows
    k = order(slab)
    return ((j // n == block) & (j % n == (rank ^ k))).astype(NARROW)


def merge_matrix(rank, rows, n, order):
    total = rows * n
    shape = (total, total)
    i = lax.broadcasted_iota(jnp.int32, shape, 0)
    j = lax.broadcasted_iota(jnp.int32, shape, 1)
    slab, block = j // rows, j % rows
    k = order(slab)
    return ((i // n == block) & (i % n == (rank ^ k))).astype(NARROW)


def outer_major(inner):
    return lambda slab: slab


def inner_major(inner, outer):
    return lambda slab: (slab % outer) * inner + slab // outer


def dot(a, b, dims):
    return lax.dot_general(a, b, ((dims[0], dims[1]), ((), ())), preferred_element_type=WIDE)


def gated_kernel(inner, outer, rows, chunks, g_ref, d_ref, *refs):
    out_refs, matrix = refs[:outer], refs[outer]
    n = inner * outer

    @pl.when(pl.program_id(0) == 0)
    def _():
        matrix[...] = split_matrix(lax.axis_index("seq"), rows, n, outer_major(inner))

    gated = (g_ref[...].astype(WIDE) * d_ref[...].astype(WIDE)).astype(NARROW)
    span = inner * rows
    for o in range(outer):
        out_refs[o][...] = dot(matrix[o * span : (o + 1) * span, :], gated, ((1,), (0,))).astype(NARROW)


def gated_slabs(gate_in, cotangent, inner, outer):
    rows, n, channels = gate_in.shape
    total = rows * n
    chunks = 3 if channels % 384 == 0 else 1
    wide = channels // chunks
    span = inner * rows
    out = pl.pallas_call(
        functools.partial(gated_kernel, inner, outer, rows, chunks),
        grid=(chunks,),
        in_specs=[pl.BlockSpec((total, wide), lambda i: (0, i))] * 2,
        out_specs=[pl.BlockSpec((span, wide), lambda i: (0, i))] * outer,
        out_shape=[jax.ShapeDtypeStruct((span, channels), NARROW)] * outer,
        scratch_shapes=[VMEM((total, total), NARROW)],
        compiler_params=params(32),
        cost_estimate=cost(2 * total * total * channels, 6 * total * channels),
        name="gated_slabs",
    )(gate_in.reshape(total, channels), cotangent.reshape(total, channels))
    return [o.reshape(inner, rows, channels) for o in out]


def inner_kernel(inner, outer, slots, group, w_ref, x_ref, *refs):
    out_refs, (kept, buf, sem) = refs[:inner], refs[inner:]
    blocks, n, length = w_ref.shape
    steps = blocks // group
    rows = group * length

    def fetch(i, s):
        return pltpu.make_async_copy(x_ref.at[pl.ds(i * rows, rows), :], buf.at[s], sem.at[s])

    for s in range(slots):
        fetch(s, s).start()
    matrix = split_matrix(lax.axis_index("seq"), blocks, n, inner_major(inner, outer))

    def step(i, carry):
        s = lax.rem(i, slots)
        fetch(i, s).wait()
        for g in range(group):
            u = dot(w_ref[i * group + g], buf[s, g * length : (g + 1) * length, :], ((1,), (0,)))
            kept[pl.ds(pl.multiple_of((i * group + g) * n, n), n), :] = u.astype(NARROW)

        @pl.when(i + slots < steps)
        def _():
            fetch(i + slots, s).start()

        return carry

    lax.fori_loop(0, steps, step, 0)
    span = outer * blocks
    for o in range(inner):
        out_refs[o][...] = dot(matrix[o * span : (o + 1) * span, :], kept[...], ((1,), (0,))).astype(NARROW)


def inner_slabs(first_factor, values, inner, outer):
    blocks, n, length = first_factor.shape
    channels = values.shape[1]
    group = 2 if blocks % 2 == 0 else 1
    slots = min(4, blocks // group)
    span = outer * blocks
    out = pl.pallas_call(
        functools.partial(inner_kernel, inner, outer, slots, group),
        in_specs=[pl.BlockSpec(memory_space=VMEM), pl.BlockSpec(memory_space=ANY)],
        out_specs=[pl.BlockSpec(memory_space=VMEM)] * inner,
        out_shape=[jax.ShapeDtypeStruct((span, channels), NARROW)] * inner,
        scratch_shapes=[
            VMEM((blocks * n, channels), NARROW),
            VMEM((slots, group * length, channels), NARROW),
            pltpu.SemaphoreType.DMA((slots,)),
        ],
        compiler_params=params(32),
        cost_estimate=cost(2 * blocks * n * length * channels, 2 * blocks * length * channels),
        name="inner_slabs",
    )(first_factor, values)
    return [o.reshape(outer, blocks, channels) for o in out]


def mix_kernel(inner, outer, rows, arrive_inner, leave_inner, transpose, parts, s_ref, *refs):
    arrive_n = inner if arrive_inner else outer
    leave_n = inner if leave_inner else outer
    in_refs, out_refs = refs[:arrive_n], refs[arrive_n : arrive_n + leave_n * parts]
    whole_ref, product = refs[arrive_n + leave_n * parts :]
    rank = lax.axis_index("seq")

    def number(group, member, by_inner):
        return member * inner + group if by_inner else group * inner + member

    def place(k):
        return pl.ds(pl.multiple_of((rank ^ k) * rows, rows), rows)

    for a in range(arrive_n):
        for b in range(inner * outer // arrive_n):
            whole_ref[place(number(a, b, arrive_inner)), :] = in_refs[a][b]
    product[...] = dot(s_ref[0], whole_ref[...], ((0 if transpose else 1,), (0,))).astype(NARROW)
    part = rows // parts
    for a in range(leave_n):
        for b in range(inner * outer // leave_n):
            block = product[place(number(a, b, leave_inner)), :]
            for p in range(parts):
                out_refs[p * leave_n + a][b] = block[p * part : (p + 1) * part]


def mix(second_factor, slabs, inner, outer, arrive_inner, leave_inner, transpose, parts, name):
    n = inner * outer
    rows, channels = slabs[0].shape[1:]
    total = n * rows
    leave_n = inner if leave_inner else outer
    member = n // leave_n
    part = rows // parts
    out = pl.pallas_call(
        functools.partial(mix_kernel, inner, outer, rows, arrive_inner, leave_inner, transpose, parts),
        in_specs=[pl.BlockSpec(memory_space=VMEM)] * (1 + len(slabs)),
        out_specs=[pl.BlockSpec(memory_space=VMEM)] * (leave_n * parts + 1),
        out_shape=[jax.ShapeDtypeStruct((member, part, channels), NARROW)] * (leave_n * parts)
        + [jax.ShapeDtypeStruct((total, channels), NARROW)],
        scratch_shapes=[VMEM((total, channels), NARROW)],
        compiler_params=params(32),
        cost_estimate=cost(2 * total * total * channels, 4 * total * channels),
        name=name,
    )(second_factor, *slabs)
    return [out[p * leave_n : (p + 1) * leave_n] for p in range(parts)], out[-1]


def grads_kernel(inner, outer, slots, group, first, w_ref, x_ref, *refs):
    slab_refs = refs[:inner]
    refs = refs[inner:] if first else refs[inner + 2 :]
    vg_ref, fg_ref, slabs, back, fg_buf, buf, out_buf, in_sem, out_sem, fg_sem = refs
    blocks, n, length = w_ref.shape
    part = slab_refs[0].shape[1]
    base = 0 if first else blocks - part
    steps = part // group
    rows = group * length
    channels = slabs.shape[1]

    def fetch(i, s):
        return pltpu.make_async_copy(x_ref.at[pl.ds((base + i * group) * length, rows), :], buf.at[s], in_sem.at[s])

    def put(i, s):
        return pltpu.make_async_copy(out_buf.at[s], vg_ref.at[pl.ds((base + i * group) * length, rows), :], out_sem.at[s])

    for s in range(slots):
        fetch(s, s).start()
    span = outer * part
    for o in range(inner):
        for b in range(outer):
            slabs[(o * outer + b) * part : (o * outer + b + 1) * part, :] = slab_refs[o][b]
    matrix = merge_matrix(lax.axis_index("seq"), part, n, inner_major(inner, outer))
    back[...] = dot(matrix, slabs[...], ((1,), (0,))).astype(NARROW)

    def step(i, carry):
        s = lax.rem(i, slots)

        @pl.when(i >= slots)
        def _():
            put(i - slots, s).wait()

        fetch(i, s).wait()
        for g in range(group):
            w = w_ref[base + i * group + g]
            f = back[pl.ds(pl.multiple_of((i * group + g) * n, n), n), :]
            here = slice(g * length, (g + 1) * length)
            out_buf[s, here, :] = dot(w, f, ((0,), (0,))).astype(NARROW)
            fg_buf[i * group + g] = dot(f, buf[s, here, :], ((1,), (1,))).astype(NARROW)
        put(i, s).start()

        @pl.when(i + slots < steps)
        def _():
            fetch(i + slots, s).start()

        return carry

    lax.fori_loop(0, steps, step, 0)
    last = pltpu.make_async_copy(fg_buf, fg_ref.at[pl.ds(base, part)], fg_sem)
    last.start()
    for i in range(steps - slots, steps):
        put(i, i % slots).wait()
    last.wait()


def grads(first_factor, values, slabs, inner, outer, earlier):
    blocks, n, length = first_factor.shape
    channels = values.shape[1]
    part = slabs[0].shape[1]
    first = earlier is None
    group = 2 if part % 2 == 0 else 1
    slots = min(4, part // group)
    shapes = [
        jax.ShapeDtypeStruct(values.shape, NARROW),
        jax.ShapeDtypeStruct(first_factor.shape, NARROW),
    ]
    return pl.pallas_call(
        functools.partial(grads_kernel, inner, outer, slots, group, first),
        in_specs=[pl.BlockSpec(memory_space=VMEM), pl.BlockSpec(memory_space=ANY)]
        + [pl.BlockSpec(memory_space=VMEM)] * inner
        + ([] if first else [pl.BlockSpec(memory_space=ANY)] * 2),
        out_specs=[pl.BlockSpec(memory_space=ANY)] * 2,
        out_shape=shapes,
        input_output_aliases={} if first else {2 + inner: 0, 3 + inner: 1},
        scratch_shapes=[
            VMEM((part * n, channels), NARROW),
            VMEM((part * n, channels), NARROW),
            VMEM((part, n, length), NARROW),
            VMEM((slots, group * length, channels), NARROW),
            VMEM((slots, group * length, channels), NARROW),
            pltpu.SemaphoreType.DMA((slots,)),
            pltpu.SemaphoreType.DMA((slots,)),
            pltpu.SemaphoreType.DMA,
        ],
        compiler_params=params(40),
        cost_estimate=cost(4 * part * n * length * channels, 4 * part * length * channels),
        name="grads",
    )(first_factor, values, *slabs, *(() if first else earlier))


def gates_kernel(inner, outer, rows, g_ref, d_ref, *refs):
    slab_refs, (mixed_ref, grad_ref, matrix, slabs) = refs[:outer], refs[outer:]
    n = inner * outer

    @pl.when(pl.program_id(0) == 0)
    def _():
        matrix[...] = merge_matrix(lax.axis_index("seq"), rows, n, outer_major(inner))

    span = inner * rows
    for o in range(outer):
        slabs[o * span : (o + 1) * span, :] = slab_refs[o][...]
    z = dot(matrix[...], slabs[...], ((1,), (0,)))
    mixed_ref[...] = (g_ref[...].astype(WIDE) * z).astype(NARROW)
    grad_ref[...] = (d_ref[...].astype(WIDE) * z).astype(NARROW)


def gates(gate_in, cotangent, slabs, inner, outer):
    rows, n, channels = gate_in.shape
    total = rows * n
    chunks = 3 if channels % 384 == 0 else 1
    wide = channels // chunks
    span = inner * rows
    out = pl.pallas_call(
        functools.partial(gates_kernel, inner, outer, rows),
        grid=(chunks,),
        in_specs=[pl.BlockSpec((total, wide), lambda i: (0, i))] * 2
        + [pl.BlockSpec((span, wide), lambda i: (0, i))] * outer,
        out_specs=[pl.BlockSpec((total, wide), lambda i: (0, i))] * 2,
        out_shape=[jax.ShapeDtypeStruct((total, channels), NARROW)] * 2,
        scratch_shapes=[VMEM((total, total), NARROW), VMEM((total, wide), NARROW)],
        compiler_params=params(32),
        cost_estimate=cost(2 * total * total * channels, 10 * total * channels),
        name="gates",
    )(
        gate_in.reshape(total, channels),
        cotangent.reshape(total, channels),
        *[s.reshape(span, channels) for s in slabs],
    )
    return [o.reshape(gate_in.shape) for o in out]


def after(arrays, *tokens):
    return list(lax.optimization_barrier(tuple(arrays) + tokens)[: len(arrays)])


def exchange(slabs, step, n, order):
    got = list(slabs)
    for k in order:
        got[k] = lax.ppermute(slabs[k], "seq", [(i, i ^ (k * step)) for i in range(n)])
    return got


def regroup(slabs):
    count = slabs[0].shape[0]
    return [jnp.stack([s[b] for s in slabs]) for b in range(count)]


def by_permutes(values, gate_in, cotangent, first_factor, second_factor, inner, outer):
    n = inner * outer
    far = [2, 3, 1] if outer == 4 else list(range(outer - 1, 0, -1))
    near = [2, 3, 1] if inner == 4 else list(range(inner - 1, 0, -1))

    def across(slabs):
        return exchange(slabs, inner, n, far)

    def beside(slabs):
        return exchange(slabs, 1, n, near)

    e = across(gated_slabs(gate_in, cotangent, inner, outer))
    e = beside(regroup(e))
    u = beside(inner_slabs(first_factor, values, inner, outer))
    u = across(regroup(u))
    halves = 2 if gate_in.shape[0] % 32 == 0 else 1
    f, e_all = mix(second_factor, e, inner, outer, True, False, True, halves, "back")
    z, u_all = mix(second_factor, u, inner, outer, False, True, False, 1, "forth")
    z = across(regroup(beside(z[0])))
    out = None
    for half in f:
        out = grads(first_factor, values, beside(regroup(across(half))), inner, outer, out)
    values_grad, first_grad = out
    second_grad = dot(e_all, u_all, ((1,), (1,))).astype(NARROW)[None]
    mixed, gate_grad = gates(gate_in, cotangent, z, inner, outer)
    return mixed, values_grad, gate_grad, first_grad, second_grad


def by_all_to_all(values, gate_in, cotangent, first_factor, second_factor):
    block_len = first_factor.shape[2]
    channels = values.shape[1]
    blocks_x = values.reshape(-1, block_len, channels)
    inner = jnp.einsum("aqp,apc->aqc", first_factor, blocks_x, preferred_element_type=WIDE).astype(NARROW)
    gated = (gate_in.astype(WIDE) * cotangent.astype(WIDE)).astype(NARROW)
    inner_t = lax.all_to_all(inner, "seq", split_axis=1, concat_axis=0, tiled=True)
    outer_t = jnp.einsum("qxa,aqc->xqc", second_factor, inner_t, preferred_element_type=WIDE).astype(NARROW)
    outer = lax.all_to_all(outer_t, "seq", split_axis=0, concat_axis=1, tiled=True)
    gated_t = lax.all_to_all(gated, "seq", split_axis=1, concat_axis=0, tiled=True)
    second_grad = jnp.einsum("xqc,aqc->qxa", gated_t, inner_t, preferred_element_type=WIDE).astype(NARROW)
    back_t = jnp.einsum("qxa,xqc->aqc", second_factor, gated_t, preferred_element_type=WIDE).astype(NARROW)
    back_inner = lax.all_to_all(back_t, "seq", split_axis=0, concat_axis=1, tiled=True)
    outer_f = outer.astype(WIDE)
    mixed = (gate_in.astype(WIDE) * outer_f).astype(NARROW)
    gate_grad = (cotangent.astype(WIDE) * outer_f).astype(NARROW)
    first_grad = jnp.einsum("aqc,apc->aqp", back_inner, blocks_x, preferred_element_type=WIDE).astype(NARROW)
    values_grad = (
        jnp.einsum("aqp,aqc->apc", first_factor, back_inner, preferred_element_type=WIDE)
        .astype(NARROW)
        .reshape(-1, channels)
    )
    return mixed, values_grad, gate_grad, first_grad, second_grad


def solution(mesh):
    n = mesh.shape["seq"]

    def on_device(values, gate_in, cotangent, first_factor, second_factor):
        rows, kept = gate_in.shape[:2]
        if n == 16 and kept == n and rows % 16 == 0 and first_factor.shape[0] == rows:
            return by_permutes(values, gate_in, cotangent, first_factor, second_factor, 4, n // 4)
        return by_all_to_all(values, gate_in, cotangent, first_factor, second_factor)

    both = ("grp", "seq")
    return jax.shard_map(
        on_device,
        mesh=mesh,
        in_specs=(
            P(both, None),
            P(both, None, None),
            P(both, None, None),
            P("seq", None, None),
            P("seq", None, None),
        ),
        out_specs=(
            P(both, None, None),
            P(both, None),
            P(both, None, None),
            P(both, None, None),
            P(both, None, None),
        ),
        check_vma=False,
    )
```

time: 156 us -> 106 us (0.68)
  the two profiles are of different devices: /device:TPU:11 before, /device:TPU:0 now
where the time goes in v1:
time: 106 us
  starting transfers between devices  39.3 us (37%)
  Pallas kernels  35.7 us (34%)
  waiting for transfers between devices  24 us (23%)
  local copies, waits for them, and re-layouts  3.62 us (3%)
  matrix products  1.4 us (1%)
  between operations  1.11 us (1%)
    ppermute x30, starting transfers between devices, exchange(): lax.ppermute(slabs[k], 'seq', [(i, i ^ k * step) for i in range(n)])  39.3 us
    ppermute x30, waiting for transfers between devices, exchange(): lax.ppermute(slabs[k], 'seq', [(i, i ^ k * step) for i in range(n)])  24 us
    pallas_call x2, Pallas kernels, grads(): pl.pallas_call(functools.partial(grads_kernel, inner, outer, slots, group...  21 us
    pallas_call x1, Pallas kernels, inner_slabs(): pl.pallas_call(functools.partial(inner_kernel, inner, outer, slots, group...  9.49 us
    unnamed x14, local copies, waits for them, and re-layouts  3.38 us
    pallas_call x1, Pallas kernels, gates(): pl.pallas_call(functools.partial(gates_kernel, inner, outer, rows), grid=...  2.53 us
  transfers between devices with their start and end apart: 30, of which 9 were waited for; matrix products, arithmetic and copies ran while one was open for 2% of the time, Pallas kernels for 30%

profile of v1, /device:TPU:0, one launch (start us, length us, event | category | flops | bytes accessed | tf_op | source)
XLA Modules:
  0.0 105.5 jit_solution(1034864902610392451)
XLA Ops:
  0.7 1.2 %copy-done.2 = bf16[32,16,768]{2,1,0:T(8,128)(2,1)S(1)} copy-done((bf16[32,16,768]{2,1,0:T(8,128)(2,1)S(1)}, bf16[32,16,768]{2,1,0:T(8,128)(2,1)}, u32[]{:S(2)}) %copy-start.2) | copy-done | bytes 786456
  1.8 1.1 %copy-done.4 = bf16[32,16,768]{2,1,0:T(8,128)(2,1)S(1)} copy-done((bf16[32,16,768]{2,1,0:T(8,128)(2,1)S(1)}, bf16[32,16,768]{2,1,0:T(8,128)(2,1)}, u32[]{:S(2)}) %copy-start.4) | copy-done | bytes 786456
  3.0 1.3 %gated_slabs.1 = (bf16[128,768]{1,0:T(8,128)(2,1)S(1)}, bf16[128,768]{1,0:T(8,128)(2,1)S(1)}, bf16[128,768]{1,0:T(8,128)(2,1)S(1)}, bf16[128,768]{1,0:T(8,128)(2,1)S(1)}) custom-call(bf16[512,768]{1,0:T(8,128)(2,1)S(1)} %bitcast.34, bf16[512,768]{1,0:T(8,128)(2,1)S(1)} %bitcast.36), custom_call_target="tpu_custom_call" | custom-call | flops 402653184 | bytes 2359296 | tf_op jit(solution)/shard_map/gated_slabs/pallas_call | solution.py:77
  4.3 3.1 %collective-permute-start.12 = (bf16[4,32,768]{2,1,0:T(8,128)(2,1)S(1)}, bf16[4,32,768]{2,1,0:T(8,128)(2,1)S(1)}, u32[]{:S(2)}, u32[]{:S(2)}) collective-permute-start(bf16[4,32,768]{2,1,0:T(8,128)(2,1)S(1)} %bitcast.47), channel_id=1, source_target_pairs={{0,4},{1,5},{2,6},{3,7},{4,0},{5,1},{6,2},{7,3},{8,12},{9,13},{10,... | collective-permute-start | bytes 589832 | tf_op jit(solution)/shard_map/ppermute | solution.py:331
  7.3 2.6 %collective-permute-start.13 = (bf16[4,32,768]{2,1,0:T(8,128)(2,1)S(1)}, bf16[4,32,768]{2,1,0:T(8,128)(2,1)S(1)}, u32[]{:S(2)}, u32[]{:S(2)}) collective-permute-start(bf16[4,32,768]{2,1,0:T(8,128)(2,1)S(1)} %bitcast.46), channel_id=1, source_target_pairs={{0,8},{1,9},{2,10},{3,11},{4,12},{5,13},{6,14},{7,15},{8,0},{9,1},... | collective-permute-start | bytes 589832 | tf_op jit(solution)/shard_map/ppermute | solution.py:331
  9.9 1.0 copy-done
  11.0 9.5 %inner_slabs.1 = (bf16[128,768]{1,0:T(8,128)(2,1)S(1)}, bf16[128,768]{1,0:T(8,128)(2,1)S(1)}, bf16[128,768]{1,0:T(8,128)(2,1)S(1)}, bf16[128,768]{1,0:T(8,128)(2,1)S(1)}) custom-call(bf16[32,16,512]{2,1,0:T(8,128)(2,1)S(1)} %copy-done, bf16[16384,768]{1,0:T(8,128)(2,1)} %x_ref.5), custom_call_target="tpu_custom_call" | custom-call | flops 402653184 | bytes 25165824 | tf_op jit(solution)/shard_map/inner_slabs/pallas_call | solution.py:129
  20.5 1.8 %collective-permute-start.1 = (bf16[4,32,768]{2,1,0:T(8,128)(2,1)S(1)}, bf16[4,32,768]{2,1,0:T(8,128)(2,1)S(1)}, u32[]{:S(2)}, u32[]{:S(2)}) collective-permute-start(bf16[4,32,768]{2,1,0:T(8,128)(2,1)S(1)} %bitcast.44), channel_id=1, source_target_pairs={{0,2},{1,3},{2,0},{3,1},{4,6},{5,7},{6,4},{7,5},{8,10},{9,11},{10,... | collective-permute-start | bytes 589832 | tf_op jit(solution)/shard_map/ppermute | solution.py:331
  22.8 1.7 %collective-permute-done.13 = bf16[4,32,768]{2,1,0:T(8,128)(2,1)S(1)} collective-permute-done((bf16[4,32,768]{2,1,0:T(8,128)(2,1)S(1)}, bf16[4,32,768]{2,1,0:T(8,128)(2,1)S(1)}, u32[]{:S(2)}, u32[]{:S(2)}) %collective-permute-start.13) | collective-permute-done | bytes 196640 | tf_op jit(solution)/shard_map/ppermute | solution.py:331
  24.7 1.6 %collective-permute-start.16 = (bf16[4,32,768]{2,1,0:T(8,128)(2,1)S(1)}, bf16[4,32,768]{2,1,0:T(8,128)(2,1)S(1)}, u32[]{:S(2)}, u32[]{:S(2)}) collective-permute-start(bf16[4,32,768]{2,1,0:T(8,128)(2,1)S(1)} %pad_maximum_fusion.10), channel_id=1, source_target_pairs={{0,2},{1,3},{2,0},{3,1},{4,6},{5,7},{6,4},{7,5},{8,10},{9,11},{10,... | collective-permute-start | bytes 589832 | tf_op jit(solution)/shard_map/ppermute | solution.py:331
  26.3 1.7 %collective-permute-done.1 = bf16[4,32,768]{2,1,0:T(8,128)(2,1)S(1)} collective-permute-done((bf16[4,32,768]{2,1,0:T(8,128)(2,1)S(1)}, bf16[4,32,768]{2,1,0:T(8,128)(2,1)S(1)}, u32[]{:S(2)}, u32[]{:S(2)}) %collective-permute-start.1) | collective-permute-done | bytes 196640 | tf_op jit(solution)/shard_map/ppermute | solution.py:331
  28.0 3.8 %collective-permute-done.2 = bf16[4,32,768]{2,1,0:T(8,128)(2,1)S(1)} collective-permute-done((bf16[4,32,768]{2,1,0:T(8,128)(2,1)S(1)}, bf16[4,32,768]{2,1,0:T(8,128)(2,1)S(1)}, u32[]{:S(2)}, u32[]{:S(2)}) %collective-permute-start.2) | collective-permute-done | bytes 196640 | tf_op jit(solution)/shard_map/ppermute | solution.py:331
  31.9 3.7 %collective-permute-start.5 = (bf16[4,32,768]{2,1,0:T(8,128)(2,1)S(1)}, bf16[4,32,768]{2,1,0:T(8,128)(2,1)S(1)}, u32[]{:S(2)}, u32[]{:S(2)}) collective-permute-start(bf16[4,32,768]{2,1,0:T(8,128)(2,1)S(1)} %pad_maximum_fusion.3), channel_id=1, source_target_pairs={{0,12},{1,13},{2,14},{3,15},{4,8},{5,9},{6,10},{7,11},{8,4},{9,5},... | collective-permute-start | bytes 589832 | tf_op jit(solution)/shard_map/ppermute | solution.py:331
  35.7 0.8 collective-permute-start.3
  36.7 1.6 %collective-permute-done.17.refs_3_ = bf16[4,32,768]{2,1,0:T(8,128)(2,1)S(1)} collective-permute-done((bf16[4,32,768]{2,1,0:T(8,128)(2,1)S(1)}, bf16[4,32,768]{2,1,0:T(8,128)(2,1)S(1)}, u32[]{:S(2)}, u32[]{:S(2)}) %collective-permute-start.17) | collective-permute-done | bytes 196640 | tf_op jit(solution)/shard_map/ppermute | solution.py:331
  39.0 1.5 %collective-permute-start.24 = (bf16[4,16,768]{2,1,0:T(8,128)(2,1)S(1)}, bf16[4,16,768]{2,1,0:T(8,128)(2,1)S(1)}, u32[]{:S(2)}, u32[]{:S(2)}) collective-permute-start(bf16[4,16,768]{2,1,0:T(8,128)(2,1)S(1)} %get-tuple-element.51), channel_id=1, source_target_pairs={{0,4},{1,5},{2,6},{3,7},{4,0},{5,1},{6,2},{7,3},{8,12},{9,13},{10,... | collective-permute-start | bytes 294920 | tf_op jit(solution)/shard_map/ppermute | solution.py:331
  40.4 2.7 %collective-permute-start.25 = (bf16[4,16,768]{2,1,0:T(8,128)(2,1)S(1)}, bf16[4,16,768]{2,1,0:T(8,128)(2,1)S(1)}, u32[]{:S(2)}, u32[]{:S(2)}) collective-permute-start(bf16[4,16,768]{2,1,0:T(8,128)(2,1)S(1)} %get-tuple-element.52), channel_id=1, source_target_pairs={{0,8},{1,9},{2,10},{3,11},{4,12},{5,13},{6,14},{7,15},{8,0},{9,1},... | collective-permute-start | bytes 294920 | tf_op jit(solution)/shard_map/ppermute | solution.py:331
  43.2 2.1 %collective-permute-start.26 = (bf16[4,16,768]{2,1,0:T(8,128)(2,1)S(1)}, bf16[4,16,768]{2,1,0:T(8,128)(2,1)S(1)}, u32[]{:S(2)}, u32[]{:S(2)}) collective-permute-start(bf16[4,16,768]{2,1,0:T(8,128)(2,1)S(1)} %get-tuple-element.53), channel_id=1, source_target_pairs={{0,12},{1,13},{2,14},{3,15},{4,8},{5,9},{6,10},{7,11},{8,4},{9,5},... | collective-permute-start | bytes 294920 | tf_op jit(solution)/shard_map/ppermute | solution.py:331
  45.3 5.5 %collective-permute-done.4.refs_2_ = bf16[4,32,768]{2,1,0:T(8,128)(2,1)S(1)} collective-permute-done((bf16[4,32,768]{2,1,0:T(8,128)(2,1)S(1)}, bf16[4,32,768]{2,1,0:T(8,128)(2,1)S(1)}, u32[]{:S(2)}, u32[]{:S(2)}) %collective-permute-start.4) | collective-permute-done | bytes 196640 | tf_op jit(solution)/shard_map/ppermute | solution.py:331
  50.8 3.0 %collective-permute-start.19 = (bf16[4,16,768]{2,1,0:T(8,128)(2,1)S(1)}, bf16[4,16,768]{2,1,0:T(8,128)(2,1)S(1)}, u32[]{:S(2)}, u32[]{:S(2)}) collective-permute-start(bf16[4,16,768]{2,1,0:T(8,128)(2,1)S(1)} %get-tuple-element.48), channel_id=1, source_target_pairs={{0,8},{1,9},{2,10},{3,11},{4,12},{5,13},{6,14},{7,15},{8,0},{9,1},... | collective-permute-start | bytes 294920 | tf_op jit(solution)/shard_map/ppermute | solution.py:331
  54.6 1.4 %fusion = bf16[1,512,512]{2,1,0:T(8,128)(2,1)} fusion(bf16[512,768]{1,0:T(8,128)(2,1)S(1)} %get-tuple-element.59, bf16[512,768]{1,0:T(8,128)(2,1)S(1)} %get-tuple-element.60), kind=kOutput, calls=%fused_computation.1 | convolution fusion | flops 402915328 | bytes 2097152 | tf_op jit(solution)/shard_map/dot_general | solution.py:54
  56.0 1.7 %collective-permute-start.20 = (bf16[4,16,768]{2,1,0:T(8,128)(2,1)S(1)}, bf16[4,16,768]{2,1,0:T(8,128)(2,1)S(1)}, u32[]{:S(2)}, u32[]{:S(2)}) collective-permute-start(bf16[4,16,768]{2,1,0:T(8,128)(2,1)S(1)} %get-tuple-element.49), channel_id=1, source_target_pairs={{0,12},{1,13},{2,14},{3,15},{4,8},{5,9},{6,10},{7,11},{8,4},{9,5},... | collective-permute-start | bytes 294920 | tf_op jit(solution)/shard_map/ppermute | solution.py:331
  57.8 1.6 %collective-permute-start.7 = (bf16[4,32,768]{2,1,0:T(8,128)(2,1)S(1)}, bf16[4,32,768]{2,1,0:T(8,128)(2,1)S(1)}, u32[]{:S(2)}, u32[]{:S(2)}) collective-permute-start(bf16[4,32,768]{2,1,0:T(8,128)(2,1)S(1)} %get-tuple-element.39), channel_id=1, source_target_pairs={{0,2},{1,3},{2,0},{3,1},{4,6},{5,7},{6,4},{7,5},{8,10},{9,11},{10,... | collective-permute-start | bytes 589832 | tf_op jit(solution)/shard_map/ppermute | solution.py:331
  59.9 5.7 %collective-permute-done.19 = bf16[4,16,768]{2,1,0:T(8,128)(2,1)S(1)} collective-permute-done((bf16[4,16,768]{2,1,0:T(8,128)(2,1)S(1)}, bf16[4,16,768]{2,1,0:T(8,128)(2,1)S(1)}, u32[]{:S(2)}, u32[]{:S(2)}) %collective-permute-start.19) | collective-permute-done | bytes 98336 | tf_op jit(solution)/shard_map/ppermute | solution.py:331
  67.7 1.0 collective-permute-start.23
  69.6 1.4 %collective-permute-done.29.refs_3_ = bf16[4,16,768]{2,1,0:T(8,128)(2,1)S(1)} collective-permute-done((bf16[4,16,768]{2,1,0:T(8,128)(2,1)S(1)}, bf16[4,16,768]{2,1,0:T(8,128)(2,1)S(1)}, u32[]{:S(2)}, u32[]{:S(2)}) %collective-permute-start.29) | collective-permute-done | bytes 98336 | tf_op jit(solution)/shard_map/ppermute | solution.py:331
  71.7 2.3 %collective-permute-done.28.refs_2_ = bf16[4,16,768]{2,1,0:T(8,128)(2,1)S(1)} collective-permute-done((bf16[4,16,768]{2,1,0:T(8,128)(2,1)S(1)}, bf16[4,16,768]{2,1,0:T(8,128)(2,1)S(1)}, u32[]{:S(2)}, u32[]{:S(2)}) %collective-permute-start.28) | collective-permute-done | bytes 98336 | tf_op jit(solution)/shard_map/ppermute | solution.py:331
  74.0 2.2 %collective-permute-start.11 = (bf16[4,32,768]{2,1,0:T(8,128)(2,1)S(1)}, bf16[4,32,768]{2,1,0:T(8,128)(2,1)S(1)}, u32[]{:S(2)}, u32[]{:S(2)}) collective-permute-start(bf16[4,32,768]{2,1,0:T(8,128)(2,1)S(1)} %pad_maximum_fusion.7), channel_id=1, source_target_pairs={{0,12},{1,13},{2,14},{3,15},{4,8},{5,9},{6,10},{7,11},{8,4},{9,5},... | collective-permute-start | bytes 589832 | tf_op jit(solution)/shard_map/ppermute | solution.py:331
  76.1 5.5 %collective-permute-start.10 = (bf16[4,32,768]{2,1,0:T(8,128)(2,1)S(1)}, bf16[4,32,768]{2,1,0:T(8,128)(2,1)S(1)}, u32[]{:S(2)}, u32[]{:S(2)}) collective-permute-start(bf16[4,32,768]{2,1,0:T(8,128)(2,1)S(1)} %pad_maximum_fusion.6), channel_id=1, source_target_pairs={{0,8},{1,9},{2,10},{3,11},{4,12},{5,13},{6,14},{7,15},{8,0},{9,1},... | collective-permute-start | bytes 589832 | tf_op jit(solution)/shard_map/ppermute | solution.py:331
  81.9 10.4 %grads.2 = (bf16[16384,768]{1,0:T(8,128)(2,1)}, bf16[32,16,512]{2,1,0:T(8,128)(2,1)}) custom-call(bf16[32,16,512]{2,1,0:T(8,128)(2,1)S(1)} %copy-done.1, bf16[16384,768]{1,0:T(8,128)(2,1)} %x_ref.5, bf16[4,16,768]{2,1,0:T(8,128)(2,1)S(1)} %pad_maximum_fusion.16.refs_0_, bf16[4,16,768]{2,1,0:T(8,128)(2,1)S(1)} %collective-permute-done.27.refs_1_, ...), custom_call_target="tpu_custom_call" | custom-call | flops 402653184 | bytes 25165824 | tf_op jit(solution)/shard_map/grads/pallas_call | solution.py:259
  92.4 10.6 %grads.3 = (bf16[16384,768]{1,0:T(8,128)(2,1)}, bf16[32,16,512]{2,1,0:T(8,128)(2,1)}) custom-call(bf16[32,16,512]{2,1,0:T(8,128)(2,1)S(1)} %copy-done.1, bf16[16384,768]{1,0:T(8,128)(2,1)} %x_ref.5, bf16[4,16,768]{2,1,0:T(8,128)(2,1)S(1)} %pad_maximum_fusion.12.refs_0_, ...), custom_call_target="tpu_custom_call", output_to_operand_aliasing={{0}: (6, {}), {1}: (7, {})} | custom-call | flops 402653184 | bytes 25165824 | tf_op jit(solution)/shard_map/grads/pallas_call | solution.py:259
  103.0 2.5 %gates.1 = (bf16[512,768]{1,0:T(8,128)(2,1)}, bf16[512,768]{1,0:T(8,128)(2,1)}) custom-call(bf16[512,768]{1,0:T(8,128)(2,1)S(1)} %bitcast.35, bf16[512,768]{1,0:T(8,128)(2,1)S(1)} %bitcast.37, bf16[128,768]{1,0:T(8,128)(2,1)S(1)} %bitcast.38, bf16[128,768]{1,0:T(8,128)(2,1)S(1)} %bitcast.41, bf16[128,768]{1,0:T(8,128)(2,1)S(1)} %bitcast.40, ...), custom_call_target="tpu_custom_call" | custom-call | flops 402653184 | bytes 3932160 | tf_op jit(solution)/shard_map/gates/pallas_call | solution.py:305
  (89 shorter events, 6.9 us)
Async XLA Ops:
  0.6 81.3 %copy-start.1 = (bf16[32,16,512]{2,1,0:T(8,128)(2,1)S(1)}, bf16[32,16,512]{2,1,0:T(8,128)(2,1)}, u32[]{:S(2)}) copy-start(bf16[32,16,512]{2,1,0:T(8,128)(2,1)} %w_ref.5) | copy-start | bytes 1572868
  3.0 35.3 %copy-start.6 = (bf16[1,512,512]{2,1,0:T(8,128)(2,1)S(1)}, bf16[1,512,512]{2,1,0:T(8,128)(2,1)}, u32[]{:S(2)}) copy-start(bf16[1,512,512]{2,1,0:T(8,128)(2,1)} %s_ref.3) | copy-start | bytes 1572868
  4.3 18.0 %collective-permute-start.12 = (bf16[4,32,768]{2,1,0:T(8,128)(2,1)S(1)}, bf16[4,32,768]{2,1,0:T(8,128)(2,1)S(1)}, u32[]{:S(2)}, u32[]{:S(2)}) collective-permute-start(bf16[4,32,768]{2,1,0:T(8,128)(2,1)S(1)} %bitcast.47), channel_id=1, source_target_pairs={{0,4},{1,5},{2,6},{3,7},{4,0},{5,1},{6,2},{7,3},{8,12},{9,13},{10,... | collective-permute-start | bytes 589832 | tf_op jit(solution)/shard_map/ppermute | solution.py:331
  7.3 17.2 %collective-permute-start.13 = (bf16[4,32,768]{2,1,0:T(8,128)(2,1)S(1)}, bf16[4,32,768]{2,1,0:T(8,128)(2,1)S(1)}, u32[]{:S(2)}, u32[]{:S(2)}) collective-permute-start(bf16[4,32,768]{2,1,0:T(8,128)(2,1)S(1)} %bitcast.46), channel_id=1, source_target_pairs={{0,8},{1,9},{2,10},{3,11},{4,12},{5,13},{6,14},{7,15},{8,0},{9,1},... | collective-permute-start | bytes 589832 | tf_op jit(solution)/shard_map/ppermute | solution.py:331
  9.9 14.6 %collective-permute-start.14 = (bf16[4,32,768]{2,1,0:T(8,128)(2,1)S(1)}, bf16[4,32,768]{2,1,0:T(8,128)(2,1)S(1)}, u32[]{:S(2)}, u32[]{:S(2)}) collective-permute-start(bf16[4,32,768]{2,1,0:T(8,128)(2,1)S(1)} %bitcast.45), channel_id=1, source_target_pairs={{0,12},{1,13},{2,14},{3,15},{4,8},{5,9},{6,10},{7,11},{8,4},{9,5},... | collective-permute-start | bytes 589832 | tf_op jit(solution)/shard_map/ppermute | solution.py:331
  20.5 7.5 %collective-permute-start.1 = (bf16[4,32,768]{2,1,0:T(8,128)(2,1)S(1)}, bf16[4,32,768]{2,1,0:T(8,128)(2,1)S(1)}, u32[]{:S(2)}, u32[]{:S(2)}) collective-permute-start(bf16[4,32,768]{2,1,0:T(8,128)(2,1)S(1)} %bitcast.44), channel_id=1, source_target_pairs={{0,2},{1,3},{2,0},{3,1},{4,6},{5,7},{6,4},{7,5},{8,10},{9,11},{10,... | collective-permute-start | bytes 589832 | tf_op jit(solution)/shard_map/ppermute | solution.py:331
  22.3 9.6 %collective-permute-start.2 = (bf16[4,32,768]{2,1,0:T(8,128)(2,1)S(1)}, bf16[4,32,768]{2,1,0:T(8,128)(2,1)S(1)}, u32[]{:S(2)}, u32[]{:S(2)}) collective-permute-start(bf16[4,32,768]{2,1,0:T(8,128)(2,1)S(1)} %bitcast.43), channel_id=1, source_target_pairs={{0,3},{1,2},{2,1},{3,0},{4,7},{5,6},{6,5},{7,4},{8,11},{9,10},{10,... | collective-permute-start | bytes 589832 | tf_op jit(solution)/shard_map/ppermute | solution.py:331
  22.3 9.5 %collective-permute-start = (bf16[4,32,768]{2,1,0:T(8,128)(2,1)S(1)}, bf16[4,32,768]{2,1,0:T(8,128)(2,1)S(1)}, u32[]{:S(2)}, u32[]{:S(2)}) collective-permute-start(bf16[4,32,768]{2,1,0:T(8,128)(2,1)S(1)} %bitcast.42), channel_id=1, source_target_pairs={{0,1},{1,0},{2,3},{3,2},{4,5},{5,4},{6,7},{7,6},{8,9},{9,8},{10,11... | collective-permute-start | bytes 589832 | tf_op jit(solution)/shard_map/ppermute | solution.py:331
  24.6 11.1 %collective-permute-start.15 = (bf16[4,32,768]{2,1,0:T(8,128)(2,1)S(1)}, bf16[4,32,768]{2,1,0:T(8,128)(2,1)S(1)}, u32[]{:S(2)}, u32[]{:S(2)}) collective-permute-start(bf16[4,32,768]{2,1,0:T(8,128)(2,1)S(1)} %pad_maximum_fusion.9), channel_id=1, source_target_pairs={{0,1},{1,0},{2,3},{3,2},{4,5},{5,4},{6,7},{7,6},{8,9},{9,8},{10,11... | collective-permute-start | bytes 589832 | tf_op jit(solution)/shard_map/ppermute | solution.py:331
  24.7 11.9 %collective-permute-start.16 = (bf16[4,32,768]{2,1,0:T(8,128)(2,1)S(1)}, bf16[4,32,768]{2,1,0:T(8,128)(2,1)S(1)}, u32[]{:S(2)}, u32[]{:S(2)}) collective-permute-start(bf16[4,32,768]{2,1,0:T(8,128)(2,1)S(1)} %pad_maximum_fusion.10), channel_id=1, source_target_pairs={{0,2},{1,3},{2,0},{3,1},{4,6},{5,7},{6,4},{7,5},{8,10},{9,11},{10,... | collective-permute-start | bytes 589832 | tf_op jit(solution)/shard_map/ppermute | solution.py:331
  28.0 10.3 %collective-permute-start.17 = (bf16[4,32,768]{2,1,0:T(8,128)(2,1)S(1)}, bf16[4,32,768]{2,1,0:T(8,128)(2,1)S(1)}, u32[]{:S(2)}, u32[]{:S(2)}) collective-permute-start(bf16[4,32,768]{2,1,0:T(8,128)(2,1)S(1)} %pad_maximum_fusion.11), channel_id=1, source_target_pairs={{0,3},{1,2},{2,1},{3,0},{4,7},{5,6},{6,5},{7,4},{8,11},{9,10},{10,... | collective-permute-start | bytes 589832 | tf_op jit(solution)/shard_map/ppermute | solution.py:331
  31.9 11.2 %collective-permute-start.5 = (bf16[4,32,768]{2,1,0:T(8,128)(2,1)S(1)}, bf16[4,32,768]{2,1,0:T(8,128)(2,1)S(1)}, u32[]{:S(2)}, u32[]{:S(2)}) collective-permute-start(bf16[4,32,768]{2,1,0:T(8,128)(2,1)S(1)} %pad_maximum_fusion.3), channel_id=1, source_target_pairs={{0,12},{1,13},{2,14},{3,15},{4,8},{5,9},{6,10},{7,11},{8,4},{9,5},... | collective-permute-start | bytes 589832 | tf_op jit(solution)/shard_map/ppermute | solution.py:331
  35.6 15.2 %collective-permute-start.4 = (bf16[4,32,768]{2,1,0:T(8,128)(2,1)S(1)}, bf16[4,32,768]{2,1,0:T(8,128)(2,1)S(1)}, u32[]{:S(2)}, u32[]{:S(2)}) collective-permute-start(bf16[4,32,768]{2,1,0:T(8,128)(2,1)S(1)} %pad_maximum_fusion.2), channel_id=1, source_target_pairs={{0,8},{1,9},{2,10},{3,11},{4,12},{5,13},{6,14},{7,15},{8,0},{9,1},... | collective-permute-start | bytes 589832 | tf_op jit(solution)/shard_map/ppermute | solution.py:331
  35.7 15.1 %collective-permute-start.3 = (bf16[4,32,768]{2,1,0:T(8,128)(2,1)S(1)}, bf16[4,32,768]{2,1,0:T(8,128)(2,1)S(1)}, u32[]{:S(2)}, u32[]{:S(2)}) collective-permute-start(bf16[4,32,768]{2,1,0:T(8,128)(2,1)S(1)} %pad_maximum_fusion.1), channel_id=1, source_target_pairs={{0,4},{1,5},{2,6},{3,7},{4,0},{5,1},{6,2},{7,3},{8,12},{9,13},{10,... | collective-permute-start | bytes 589832 | tf_op jit(solution)/shard_map/ppermute | solution.py:331
  39.0 17.0 %collective-permute-start.24 = (bf16[4,16,768]{2,1,0:T(8,128)(2,1)S(1)}, bf16[4,16,768]{2,1,0:T(8,128)(2,1)S(1)}, u32[]{:S(2)}, u32[]{:S(2)}) collective-permute-start(bf16[4,16,768]{2,1,0:T(8,128)(2,1)S(1)} %get-tuple-element.51), channel_id=1, source_target_pairs={{0,4},{1,5},{2,6},{3,7},{4,0},{5,1},{6,2},{7,3},{8,12},{9,13},{10,... | collective-permute-start | bytes 294920 | tf_op jit(solution)/shard_map/ppermute | solution.py:331
  40.4 17.2 %collective-permute-start.25 = (bf16[4,16,768]{2,1,0:T(8,128)(2,1)S(1)}, bf16[4,16,768]{2,1,0:T(8,128)(2,1)S(1)}, u32[]{:S(2)}, u32[]{:S(2)}) collective-permute-start(bf16[4,16,768]{2,1,0:T(8,128)(2,1)S(1)} %get-tuple-element.52), channel_id=1, source_target_pairs={{0,8},{1,9},{2,10},{3,11},{4,12},{5,13},{6,14},{7,15},{8,0},{9,1},... | collective-permute-start | bytes 294920 | tf_op jit(solution)/shard_map/ppermute | solution.py:331
  43.2 14.6 %collective-permute-start.26 = (bf16[4,16,768]{2,1,0:T(8,128)(2,1)S(1)}, bf16[4,16,768]{2,1,0:T(8,128)(2,1)S(1)}, u32[]{:S(2)}, u32[]{:S(2)}) collective-permute-start(bf16[4,16,768]{2,1,0:T(8,128)(2,1)S(1)} %get-tuple-element.53), channel_id=1, source_target_pairs={{0,12},{1,13},{2,14},{3,15},{4,8},{5,9},{6,10},{7,11},{8,4},{9,5},... | collective-permute-start | bytes 294920 | tf_op jit(solution)/shard_map/ppermute | solution.py:331
  50.8 8.6 %collective-permute-start.18 = (bf16[4,16,768]{2,1,0:T(8,128)(2,1)S(1)}, bf16[4,16,768]{2,1,0:T(8,128)(2,1)S(1)}, u32[]{:S(2)}, u32[]{:S(2)}) collective-permute-start(bf16[4,16,768]{2,1,0:T(8,128)(2,1)S(1)} %get-tuple-element.47), channel_id=1, source_target_pairs={{0,4},{1,5},{2,6},{3,7},{4,0},{5,1},{6,2},{7,3},{8,12},{9,13},{10,... | collective-permute-start | bytes 294920 | tf_op jit(solution)/shard_map/ppermute | solution.py:331
  50.8 14.7 %collective-permute-start.19 = (bf16[4,16,768]{2,1,0:T(8,128)(2,1)S(1)}, bf16[4,16,768]{2,1,0:T(8,128)(2,1)S(1)}, u32[]{:S(2)}, u32[]{:S(2)}) collective-permute-start(bf16[4,16,768]{2,1,0:T(8,128)(2,1)S(1)} %get-tuple-element.48), channel_id=1, source_target_pairs={{0,8},{1,9},{2,10},{3,11},{4,12},{5,13},{6,14},{7,15},{8,0},{9,1},... | collective-permute-start | bytes 294920 | tf_op jit(solution)/shard_map/ppermute | solution.py:331
  56.0 10.2 %collective-permute-start.20 = (bf16[4,16,768]{2,1,0:T(8,128)(2,1)S(1)}, bf16[4,16,768]{2,1,0:T(8,128)(2,1)S(1)}, u32[]{:S(2)}, u32[]{:S(2)}) collective-permute-start(bf16[4,16,768]{2,1,0:T(8,128)(2,1)S(1)} %get-tuple-element.49), channel_id=1, source_target_pairs={{0,12},{1,13},{2,14},{3,15},{4,8},{5,9},{6,10},{7,11},{8,4},{9,5},... | collective-permute-start | bytes 294920 | tf_op jit(solution)/shard_map/ppermute | solution.py:331
  57.7 9.4 %collective-permute-start.6 = (bf16[4,32,768]{2,1,0:T(8,128)(2,1)S(1)}, bf16[4,32,768]{2,1,0:T(8,128)(2,1)S(1)}, u32[]{:S(2)}, u32[]{:S(2)}) collective-permute-start(bf16[4,32,768]{2,1,0:T(8,128)(2,1)S(1)} %get-tuple-element.38), channel_id=1, source_target_pairs={{0,1},{1,0},{2,3},{3,2},{4,5},{5,4},{6,7},{7,6},{8,9},{9,8},{10,11... | collective-permute-start | bytes 589832 | tf_op jit(solution)/shard_map/ppermute | solution.py:331
  57.8 9.9 %collective-permute-start.7 = (bf16[4,32,768]{2,1,0:T(8,128)(2,1)S(1)}, bf16[4,32,768]{2,1,0:T(8,128)(2,1)S(1)}, u32[]{:S(2)}, u32[]{:S(2)}) collective-permute-start(bf16[4,32,768]{2,1,0:T(8,128)(2,1)S(1)} %get-tuple-element.39), channel_id=1, source_target_pairs={{0,2},{1,3},{2,0},{3,1},{4,6},{5,7},{6,4},{7,5},{8,10},{9,11},{10,... | collective-permute-start | bytes 589832 | tf_op jit(solution)/shard_map/ppermute | solution.py:331
  59.4 9.5 %collective-permute-start.8 = (bf16[4,32,768]{2,1,0:T(8,128)(2,1)S(1)}, bf16[4,32,768]{2,1,0:T(8,128)(2,1)S(1)}, u32[]{:S(2)}, u32[]{:S(2)}) collective-permute-start(bf16[4,32,768]{2,1,0:T(8,128)(2,1)S(1)} %get-tuple-element.40), channel_id=1, source_target_pairs={{0,3},{1,2},{2,1},{3,0},{4,7},{5,6},{6,5},{7,4},{8,11},{9,10},{10,... | collective-permute-start | bytes 589832 | tf_op jit(solution)/shard_map/ppermute | solution.py:331
  65.5 5.5 %collective-permute-start.29 = (bf16[4,16,768]{2,1,0:T(8,128)(2,1)S(1)}, bf16[4,16,768]{2,1,0:T(8,128)(2,1)S(1)}, u32[]{:S(2)}, u32[]{:S(2)}) collective-permute-start(bf16[4,16,768]{2,1,0:T(8,128)(2,1)S(1)} %pad_maximum_fusion.19), channel_id=1, source_target_pairs={{0,3},{1,2},{2,1},{3,0},{4,7},{5,6},{6,5},{7,4},{8,11},{9,10},{10,... | collective-permute-start | bytes 294920 | tf_op jit(solution)/shard_map/ppermute | solution.py:331
  66.2 7.8 %collective-permute-start.28 = (bf16[4,16,768]{2,1,0:T(8,128)(2,1)S(1)}, bf16[4,16,768]{2,1,0:T(8,128)(2,1)S(1)}, u32[]{:S(2)}, u32[]{:S(2)}) collective-permute-start(bf16[4,16,768]{2,1,0:T(8,128)(2,1)S(1)} %pad_maximum_fusion.18), channel_id=1, source_target_pairs={{0,2},{1,3},{2,0},{3,1},{4,6},{5,7},{6,4},{7,5},{8,10},{9,11},{10,... | collective-permute-start | bytes 294920 | tf_op jit(solution)/shard_map/ppermute | solution.py:331
  67.1 9.0 %collective-permute-start.27 = (bf16[4,16,768]{2,1,0:T(8,128)(2,1)S(1)}, bf16[4,16,768]{2,1,0:T(8,128)(2,1)S(1)}, u32[]{:S(2)}, u32[]{:S(2)}) collective-permute-start(bf16[4,16,768]{2,1,0:T(8,128)(2,1)S(1)} %pad_maximum_fusion.17), channel_id=1, source_target_pairs={{0,1},{1,0},{2,3},{3,2},{4,5},{5,4},{6,7},{7,6},{8,9},{9,8},{10,11... | collective-permute-start | bytes 294920 | tf_op jit(solution)/shard_map/ppermute | solution.py:331
  67.7 14.0 %collective-permute-start.23 = (bf16[4,16,768]{2,1,0:T(8,128)(2,1)S(1)}, bf16[4,16,768]{2,1,0:T(8,128)(2,1)S(1)}, u32[]{:S(2)}, u32[]{:S(2)}) collective-permute-start(bf16[4,16,768]{2,1,0:T(8,128)(2,1)S(1)} %pad_maximum_fusion.15), channel_id=1, source_target_pairs={{0,3},{1,2},{2,1},{3,0},{4,7},{5,6},{6,5},{7,4},{8,11},{9,10},{10,... | collective-permute-start | bytes 294920 | tf_op jit(solution)/shard_map/ppermute | solution.py:331
  69.0 23.4 %collective-permute-start.22 = (bf16[4,16,768]{2,1,0:T(8,128)(2,1)S(1)}, bf16[4,16,768]{2,1,0:T(8,128)(2,1)S(1)}, u32[]{:S(2)}, u32[]{:S(2)}) collective-permute-start(bf16[4,16,768]{2,1,0:T(8,128)(2,1)S(1)} %pad_maximum_fusion.14), channel_id=1, source_target_pairs={{0,2},{1,3},{2,0},{3,1},{4,6},{5,7},{6,4},{7,5},{8,10},{9,11},{10,... | collective-permute-start | bytes 294920 | tf_op jit(solution)/shard_map/ppermute | solution.py:331
  71.1 21.3 %collective-permute-start.21 = (bf16[4,16,768]{2,1,0:T(8,128)(2,1)S(1)}, bf16[4,16,768]{2,1,0:T(8,128)(2,1)S(1)}, u32[]{:S(2)}, u32[]{:S(2)}) collective-permute-start(bf16[4,16,768]{2,1,0:T(8,128)(2,1)S(1)} %pad_maximum_fusion.13), channel_id=1, source_target_pairs={{0,1},{1,0},{2,3},{3,2},{4,5},{5,4},{6,7},{7,6},{8,9},{9,8},{10,11... | collective-permute-start | bytes 294920 | tf_op jit(solution)/shard_map/ppermute | solution.py:331
  74.0 29.0 %collective-permute-start.11 = (bf16[4,32,768]{2,1,0:T(8,128)(2,1)S(1)}, bf16[4,32,768]{2,1,0:T(8,128)(2,1)S(1)}, u32[]{:S(2)}, u32[]{:S(2)}) collective-permute-start(bf16[4,32,768]{2,1,0:T(8,128)(2,1)S(1)} %pad_maximum_fusion.7), channel_id=1, source_target_pairs={{0,12},{1,13},{2,14},{3,15},{4,8},{5,9},{6,10},{7,11},{8,4},{9,5},... | collective-permute-start | bytes 589832 | tf_op jit(solution)/shard_map/ppermute | solution.py:331
  76.1 26.8 %collective-permute-start.10 = (bf16[4,32,768]{2,1,0:T(8,128)(2,1)S(1)}, bf16[4,32,768]{2,1,0:T(8,128)(2,1)S(1)}, u32[]{:S(2)}, u32[]{:S(2)}) collective-permute-start(bf16[4,32,768]{2,1,0:T(8,128)(2,1)S(1)} %pad_maximum_fusion.6), channel_id=1, source_target_pairs={{0,8},{1,9},{2,10},{3,11},{4,12},{5,13},{6,14},{7,15},{8,0},{9,1},... | collective-permute-start | bytes 589832 | tf_op jit(solution)/shard_map/ppermute | solution.py:331
  81.7 21.3 %collective-permute-start.9 = (bf16[4,32,768]{2,1,0:T(8,128)(2,1)S(1)}, bf16[4,32,768]{2,1,0:T(8,128)(2,1)S(1)}, u32[]{:S(2)}, u32[]{:S(2)}) collective-permute-start(bf16[4,32,768]{2,1,0:T(8,128)(2,1)S(1)} %pad_maximum_fusion.5), channel_id=1, source_target_pairs={{0,4},{1,5},{2,6},{3,7},{4,0},{5,1},{6,2},{7,3},{8,12},{9,13},{10,... | collective-permute-start | bytes 589832 | tf_op jit(solution)/shard_map/ppermute | solution.py:331
  (5 other events, 24.7 us)

commit v2 on v1

v2 whole, which is shorter than its diff:
```python
import functools

import jax
import jax.numpy as jnp
from jax import lax
from jax.experimental import pallas as pl
from jax.experimental.pallas import tpu as pltpu
from jax.sharding import PartitionSpec as P

WIDE = jnp.float32
NARROW = jnp.bfloat16
MIB = 1 << 20
VMEM = pltpu.VMEM
ANY = pltpu.HBM


def params(mib):
    return pltpu.CompilerParams(vmem_limit_bytes=mib * MIB)


def cost(flops, nbytes):
    return pl.CostEstimate(flops=flops, bytes_accessed=nbytes, transcendentals=0)


def split_matrix(rank, rows, n, order):
    total = rows * n
    shape = (total, total)
    i = lax.broadcasted_iota(jnp.int32, shape, 0)
    j = lax.broadcasted_iota(jnp.int32, shape, 1)
    slab, block = i // rows, i % rows
    k = order(slab)
    return ((j // n == block) & (j % n == (rank ^ k))).astype(NARROW)


def merge_matrix(rank, rows, n, order):
    total = rows * n
    shape = (total, total)
    i = lax.broadcasted_iota(jnp.int32, shape, 0)
    j = lax.broadcasted_iota(jnp.int32, shape, 1)
    slab, block = j // rows, j % rows
    k = order(slab)
    return ((i // n == block) & (i % n == (rank ^ k))).astype(NARROW)


def count_of(n, mode):
    by_inner, inner = mode
    return inner if by_inner else n // inner


def number(mode, group, member):
    by_inner, inner = mode
    return member * inner + group if by_inner else group * inner + member


def major(n, mode):
    each = n // count_of(n, mode)
    return lambda place: number(mode, place // each, place % each)


def dot(a, b, dims):
    return lax.dot_general(a, b, (dims, ((), ())), preferred_element_type=WIDE)


def gated_kernel(n, mode, rows, g_ref, d_ref, *refs):
    count = count_of(n, mode)
    out_refs, matrix = refs[:count], refs[count]
    @pl.when(pl.program_id(0) == 0)
    def _():
        matrix[...] = split_matrix(lax.axis_index("seq"), rows, n, major(n, mode))

    gated = (g_ref[...].astype(WIDE) * d_ref[...].astype(WIDE)).astype(NARROW)
    span = n // count * rows
    for o in range(count):
        out_refs[o][...] = dot(matrix[o * span : (o + 1) * span, :], gated, ((1,), (0,))).astype(NARROW)


def gated_slabs(gate_in, cotangent, mode):
    rows, n, channels = gate_in.shape
    total = rows * n
    chunks = 3 if channels % 384 == 0 else 1
    wide = channels // chunks
    count = count_of(n, mode)
    span = n // count * rows
    out = pl.pallas_call(
        functools.partial(gated_kernel, n, mode, rows),
        grid=(chunks,),
        in_specs=[pl.BlockSpec((total, wide), lambda i: (0, i))] * 2,
        out_specs=[pl.BlockSpec((span, wide), lambda i: (0, i))] * count,
        out_shape=[jax.ShapeDtypeStruct((span, channels), NARROW)] * count,
        scratch_shapes=[VMEM((total, total), NARROW)],
        compiler_params=params(58),
        cost_estimate=cost(2 * total * total * channels, 6 * total * channels),
        name="gated_slabs",
    )(gate_in.reshape(total, channels), cotangent.reshape(total, channels))
    return [o.reshape(n // count, rows, channels) for o in out]


def inner_kernel(mode, group, w_ref, x_ref, *refs):
    n, length = w_ref.shape[1:]
    count = count_of(n, mode)
    out_refs, (kept_a, kept_b, kept, sem) = refs[:count], refs[count:]
    rows = group * length
    blocks = w_ref.shape[0]
    steps = blocks // group // 2

    def fetch(i, kept_x, base):
        here = pl.ds(pl.multiple_of(i * rows, rows), rows)
        there = pl.ds(pl.multiple_of((base + i) * rows, rows), rows)
        return pltpu.make_async_copy(x_ref.at[there, :], kept_x.at[here, :], sem.at[base + i])

    parts = ((kept_a, 0), (kept_b, steps))
    for kept_x, base in parts:
        for i in range(steps):
            fetch(i, kept_x, base).start()
    matrix = split_matrix(lax.axis_index("seq"), blocks, n, major(n, mode))
    for kept_x, base in parts:

        def step(i, carry, kept_x=kept_x, base=base):
            fetch(i, kept_x, base).wait()
            for g in range(group):
                block = (base + i) * group + g
                x = kept_x[pl.ds(pl.multiple_of((i * group + g) * length, length), length), :]
                u = dot(w_ref[block], x, ((1,), (0,)))
                kept[pl.ds(pl.multiple_of(block * n, n), n), :] = u.astype(NARROW)
            return carry

        lax.fori_loop(0, steps, step, 0)
    span = n // count * blocks
    for o in range(count):
        out_refs[o][...] = dot(matrix[o * span : (o + 1) * span, :], kept[...], ((1,), (0,))).astype(NARROW)


def inner_slabs(first_factor, values, mode):
    blocks, n, length = first_factor.shape
    channels = values.shape[1]
    group = 2 if blocks % 4 == 0 else 1
    count = count_of(n, mode)
    span = n // count * blocks
    half = VMEM((blocks // 2 * length, channels), NARROW)
    *out, kept_a, kept_b = pl.pallas_call(
        functools.partial(inner_kernel, mode, group),
        in_specs=[pl.BlockSpec(memory_space=VMEM), pl.BlockSpec(memory_space=ANY)],
        out_specs=[pl.BlockSpec(memory_space=VMEM)] * (count + 2),
        out_shape=[jax.ShapeDtypeStruct((span, channels), NARROW)] * count + [half] * 2,
        scratch_shapes=[VMEM((blocks * n, channels), NARROW), pltpu.SemaphoreType.DMA((blocks // group,))],
        compiler_params=params(32),
        cost_estimate=cost(2 * blocks * n * length * channels, 2 * blocks * length * channels),
        name="inner_slabs",
    )(first_factor, values)
    return [o.reshape(n // count, blocks, channels) for o in out], [kept_a, kept_b]


def mix_kernel(n, arrive, leave, transpose, s_ref, *refs):
    (arrive_mode, arrive_parts), (leave_mode, leave_parts) = arrive, leave
    arrive_n = count_of(n, arrive_mode)
    leave_n = count_of(n, leave_mode)
    in_refs = refs[: arrive_n * arrive_parts]
    out_refs = refs[arrive_n * arrive_parts :][: leave_n * leave_parts]
    whole_ref, product = refs[arrive_n * arrive_parts + leave_n * leave_parts :]
    rank = lax.axis_index("seq")
    rows = whole_ref.shape[0] // n

    def place(group, member, mode, part, parts):
        k = number(mode, group, member)
        size = rows // parts
        return pl.ds(pl.multiple_of((rank ^ k) * rows + part * size, size), size)

    for p in range(arrive_parts):
        for a in range(arrive_n):
            for b in range(n // arrive_n):
                whole_ref[place(a, b, arrive_mode, p, arrive_parts), :] = in_refs[p * arrive_n + a][b]
    product[...] = dot(s_ref[0], whole_ref[...], ((0 if transpose else 1,), (0,))).astype(NARROW)
    for p in range(leave_parts):
        for a in range(leave_n):
            for b in range(n // leave_n):
                out_refs[p * leave_n + a][b] = product[place(a, b, leave_mode, p, leave_parts), :]


def mix(second_factor, slabs, n, arrive, leave, transpose, name):
    total = second_factor.shape[1]
    channels = slabs[0][0].shape[2]
    leave_n = count_of(n, leave[0])
    part = total // n // leave[1]
    flat = [s for half in slabs for s in half]
    out = pl.pallas_call(
        functools.partial(mix_kernel, n, arrive, leave, transpose),
        in_specs=[pl.BlockSpec(memory_space=VMEM)] * (1 + len(flat)),
        out_specs=[pl.BlockSpec(memory_space=VMEM)] * (leave_n * leave[1] + 1),
        out_shape=[jax.ShapeDtypeStruct((n // leave_n, part, channels), NARROW)] * (leave_n * leave[1])
        + [jax.ShapeDtypeStruct((total, channels), NARROW)],
        scratch_shapes=[VMEM((total, channels), NARROW)],
        compiler_params=params(10),
        cost_estimate=cost(2 * total * total * channels, 4 * total * channels),
        name=name,
    )(second_factor, *flat)
    return [out[p * leave_n : (p + 1) * leave_n] for p in range(leave[1])], out[-1]


def grads_kernel(mode, slots, group, half, held, w_ref, *refs):
    n, length = w_ref.shape[1:]
    x_refs, refs = refs[:held], refs[held:]
    count = count_of(n, mode)
    slab_refs = refs[:count]
    refs = refs[count:] if half == 0 else refs[count + 2 :]
    vg_ref, fg_ref, slabs, back, fg_buf, out_buf, out_sem, fg_sem = refs
    part = slab_refs[0].shape[1]
    base = half * part
    steps = part // group
    rows = group * length

    def put(i, s):
        there = pl.ds(pl.multiple_of(base * length + i * rows, rows), rows)
        return pltpu.make_async_copy(out_buf.at[s], vg_ref.at[there, :], out_sem.at[s])

    every = n // count
    for o in range(count):
        for b in range(every):
            slabs[(o * every + b) * part : (o * every + b + 1) * part, :] = slab_refs[o][b]
    matrix = merge_matrix(lax.axis_index("seq"), part, n, major(n, mode))
    back[...] = dot(matrix, slabs[...], ((1,), (0,))).astype(NARROW)

    each = steps // held

    def step(x_ref, start, i, carry):
        s = lax.rem(i, slots)

        @pl.when(i >= slots)
        def _():
            put(i - slots, s).wait()

        for g in range(group):
            block = i * group + g
            w = w_ref[base + block]
            f = back[pl.ds(pl.multiple_of(block * n, n), n), :]
            out_buf[s, g * length : (g + 1) * length, :] = dot(w, f, ((0,), (0,))).astype(NARROW)
            x = x_ref[pl.ds(pl.multiple_of((block - start * group) * length, length), length), :]
            fg_buf[block] = dot(f, x, ((1,), (1,))).astype(NARROW)
        put(i, s).start()
        return carry

    for h in range(held):
        lax.fori_loop(h * each, (h + 1) * each, functools.partial(step, x_refs[h], h * each), 0)
    last = pltpu.make_async_copy(fg_buf, fg_ref.at[pl.ds(base, part)], fg_sem)
    last.start()
    for i in range(steps - slots, steps):
        put(i, i % slots).wait()
    last.wait()


def grads(first_factor, kept_x, slabs, mode, half, earlier):
    blocks, n, length = first_factor.shape
    channels = kept_x[0].shape[1]
    held, count = len(kept_x), len(slabs)
    part = slabs[0].shape[1]
    group = next(g for g in (4, 2, 1) if part % g == 0)
    slots = min(3, part // group)
    shapes = [
        jax.ShapeDtypeStruct((blocks * length, channels), NARROW),
        jax.ShapeDtypeStruct(first_factor.shape, NARROW),
    ]
    return pl.pallas_call(
        functools.partial(grads_kernel, mode, slots, group, half, held),
        in_specs=[pl.BlockSpec(memory_space=VMEM)] * (1 + held + count)
        + ([] if half == 0 else [pl.BlockSpec(memory_space=ANY)] * 2),
        out_specs=[pl.BlockSpec(memory_space=ANY)] * 2,
        out_shape=shapes,
        input_output_aliases={} if half == 0 else {1 + held + count: 0, 2 + held + count: 1},
        scratch_shapes=[
            VMEM((part * n, channels), NARROW),
            VMEM((part * n, channels), NARROW),
            VMEM((part, n, length), NARROW),
            VMEM((slots, group * length, channels), NARROW),
            pltpu.SemaphoreType.DMA((slots,)),
            pltpu.SemaphoreType.DMA,
        ],
        compiler_params=params(16),
        cost_estimate=cost(4 * part * n * length * channels, 2 * part * length * channels),
        name="grads",
    )(first_factor, *kept_x, *slabs, *(earlier or ()))


def gates_kernel(n, mode, rows, g_ref, d_ref, *refs):
    count = count_of(n, mode)
    slab_refs, (mixed_ref, grad_ref, matrix, slabs) = refs[:count], refs[count:]
    @pl.when(pl.program_id(0) == 0)
    def _():
        matrix[...] = merge_matrix(lax.axis_index("seq"), rows, n, major(n, mode))

    span = n // count * rows
    for o in range(count):
        slabs[o * span : (o + 1) * span, :] = slab_refs[o][...]
    z = dot(matrix[...], slabs[...], ((1,), (0,)))
    mixed_ref[...] = (g_ref[...].astype(WIDE) * z).astype(NARROW)
    grad_ref[...] = (d_ref[...].astype(WIDE) * z).astype(NARROW)


def gates(gate_in, cotangent, slabs, mode):
    rows, n, channels = gate_in.shape
    total = rows * n
    chunks = 3 if channels % 384 == 0 else 1
    wide = channels // chunks
    count = count_of(n, mode)
    span = n // count * rows
    out = pl.pallas_call(
        functools.partial(gates_kernel, n, mode, rows),
        grid=(chunks,),
        in_specs=[pl.BlockSpec((total, wide), lambda i: (0, i))] * 2
        + [pl.BlockSpec((span, wide), lambda i: (0, i))] * count,
        out_specs=[pl.BlockSpec((total, wide), lambda i: (0, i))] * 2,
        out_shape=[jax.ShapeDtypeStruct((total, channels), NARROW)] * 2,
        scratch_shapes=[VMEM((total, total), NARROW), VMEM((total, wide), NARROW)],
        compiler_params=params(10),
        cost_estimate=cost(2 * total * total * channels, 10 * total * channels),
        name="gates",
    )(
        gate_in.reshape(total, channels),
        cotangent.reshape(total, channels),
        *[s.reshape(span, channels) for s in slabs],
    )
    return [o.reshape(gate_in.shape) for o in out]


def after(arrays, *tokens):
    return list(lax.optimization_barrier(tuple(arrays) + tokens)[: len(arrays)])


def regroup(slabs):
    count = slabs[0].shape[0]
    return [jnp.stack([s[b] for s in slabs]) for b in range(count)]


def by_permutes(values, gate_in, cotangent, first_factor, second_factor, inner):
    n = gate_in.shape[1]
    near, far = (True, inner), (False, inner)

    def permutes(slabs, step):
        got = list(slabs)
        count = len(slabs)
        for k in [2, 3, 1] if count == 4 else range(count - 1, 0, -1):
            got[k] = lax.ppermute(slabs[k], "seq", [(i, i ^ (k * step)) for i in range(n)])
        return got

    def across(slabs):
        return permutes(slabs, inner)

    def beside(slabs):
        return permutes(slabs, 1)

    gated = gated_slabs(gate_in, cotangent, far)
    e = across(gated)
    (factor,) = after([first_factor], gated[0])
    u, kept_x = inner_slabs(factor, values, far)
    e = beside(regroup(after(e, u[0])))
    u = across(u)
    (f,), e_all = mix(second_factor, [e], n, (near, 1), (far, 1), True, "back")
    f = across(f)
    u = beside(regroup(u))
    (z,), u_all = mix(second_factor, [u], n, (near, 1), (near, 1), False, "forth")
    z = across(regroup(beside(z)))
    f = beside(regroup(f))
    out = None
    part = gate_in.shape[0] // 2
    for half in range(2):
        slabs = [x[:, half * part : (half + 1) * part] for x in f]
        out = grads(first_factor, [kept_x[half]], slabs, near, half, out)
    values_grad, first_grad = out
    second_grad = dot(*after([e_all, u_all], first_grad), ((1,), (1,))).astype(NARROW)[None]
    gate_in, cotangent = after([gate_in, cotangent], first_grad)
    mixed, gate_grad = gates(gate_in, cotangent, z, far)
    return mixed, values_grad, gate_grad, first_grad, second_grad


def by_all_to_all(values, gate_in, cotangent, first_factor, second_factor):
    block_len = first_factor.shape[2]
    channels = values.shape[1]
    blocks_x = values.reshape(-1, block_len, channels)
    inner = jnp.einsum("aqp,apc->aqc", first_factor, blocks_x, preferred_element_type=WIDE).astype(NARROW)
    gated = (gate_in.astype(WIDE) * cotangent.astype(WIDE)).astype(NARROW)
    inner_t = lax.all_to_all(inner, "seq", split_axis=1, concat_axis=0, tiled=True)
    outer_t = jnp.einsum("qxa,aqc->xqc", second_factor, inner_t, preferred_element_type=WIDE).astype(NARROW)
    outer = lax.all_to_all(outer_t, "seq", split_axis=0, concat_axis=1, tiled=True)
    gated_t = lax.all_to_all(gated, "seq", split_axis=1, concat_axis=0, tiled=True)
    second_grad = jnp.einsum("xqc,aqc->qxa", gated_t, inner_t, preferred_element_type=WIDE).astype(NARROW)
    back_t = jnp.einsum("qxa,xqc->aqc", second_factor, gated_t, preferred_element_type=WIDE).astype(NARROW)
    back_inner = lax.all_to_all(back_t, "seq", split_axis=0, concat_axis=1, tiled=True)
    outer_f = outer.astype(WIDE)
    mixed = (gate_in.astype(WIDE) * outer_f).astype(NARROW)
    gate_grad = (cotangent.astype(WIDE) * outer_f).astype(NARROW)
    first_grad = jnp.einsum("aqc,apc->aqp", back_inner, blocks_x, preferred_element_type=WIDE).astype(NARROW)
    values_grad = (
        jnp.einsum("aqp,aqc->apc", first_factor, back_inner, preferred_element_type=WIDE)
        .astype(NARROW)
        .reshape(-1, channels)
    )
    return mixed, values_grad, gate_grad, first_grad, second_grad


def solution(mesh):
    n = mesh.shape["seq"]

    def on_device(values, gate_in, cotangent, first_factor, second_factor):
        rows, kept = gate_in.shape[:2]
        if n == 16 and kept == n and rows % 32 == 0 and first_factor.shape[0] == rows:
            return by_permutes(values, gate_in, cotangent, first_factor, second_factor, 4)
        return by_all_to_all(values, gate_in, cotangent, first_factor, second_factor)

    both = ("grp", "seq")
    return jax.shard_map(
        on_device,
        mesh=mesh,
        in_specs=(
            P(both, None),
            P(both, None, None),
            P(both, None, None),
            P("seq", None, None),
            P("seq", None, None),
        ),
        out_specs=(
            P(both, None, None),
            P(both, None),
            P(both, None, None),
            P(both, None, None),
            P(both, None, None),
        ),
        check_vma=False,
    )
```

time: 106 us -> 98.2 us (0.926)
  the two profiles are of different devices: /device:TPU:0 before, /device:TPU:11 now
where the time goes in v2:
time: 98.2 us; the launch traced here: 97.3 us
  Pallas kernels  35 us (36%)
  starting transfers between devices  32.3 us (33%)
  waiting for transfers between devices  25.8 us (26%)
  matrix products  1.4 us (1%)
  local copies, waits for them, and re-layouts  1.18 us (1%)
  between operations  1.08 us (1%)
    ppermute x24, starting transfers between devices, permutes(): lax.ppermute(slabs[k], 'seq', [(i, i ^ k * step) for i in range(n)])  32.3 us
    ppermute x24, waiting for transfers between devices, permutes(): lax.ppermute(slabs[k], 'seq', [(i, i ^ k * step) for i in range(n)])  25.8 us
    pallas_call x2, Pallas kernels, grads(): pl.pallas_call(functools.partial(grads_kernel, mode, slots, group, half,...  16.5 us
    pallas_call x1, Pallas kernels, inner_slabs(): pl.pallas_call(functools.partial(inner_kernel, mode, group), in_specs=[pl...  11 us
    pallas_call x1, Pallas kernels, gated_slabs(): pl.pallas_call(functools.partial(gated_kernel, n, mode, rows), grid=(chun...  3.67 us
    pallas_call x1, Pallas kernels, gates(): pl.pallas_call(functools.partial(gates_kernel, n, mode, rows), grid=(chun...  2.53 us
  transfers between devices with their start and end apart: 24, of which 8 were waited for; matrix products, arithmetic and copies ran while one was open for 3% of the time, Pallas kernels for 30%

profile of v2, /device:TPU:11, one launch (start us, length us, event | category | flops | bytes accessed | tf_op | source)
XLA Modules:
  0.0 97.3 jit_solution(11610411668940030346)
XLA Ops:
  0.7 3.7 %gated_slabs.1 = (bf16[128,768]{1,0:T(8,128)(2,1)}, bf16[128,768]{1,0:T(8,128)(2,1)}, bf16[128,768]{1,0:T(8,128)(2,1)}, bf16[128,768]{1,0:T(8,128)(2,1)}) custom-call(bf16[512,768]{1,0:T(8,128)(2,1)} %bitcast.29, bf16[512,768]{1,0:T(8,128)(2,1)} %bitcast.31), custom_call_target="tpu_custom_call" | custom-call | flops 402653184 | bytes 2359296 | tf_op jit(solution)/shard_map/gated_slabs/pallas_call | solution.py:84
  4.6 2.3 %collective-permute-start.1 = (bf16[4,32,768]{2,1,0:T(8,128)(2,1)}, bf16[4,32,768]{2,1,0:T(8,128)(2,1)S(1)}, u32[]{:S(2)}, u32[]{:S(2)}) collective-permute-start(bf16[4,32,768]{2,1,0:T(8,128)(2,1)} %bitcast.44), channel_id=1, source_target_pairs={{0,8},{1,9},{2,10},{3,11},{4,12},{5,13},{6,14},{7,15},{8,0},{9,1},... | collective-permute-start | bytes 589832 | tf_op jit(solution)/shard_map/ppermute | solution.py:340
  7.0 11.0 %inner_slabs.1 = (bf16[128,768]{1,0:T(8,128)(2,1)}, bf16[128,768]{1,0:T(8,128)(2,1)}, bf16[128,768]{1,0:T(8,128)(2,1)}, bf16[128,768]{1,0:T(8,128)(2,1)}, bf16[8...) custom-call(bf16[32,16,512]{2,1,0:T(8,128)(2,1)} %w_ref.4, bf16[16384,768]{1,0:T(8,128)(2,1)} %x_ref.1), custom_call_target="tpu_custom_call" | custom-call | flops 402653184 | bytes 25165824 | tf_op jit(solution)/shard_map/inner_slabs/pallas_call | solution.py:140
  18.0 1.4 %collective-permute-start.14 = (bf16[4,32,768]{2,1,0:T(8,128)(2,1)}, bf16[4,32,768]{2,1,0:T(8,128)(2,1)S(1)}, u32[]{:S(2)}, u32[]{:S(2)}) collective-permute-start(bf16[4,32,768]{2,1,0:T(8,128)(2,1)} %bitcast.42), channel_id=1, source_target_pairs={{0,12},{1,13},{2,14},{3,15},{4,8},{5,9},{6,10},{7,11},{8,4},{9,5},... | collective-permute-start | bytes 589832 | tf_op jit(solution)/shard_map/ppermute | solution.py:340
  19.4 3.1 %collective-permute-start.12 = (bf16[4,32,768]{2,1,0:T(8,128)(2,1)}, bf16[4,32,768]{2,1,0:T(8,128)(2,1)S(1)}, u32[]{:S(2)}, u32[]{:S(2)}) collective-permute-start(bf16[4,32,768]{2,1,0:T(8,128)(2,1)} %bitcast.41), channel_id=1, source_target_pairs={{0,4},{1,5},{2,6},{3,7},{4,0},{5,1},{6,2},{7,3},{8,12},{9,13},{10,... | collective-permute-start | bytes 589832 | tf_op jit(solution)/shard_map/ppermute | solution.py:340
  22.5 0.9 slice_bitcast_fusion
  23.5 3.9 %collective-permute-done.2 = bf16[4,32,768]{2,1,0:T(8,128)(2,1)S(1)} collective-permute-done((bf16[4,32,768]{2,1,0:T(8,128)(2,1)}, bf16[4,32,768]{2,1,0:T(8,128)(2,1)S(1)}, u32[]{:S(2)}, u32[]{:S(2)}) %collective-permute-start.2) | collective-permute-done | bytes 196640 | tf_op jit(solution)/shard_map/ppermute | solution.py:340
  27.5 5.7 %collective-permute-start.5 = (bf16[4,32,768]{2,1,0:T(8,128)(2,1)S(1)}, bf16[4,32,768]{2,1,0:T(8,128)(2,1)S(1)}, u32[]{:S(2)}, u32[]{:S(2)}) collective-permute-start(bf16[4,32,768]{2,1,0:T(8,128)(2,1)S(1)} %pad_maximum_fusion.3), channel_id=1, source_target_pairs={{0,3},{1,2},{2,1},{3,0},{4,7},{5,6},{6,5},{7,4},{8,11},{9,10},{10,... | collective-permute-start | bytes 589832 | tf_op jit(solution)/shard_map/ppermute | solution.py:340
  33.3 1.5 %collective-permute-start.4 = (bf16[4,32,768]{2,1,0:T(8,128)(2,1)S(1)}, bf16[4,32,768]{2,1,0:T(8,128)(2,1)S(1)}, u32[]{:S(2)}, u32[]{:S(2)}) collective-permute-start(bf16[4,32,768]{2,1,0:T(8,128)(2,1)S(1)} %pad_maximum_fusion.2), channel_id=1, source_target_pairs={{0,2},{1,3},{2,0},{3,1},{4,6},{5,7},{6,4},{7,5},{8,10},{9,11},{10,... | collective-permute-start | bytes 589832 | tf_op jit(solution)/shard_map/ppermute | solution.py:340
  34.8 1.8 %collective-permute-done.14 = bf16[4,32,768]{2,1,0:T(8,128)(2,1)S(1)} collective-permute-done((bf16[4,32,768]{2,1,0:T(8,128)(2,1)}, bf16[4,32,768]{2,1,0:T(8,128)(2,1)S(1)}, u32[]{:S(2)}, u32[]{:S(2)}) %collective-permute-start.14) | collective-permute-done | bytes 196640 | tf_op jit(solution)/shard_map/ppermute | solution.py:340
  36.6 3.2 %collective-permute-start.3 = (bf16[4,32,768]{2,1,0:T(8,128)(2,1)S(1)}, bf16[4,32,768]{2,1,0:T(8,128)(2,1)S(1)}, u32[]{:S(2)}, u32[]{:S(2)}) collective-permute-start(bf16[4,32,768]{2,1,0:T(8,128)(2,1)S(1)} %pad_maximum_fusion.1), channel_id=1, source_target_pairs={{0,1},{1,0},{2,3},{3,2},{4,5},{5,4},{6,7},{7,6},{8,9},{9,8},{10,11... | collective-permute-start | bytes 589832 | tf_op jit(solution)/shard_map/ppermute | solution.py:340
  40.1 2.0 %collective-permute-start.17 = (bf16[4,32,768]{2,1,0:T(8,128)(2,1)S(1)}, bf16[4,32,768]{2,1,0:T(8,128)(2,1)S(1)}, u32[]{:S(2)}, u32[]{:S(2)}) collective-permute-start(bf16[4,32,768]{2,1,0:T(8,128)(2,1)S(1)} %pad_maximum_fusion.11), channel_id=1, source_target_pairs={{0,3},{1,2},{2,1},{3,0},{4,7},{5,6},{6,5},{7,4},{8,11},{9,10},{10,... | collective-permute-start | bytes 589832 | tf_op jit(solution)/shard_map/ppermute | solution.py:340
  42.1 1.3 %collective-permute-start.16 = (bf16[4,32,768]{2,1,0:T(8,128)(2,1)S(1)}, bf16[4,32,768]{2,1,0:T(8,128)(2,1)S(1)}, u32[]{:S(2)}, u32[]{:S(2)}) collective-permute-start(bf16[4,32,768]{2,1,0:T(8,128)(2,1)S(1)} %pad_maximum_fusion.10), channel_id=1, source_target_pairs={{0,2},{1,3},{2,0},{3,1},{4,6},{5,7},{6,4},{7,5},{8,10},{9,11},{10,... | collective-permute-start | bytes 589832 | tf_op jit(solution)/shard_map/ppermute | solution.py:340
  43.6 0.7 back.1
  44.3 2.0 %collective-permute-start.6 = (bf16[4,32,768]{2,1,0:T(8,128)(2,1)S(1)}, bf16[4,32,768]{2,1,0:T(8,128)(2,1)S(1)}, u32[]{:S(2)}, u32[]{:S(2)}) collective-permute-start(bf16[4,32,768]{2,1,0:T(8,128)(2,1)S(1)} %get-tuple-element.51), channel_id=1, source_target_pairs={{0,4},{1,5},{2,6},{3,7},{4,0},{5,1},{6,2},{7,3},{8,12},{9,13},{10,... | collective-permute-start | bytes 589832 | tf_op jit(solution)/shard_map/ppermute | solution.py:340
  46.4 1.1 %collective-permute-start.7 = (bf16[4,32,768]{2,1,0:T(8,128)(2,1)S(1)}, bf16[4,32,768]{2,1,0:T(8,128)(2,1)S(1)}, u32[]{:S(2)}, u32[]{:S(2)}) collective-permute-start(bf16[4,32,768]{2,1,0:T(8,128)(2,1)S(1)} %get-tuple-element.52), channel_id=1, source_target_pairs={{0,8},{1,9},{2,10},{3,11},{4,12},{5,13},{6,14},{7,15},{8,0},{9,1},... | collective-permute-start | bytes 589832 | tf_op jit(solution)/shard_map/ppermute | solution.py:340
  47.5 1.2 %collective-permute-start.8 = (bf16[4,32,768]{2,1,0:T(8,128)(2,1)S(1)}, bf16[4,32,768]{2,1,0:T(8,128)(2,1)S(1)}, u32[]{:S(2)}, u32[]{:S(2)}) collective-permute-start(bf16[4,32,768]{2,1,0:T(8,128)(2,1)S(1)} %get-tuple-element.53), channel_id=1, source_target_pairs={{0,12},{1,13},{2,14},{3,15},{4,8},{5,9},{6,10},{7,11},{8,4},{9,5},... | collective-permute-start | bytes 589832 | tf_op jit(solution)/shard_map/ppermute | solution.py:340
  48.7 3.3 %collective-permute-done.16.refs_2_ = bf16[4,32,768]{2,1,0:T(8,128)(2,1)S(1)} collective-permute-done((bf16[4,32,768]{2,1,0:T(8,128)(2,1)S(1)}, bf16[4,32,768]{2,1,0:T(8,128)(2,1)S(1)}, u32[]{:S(2)}, u32[]{:S(2)}) %collective-permute-start.16) | collective-permute-done | bytes 196640 | tf_op jit(solution)/shard_map/ppermute | solution.py:340
  52.1 0.7 forth.1
  52.8 1.6 %collective-permute-start.19 = (bf16[4,32,768]{2,1,0:T(8,128)(2,1)S(1)}, bf16[4,32,768]{2,1,0:T(8,128)(2,1)S(1)}, u32[]{:S(2)}, u32[]{:S(2)}) collective-permute-start(bf16[4,32,768]{2,1,0:T(8,128)(2,1)S(1)} %get-tuple-element.66), channel_id=1, source_target_pairs={{0,2},{1,3},{2,0},{3,1},{4,6},{5,7},{6,4},{7,5},{8,10},{9,11},{10,... | collective-permute-start | bytes 589832 | tf_op jit(solution)/shard_map/ppermute | solution.py:340
  54.4 1.0 %collective-permute-start.20 = (bf16[4,32,768]{2,1,0:T(8,128)(2,1)S(1)}, bf16[4,32,768]{2,1,0:T(8,128)(2,1)S(1)}, u32[]{:S(2)}, u32[]{:S(2)}) collective-permute-start(bf16[4,32,768]{2,1,0:T(8,128)(2,1)S(1)} %get-tuple-element.67), channel_id=1, source_target_pairs={{0,3},{1,2},{2,1},{3,0},{4,7},{5,6},{6,5},{7,4},{8,11},{9,10},{10,... | collective-permute-start | bytes 589832 | tf_op jit(solution)/shard_map/ppermute | solution.py:340
  55.5 4.1 %collective-permute-done.7 = bf16[4,32,768]{2,1,0:T(8,128)(2,1)S(1)} collective-permute-done((bf16[4,32,768]{2,1,0:T(8,128)(2,1)S(1)}, bf16[4,32,768]{2,1,0:T(8,128)(2,1)S(1)}, u32[]{:S(2)}, u32[]{:S(2)}) %collective-permute-start.7) | collective-permute-done | bytes 196640 | tf_op jit(solution)/shard_map/ppermute | solution.py:340
  59.6 5.3 %collective-permute-done.8 = bf16[4,32,768]{2,1,0:T(8,128)(2,1)S(1)} collective-permute-done((bf16[4,32,768]{2,1,0:T(8,128)(2,1)S(1)}, bf16[4,32,768]{2,1,0:T(8,128)(2,1)S(1)}, u32[]{:S(2)}, u32[]{:S(2)}) %collective-permute-start.8) | collective-permute-done | bytes 196640 | tf_op jit(solution)/shard_map/ppermute | solution.py:340
  65.0 1.6 %collective-permute-start.11 = (bf16[4,32,768]{2,1,0:T(8,128)(2,1)S(1)}, bf16[4,32,768]{2,1,0:T(8,128)(2,1)S(1)}, u32[]{:S(2)}, u32[]{:S(2)}) collective-permute-start(bf16[4,32,768]{2,1,0:T(8,128)(2,1)S(1)} %pad_maximum_fusion.7), channel_id=1, source_target_pairs={{0,3},{1,2},{2,1},{3,0},{4,7},{5,6},{6,5},{7,4},{8,11},{9,10},{10,... | collective-permute-start | bytes 589832 | tf_op jit(solution)/shard_map/ppermute | solution.py:340
  66.6 1.2 %collective-permute-start.10 = (bf16[4,32,768]{2,1,0:T(8,128)(2,1)S(1)}, bf16[4,32,768]{2,1,0:T(8,128)(2,1)S(1)}, u32[]{:S(2)}, u32[]{:S(2)}) collective-permute-start(bf16[4,32,768]{2,1,0:T(8,128)(2,1)S(1)} %pad_maximum_fusion.6), channel_id=1, source_target_pairs={{0,2},{1,3},{2,0},{3,1},{4,6},{5,7},{6,4},{7,5},{8,10},{9,11},{10,... | collective-permute-start | bytes 589832 | tf_op jit(solution)/shard_map/ppermute | solution.py:340
  68.0 1.3 %collective-permute-start.23 = (bf16[4,32,768]{2,1,0:T(8,128)(2,1)S(1)}, bf16[4,32,768]{2,1,0:T(8,128)(2,1)S(1)}, u32[]{:S(2)}, u32[]{:S(2)}) collective-permute-start(bf16[4,32,768]{2,1,0:T(8,128)(2,1)S(1)} %pad_maximum_fusion.15), channel_id=1, source_target_pairs={{0,12},{1,13},{2,14},{3,15},{4,8},{5,9},{6,10},{7,11},{8,4},{9,5},... | collective-permute-start | bytes 589832 | tf_op jit(solution)/shard_map/ppermute | solution.py:340
  69.6 2.3 %collective-permute-done.11 = bf16[4,32,768]{2,1,0:T(8,128)(2,1)S(1)} collective-permute-done((bf16[4,32,768]{2,1,0:T(8,128)(2,1)S(1)}, bf16[4,32,768]{2,1,0:T(8,128)(2,1)S(1)}, u32[]{:S(2)}, u32[]{:S(2)}) %collective-permute-start.11) | collective-permute-done | bytes 196640 | tf_op jit(solution)/shard_map/ppermute | solution.py:340
  72.0 4.8 %collective-permute-done.10 = bf16[4,32,768]{2,1,0:T(8,128)(2,1)S(1)} collective-permute-done((bf16[4,32,768]{2,1,0:T(8,128)(2,1)S(1)}, bf16[4,32,768]{2,1,0:T(8,128)(2,1)S(1)}, u32[]{:S(2)}, u32[]{:S(2)}) %collective-permute-start.10) | collective-permute-done | bytes 196640 | tf_op jit(solution)/shard_map/ppermute | solution.py:340
  76.8 8.2 %grads.2 = (bf16[16384,768]{1,0:T(8,128)(2,1)}, bf16[32,16,512]{2,1,0:T(8,128)(2,1)}) custom-call(bf16[32,16,512]{2,1,0:T(8,128)(2,1)S(1)} %copy-done, bf16[8192,768]{1,0:T(8,128)(2,1)S(1)} %get-tuple-element.54.refs_0_, bf16[4,16,768]{2,1,0:T(8,128)(2,1)S(1)} %get-tuple-element.113.refs_1_, bf16[4,16,768]{2,1,0:T(8,128)(2,1)S(1)} %get-tuple-element.111.refs_2_, ...), custom_call_target="tpu_custom_call" | custom-call | flops 402653184 | bytes 12582912 | tf_op jit(solution)/shard_map/grads/pallas_call | solution.py:261
  85.1 8.2 %grads.3 = (bf16[16384,768]{1,0:T(8,128)(2,1)}, bf16[32,16,512]{2,1,0:T(8,128)(2,1)}) custom-call(bf16[32,16,512]{2,1,0:T(8,128)(2,1)S(1)} %copy-done, bf16[8192,768]{1,0:T(8,128)(2,1)S(1)} %get-tuple-element.42.refs_0_, bf16[4,16,768]{2,1,0:T(8,128)(2,1)S(1)} %get-tuple-element.114.refs_1_, ...), custom_call_target="tpu_custom_call", output_to_operand_aliasing={{0}: (6, {}), {1}: (7, {})} | custom-call | flops 402653184 | bytes 12582912 | tf_op jit(solution)/shard_map/grads/pallas_call | solution.py:261
  93.3 1.4 %fusion = bf16[1,512,512]{2,1,0:T(8,128)(2,1)} fusion(bf16[512,768]{1,0:T(8,128)(2,1)S(1)} %get-tuple-element.73, bf16[512,768]{1,0:T(8,128)(2,1)S(1)} %get-tuple-element.74), kind=kOutput, calls=%fused_computation.1 | convolution fusion | flops 402915328 | bytes 2097152 | tf_op jit(solution)/shard_map/dot_general | solution.py:61
  94.7 2.5 %gates.1 = (bf16[512,768]{1,0:T(8,128)(2,1)}, bf16[512,768]{1,0:T(8,128)(2,1)}) custom-call(bf16[512,768]{1,0:T(8,128)(2,1)S(1)} %bitcast.30, bf16[512,768]{1,0:T(8,128)(2,1)S(1)} %bitcast.32, bf16[128,768]{1,0:T(8,128)(2,1)S(1)} %bitcast.33, bf16[128,768]{1,0:T(8,128)(2,1)S(1)} %bitcast.36, bf16[128,768]{1,0:T(8,128)(2,1)S(1)} %bitcast.35, ...), custom_call_target="tpu_custom_call" | custom-call | flops 402653184 | bytes 3932160 | tf_op jit(solution)/shard_map/gates/pallas_call | solution.py:304
  (68 shorter events, 1.7 us)
Async XLA Ops:
  0.6 76.1 %copy-start = (bf16[32,16,512]{2,1,0:T(8,128)(2,1)S(1)}, bf16[32,16,512]{2,1,0:T(8,128)(2,1)}, u32[]{:S(2)}) copy-start(bf16[32,16,512]{2,1,0:T(8,128)(2,1)} %w_ref.4) | copy-start | bytes 1572868
  0.6 43.0 %copy-start.3 = (bf16[1,512,512]{2,1,0:T(8,128)(2,1)S(1)}, bf16[1,512,512]{2,1,0:T(8,128)(2,1)}, u32[]{:S(2)}) copy-start(bf16[1,512,512]{2,1,0:T(8,128)(2,1)} %s_ref.3) | copy-start | bytes 1572868
  4.3 23.1 %copy-start.4 = (bf16[128,768]{1,0:T(8,128)(2,1)S(1)}, bf16[128,768]{1,0:T(8,128)(2,1)}, u32[]{:S(2)}) copy-start(bf16[128,768]{1,0:T(8,128)(2,1)} %get-tuple-element.40) | copy-start | bytes 589828
  4.3 19.0 %collective-permute-start = (bf16[4,32,768]{2,1,0:T(8,128)(2,1)}, bf16[4,32,768]{2,1,0:T(8,128)(2,1)S(1)}, u32[]{:S(2)}, u32[]{:S(2)}) collective-permute-start(bf16[4,32,768]{2,1,0:T(8,128)(2,1)} %bitcast.45), channel_id=1, source_target_pairs={{0,4},{1,5},{2,6},{3,7},{4,0},{5,1},{6,2},{7,3},{8,12},{9,13},{10,... | collective-permute-start | bytes 589832 | tf_op jit(solution)/shard_map/ppermute | solution.py:340
  4.6 18.9 %collective-permute-start.1 = (bf16[4,32,768]{2,1,0:T(8,128)(2,1)}, bf16[4,32,768]{2,1,0:T(8,128)(2,1)S(1)}, u32[]{:S(2)}, u32[]{:S(2)}) collective-permute-start(bf16[4,32,768]{2,1,0:T(8,128)(2,1)} %bitcast.44), channel_id=1, source_target_pairs={{0,8},{1,9},{2,10},{3,11},{4,12},{5,13},{6,14},{7,15},{8,0},{9,1},... | collective-permute-start | bytes 589832 | tf_op jit(solution)/shard_map/ppermute | solution.py:340
  6.9 20.5 %collective-permute-start.2 = (bf16[4,32,768]{2,1,0:T(8,128)(2,1)}, bf16[4,32,768]{2,1,0:T(8,128)(2,1)S(1)}, u32[]{:S(2)}, u32[]{:S(2)}) collective-permute-start(bf16[4,32,768]{2,1,0:T(8,128)(2,1)} %bitcast.43), channel_id=1, source_target_pairs={{0,12},{1,13},{2,14},{3,15},{4,8},{5,9},{6,10},{7,11},{8,4},{9,5},... | collective-permute-start | bytes 589832 | tf_op jit(solution)/shard_map/ppermute | solution.py:340
  18.0 18.6 %collective-permute-start.14 = (bf16[4,32,768]{2,1,0:T(8,128)(2,1)}, bf16[4,32,768]{2,1,0:T(8,128)(2,1)S(1)}, u32[]{:S(2)}, u32[]{:S(2)}) collective-permute-start(bf16[4,32,768]{2,1,0:T(8,128)(2,1)} %bitcast.42), channel_id=1, source_target_pairs={{0,12},{1,13},{2,14},{3,15},{4,8},{5,9},{6,10},{7,11},{8,4},{9,5},... | collective-permute-start | bytes 589832 | tf_op jit(solution)/shard_map/ppermute | solution.py:340
  19.4 20.5 %collective-permute-start.12 = (bf16[4,32,768]{2,1,0:T(8,128)(2,1)}, bf16[4,32,768]{2,1,0:T(8,128)(2,1)S(1)}, u32[]{:S(2)}, u32[]{:S(2)}) collective-permute-start(bf16[4,32,768]{2,1,0:T(8,128)(2,1)} %bitcast.41), channel_id=1, source_target_pairs={{0,4},{1,5},{2,6},{3,7},{4,0},{5,1},{6,2},{7,3},{8,12},{9,13},{10,... | collective-permute-start | bytes 589832 | tf_op jit(solution)/shard_map/ppermute | solution.py:340
  23.4 16.6 %collective-permute-start.13 = (bf16[4,32,768]{2,1,0:T(8,128)(2,1)}, bf16[4,32,768]{2,1,0:T(8,128)(2,1)S(1)}, u32[]{:S(2)}, u32[]{:S(2)}) collective-permute-start(bf16[4,32,768]{2,1,0:T(8,128)(2,1)} %bitcast.40), channel_id=1, source_target_pairs={{0,8},{1,9},{2,10},{3,11},{4,12},{5,13},{6,14},{7,15},{8,0},{9,1},... | collective-permute-start | bytes 589832 | tf_op jit(solution)/shard_map/ppermute | solution.py:340
  27.5 16.0 %collective-permute-start.5 = (bf16[4,32,768]{2,1,0:T(8,128)(2,1)S(1)}, bf16[4,32,768]{2,1,0:T(8,128)(2,1)S(1)}, u32[]{:S(2)}, u32[]{:S(2)}) collective-permute-start(bf16[4,32,768]{2,1,0:T(8,128)(2,1)S(1)} %pad_maximum_fusion.3), channel_id=1, source_target_pairs={{0,3},{1,2},{2,1},{3,0},{4,7},{5,6},{6,5},{7,4},{8,11},{9,10},{10,... | collective-permute-start | bytes 589832 | tf_op jit(solution)/shard_map/ppermute | solution.py:340
  33.3 10.3 %collective-permute-start.4 = (bf16[4,32,768]{2,1,0:T(8,128)(2,1)S(1)}, bf16[4,32,768]{2,1,0:T(8,128)(2,1)S(1)}, u32[]{:S(2)}, u32[]{:S(2)}) collective-permute-start(bf16[4,32,768]{2,1,0:T(8,128)(2,1)S(1)} %pad_maximum_fusion.2), channel_id=1, source_target_pairs={{0,2},{1,3},{2,0},{3,1},{4,6},{5,7},{6,4},{7,5},{8,10},{9,11},{10,... | collective-permute-start | bytes 589832 | tf_op jit(solution)/shard_map/ppermute | solution.py:340
  36.6 7.0 %collective-permute-start.3 = (bf16[4,32,768]{2,1,0:T(8,128)(2,1)S(1)}, bf16[4,32,768]{2,1,0:T(8,128)(2,1)S(1)}, u32[]{:S(2)}, u32[]{:S(2)}) collective-permute-start(bf16[4,32,768]{2,1,0:T(8,128)(2,1)S(1)} %pad_maximum_fusion.1), channel_id=1, source_target_pairs={{0,1},{1,0},{2,3},{3,2},{4,5},{5,4},{6,7},{7,6},{8,9},{9,8},{10,11... | collective-permute-start | bytes 589832 | tf_op jit(solution)/shard_map/ppermute | solution.py:340
  40.1 7.4 %collective-permute-start.17 = (bf16[4,32,768]{2,1,0:T(8,128)(2,1)S(1)}, bf16[4,32,768]{2,1,0:T(8,128)(2,1)S(1)}, u32[]{:S(2)}, u32[]{:S(2)}) collective-permute-start(bf16[4,32,768]{2,1,0:T(8,128)(2,1)S(1)} %pad_maximum_fusion.11), channel_id=1, source_target_pairs={{0,3},{1,2},{2,1},{3,0},{4,7},{5,6},{6,5},{7,4},{8,11},{9,10},{10,... | collective-permute-start | bytes 589832 | tf_op jit(solution)/shard_map/ppermute | solution.py:340
  42.1 9.9 %collective-permute-start.16 = (bf16[4,32,768]{2,1,0:T(8,128)(2,1)S(1)}, bf16[4,32,768]{2,1,0:T(8,128)(2,1)S(1)}, u32[]{:S(2)}, u32[]{:S(2)}) collective-permute-start(bf16[4,32,768]{2,1,0:T(8,128)(2,1)S(1)} %pad_maximum_fusion.10), channel_id=1, source_target_pairs={{0,2},{1,3},{2,0},{3,1},{4,6},{5,7},{6,4},{7,5},{8,10},{9,11},{10,... | collective-permute-start | bytes 589832 | tf_op jit(solution)/shard_map/ppermute | solution.py:340
  43.5 8.6 %collective-permute-start.15 = (bf16[4,32,768]{2,1,0:T(8,128)(2,1)S(1)}, bf16[4,32,768]{2,1,0:T(8,128)(2,1)S(1)}, u32[]{:S(2)}, u32[]{:S(2)}) collective-permute-start(bf16[4,32,768]{2,1,0:T(8,128)(2,1)S(1)} %pad_maximum_fusion.9), channel_id=1, source_target_pairs={{0,1},{1,0},{2,3},{3,2},{4,5},{5,4},{6,7},{7,6},{8,9},{9,8},{10,11... | collective-permute-start | bytes 589832 | tf_op jit(solution)/shard_map/ppermute | solution.py:340
  44.3 10.1 %collective-permute-start.6 = (bf16[4,32,768]{2,1,0:T(8,128)(2,1)S(1)}, bf16[4,32,768]{2,1,0:T(8,128)(2,1)S(1)}, u32[]{:S(2)}, u32[]{:S(2)}) collective-permute-start(bf16[4,32,768]{2,1,0:T(8,128)(2,1)S(1)} %get-tuple-element.51), channel_id=1, source_target_pairs={{0,4},{1,5},{2,6},{3,7},{4,0},{5,1},{6,2},{7,3},{8,12},{9,13},{10,... | collective-permute-start | bytes 589832 | tf_op jit(solution)/shard_map/ppermute | solution.py:340
  46.4 13.2 %collective-permute-start.7 = (bf16[4,32,768]{2,1,0:T(8,128)(2,1)S(1)}, bf16[4,32,768]{2,1,0:T(8,128)(2,1)S(1)}, u32[]{:S(2)}, u32[]{:S(2)}) collective-permute-start(bf16[4,32,768]{2,1,0:T(8,128)(2,1)S(1)} %get-tuple-element.52), channel_id=1, source_target_pairs={{0,8},{1,9},{2,10},{3,11},{4,12},{5,13},{6,14},{7,15},{8,0},{9,1},... | collective-permute-start | bytes 589832 | tf_op jit(solution)/shard_map/ppermute | solution.py:340
  47.5 17.4 %collective-permute-start.8 = (bf16[4,32,768]{2,1,0:T(8,128)(2,1)S(1)}, bf16[4,32,768]{2,1,0:T(8,128)(2,1)S(1)}, u32[]{:S(2)}, u32[]{:S(2)}) collective-permute-start(bf16[4,32,768]{2,1,0:T(8,128)(2,1)S(1)} %get-tuple-element.53), channel_id=1, source_target_pairs={{0,12},{1,13},{2,14},{3,15},{4,8},{5,9},{6,10},{7,11},{8,4},{9,5},... | collective-permute-start | bytes 589832 | tf_op jit(solution)/shard_map/ppermute | solution.py:340
  52.8 15.1 %collective-permute-start.18 = (bf16[4,32,768]{2,1,0:T(8,128)(2,1)S(1)}, bf16[4,32,768]{2,1,0:T(8,128)(2,1)S(1)}, u32[]{:S(2)}, u32[]{:S(2)}) collective-permute-start(bf16[4,32,768]{2,1,0:T(8,128)(2,1)S(1)} %get-tuple-element.65), channel_id=1, source_target_pairs={{0,1},{1,0},{2,3},{3,2},{4,5},{5,4},{6,7},{7,6},{8,9},{9,8},{10,11... | collective-permute-start | bytes 589832 | tf_op jit(solution)/shard_map/ppermute | solution.py:340
  52.8 15.1 %collective-permute-start.19 = (bf16[4,32,768]{2,1,0:T(8,128)(2,1)S(1)}, bf16[4,32,768]{2,1,0:T(8,128)(2,1)S(1)}, u32[]{:S(2)}, u32[]{:S(2)}) collective-permute-start(bf16[4,32,768]{2,1,0:T(8,128)(2,1)S(1)} %get-tuple-element.66), channel_id=1, source_target_pairs={{0,2},{1,3},{2,0},{3,1},{4,6},{5,7},{6,4},{7,5},{8,10},{9,11},{10,... | collective-permute-start | bytes 589832 | tf_op jit(solution)/shard_map/ppermute | solution.py:340
  54.4 13.5 %collective-permute-start.20 = (bf16[4,32,768]{2,1,0:T(8,128)(2,1)S(1)}, bf16[4,32,768]{2,1,0:T(8,128)(2,1)S(1)}, u32[]{:S(2)}, u32[]{:S(2)}) collective-permute-start(bf16[4,32,768]{2,1,0:T(8,128)(2,1)S(1)} %get-tuple-element.67), channel_id=1, source_target_pairs={{0,3},{1,2},{2,1},{3,0},{4,7},{5,6},{6,5},{7,4},{8,11},{9,10},{10,... | collective-permute-start | bytes 589832 | tf_op jit(solution)/shard_map/ppermute | solution.py:340
  65.0 7.0 %collective-permute-start.11 = (bf16[4,32,768]{2,1,0:T(8,128)(2,1)S(1)}, bf16[4,32,768]{2,1,0:T(8,128)(2,1)S(1)}, u32[]{:S(2)}, u32[]{:S(2)}) collective-permute-start(bf16[4,32,768]{2,1,0:T(8,128)(2,1)S(1)} %pad_maximum_fusion.7), channel_id=1, source_target_pairs={{0,3},{1,2},{2,1},{3,0},{4,7},{5,6},{6,5},{7,4},{8,11},{9,10},{10,... | collective-permute-start | bytes 589832 | tf_op jit(solution)/shard_map/ppermute | solution.py:340
  66.6 10.1 %collective-permute-start.10 = (bf16[4,32,768]{2,1,0:T(8,128)(2,1)S(1)}, bf16[4,32,768]{2,1,0:T(8,128)(2,1)S(1)}, u32[]{:S(2)}, u32[]{:S(2)}) collective-permute-start(bf16[4,32,768]{2,1,0:T(8,128)(2,1)S(1)} %pad_maximum_fusion.6), channel_id=1, source_target_pairs={{0,2},{1,3},{2,0},{3,1},{4,6},{5,7},{6,4},{7,5},{8,10},{9,11},{10,... | collective-permute-start | bytes 589832 | tf_op jit(solution)/shard_map/ppermute | solution.py:340
  67.8 8.9 %collective-permute-start.9 = (bf16[4,32,768]{2,1,0:T(8,128)(2,1)S(1)}, bf16[4,32,768]{2,1,0:T(8,128)(2,1)S(1)}, u32[]{:S(2)}, u32[]{:S(2)}) collective-permute-start(bf16[4,32,768]{2,1,0:T(8,128)(2,1)S(1)} %pad_maximum_fusion.5), channel_id=1, source_target_pairs={{0,1},{1,0},{2,3},{3,2},{4,5},{5,4},{6,7},{7,6},{8,9},{9,8},{10,11... | collective-permute-start | bytes 589832 | tf_op jit(solution)/shard_map/ppermute | solution.py:340
  68.0 26.7 %collective-permute-start.23 = (bf16[4,32,768]{2,1,0:T(8,128)(2,1)S(1)}, bf16[4,32,768]{2,1,0:T(8,128)(2,1)S(1)}, u32[]{:S(2)}, u32[]{:S(2)}) collective-permute-start(bf16[4,32,768]{2,1,0:T(8,128)(2,1)S(1)} %pad_maximum_fusion.15), channel_id=1, source_target_pairs={{0,12},{1,13},{2,14},{3,15},{4,8},{5,9},{6,10},{7,11},{8,4},{9,5},... | collective-permute-start | bytes 589832 | tf_op jit(solution)/shard_map/ppermute | solution.py:340
  69.4 25.3 %collective-permute-start.22 = (bf16[4,32,768]{2,1,0:T(8,128)(2,1)S(1)}, bf16[4,32,768]{2,1,0:T(8,128)(2,1)S(1)}, u32[]{:S(2)}, u32[]{:S(2)}) collective-permute-start(bf16[4,32,768]{2,1,0:T(8,128)(2,1)S(1)} %pad_maximum_fusion.14), channel_id=1, source_target_pairs={{0,8},{1,9},{2,10},{3,11},{4,12},{5,13},{6,14},{7,15},{8,0},{9,1},... | collective-permute-start | bytes 589832 | tf_op jit(solution)/shard_map/ppermute | solution.py:340
  71.9 22.8 %collective-permute-start.21 = (bf16[4,32,768]{2,1,0:T(8,128)(2,1)S(1)}, bf16[4,32,768]{2,1,0:T(8,128)(2,1)S(1)}, u32[]{:S(2)}, u32[]{:S(2)}) collective-permute-start(bf16[4,32,768]{2,1,0:T(8,128)(2,1)S(1)} %pad_maximum_fusion.13), channel_id=1, source_target_pairs={{0,4},{1,5},{2,6},{3,7},{4,0},{5,1},{6,2},{7,3},{8,12},{9,13},{10,... | collective-permute-start | bytes 589832 | tf_op jit(solution)/shard_map/ppermute | solution.py:340
  76.8 17.9 %copy-start.1 = (bf16[32,16,768]{2,1,0:T(8,128)(2,1)S(1)}, bf16[32,16,768]{2,1,0:T(8,128)(2,1)}, u32[]{:S(2)}) copy-start(bf16[32,16,768]{2,1,0:T(8,128)(2,1)} %param.6) | copy-start | bytes 2359300
  76.8 17.9 %copy-start.2 = (bf16[32,16,768]{2,1,0:T(8,128)(2,1)S(1)}, bf16[32,16,768]{2,1,0:T(8,128)(2,1)}, u32[]{:S(2)}) copy-start(bf16[32,16,768]{2,1,0:T(8,128)(2,1)} %param.7) | copy-start | bytes 2359300

commit v3 on v2

--- a/solution.py
+++ b/solution.py
@@ -63,31 +63,39 @@
 
 def gated_kernel(n, mode, rows, g_ref, d_ref, *refs):
     count = count_of(n, mode)
-    out_refs, matrix = refs[:count], refs[count]
-    @pl.when(pl.program_id(0) == 0)
-    def _():
-        matrix[...] = split_matrix(lax.axis_index("seq"), rows, n, major(n, mode))
-
-    gated = (g_ref[...].astype(WIDE) * d_ref[...].astype(WIDE)).astype(NARROW)
+    out_refs, (g_buf, d_buf, sem) = refs[:count], refs[count:]
+    total = rows * n
+    half = total // 2
+    pieces = [slice(0, half), slice(half, total)]
+    copies = [
+        (pltpu.make_async_copy(g_ref.at[p, :], g_buf.at[p, :], sem.at[0, i]),
+         pltpu.make_async_copy(d_ref.at[p, :], d_buf.at[p, :], sem.at[1, i]))
+        for i, p in enumerate(pieces)
+    ]
+    for pair in copies:
+        for copy in pair:
+            copy.start()
+    matrix = split_matrix(lax.axis_index("seq"), rows, n, major(n, mode))
+    for p, pair in zip(pieces, copies):
+        for copy in pair:
+            copy.wait()
+        g_buf[p, :] = (g_buf[p, :].astype(WIDE) * d_buf[p, :].astype(WIDE)).astype(NARROW)
     span = n // count * rows
     for o in range(count):
-        out_refs[o][...] = dot(matrix[o * span : (o + 1) * span, :], gated, ((1,), (0,))).astype(NARROW)
+        out_refs[o][...] = dot(matrix[o * span : (o + 1) * span, :], g_buf[...], ((1,), (0,))).astype(NARROW)
 
 
 def gated_slabs(gate_in, cotangent, mode):
     rows, n, channels = gate_in.shape
     total = rows * n
-    chunks = 3 if channels % 384 == 0 else 1
-    wide = channels // chunks
     count = count_of(n, mode)
     span = n // count * rows
     out = pl.pallas_call(
         functools.partial(gated_kernel, n, mode, rows),
-        grid=(chunks,),
-        in_specs=[pl.BlockSpec((total, wide), lambda i: (0, i))] * 2,
-        out_specs=[pl.BlockSpec((span, wide), lambda i: (0, i))] * count,
+        in_specs=[pl.BlockSpec(memory_space=ANY)] * 2,
+        out_specs=[pl.BlockSpec(memory_space=VMEM)] * count,
         out_shape=[jax.ShapeDtypeStruct((span, channels), NARROW)] * count,
-        scratch_shapes=[VMEM((total, total), NARROW)],
+        scratch_shapes=[VMEM((total, channels), NARROW)] * 2 + [pltpu.SemaphoreType.DMA((2, 2))],
         compiler_params=params(58),
         cost_estimate=cost(2 * total * total * channels, 6 * total * channels),
         name="gated_slabs",
@@ -95,10 +103,10 @@
     return [o.reshape(n // count, rows, channels) for o in out]
 
 
-def inner_kernel(mode, group, w_ref, x_ref, *refs):
+def inner_kernel(mode, merges, group, w_ref, x_ref, *refs):
     n, length = w_ref.shape[1:]
     count = count_of(n, mode)
-    out_refs, (kept_a, kept_b, kept, sem) = refs[:count], refs[count:]
+    out_refs, (kept_a, kept_b, *merge_refs, kept, sem) = refs[:count], refs[count:]
     rows = group * length
     blocks = w_ref.shape[0]
     steps = blocks // group // 2
@@ -112,7 +120,10 @@
     for kept_x, base in parts:
         for i in range(steps):
             fetch(i, kept_x, base).start()
-    matrix = split_matrix(lax.axis_index("seq"), blocks, n, major(n, mode))
+    rank = lax.axis_index("seq")
+    matrix = split_matrix(rank, blocks, n, major(n, mode))
+    for merge_mode, merge_ref in zip(merges, merge_refs):
+        merge_ref[...] = merge_matrix(rank, blocks, n, major(n, merge_mode))
     for kept_x, base in parts:
 
         def step(i, carry, kept_x=kept_x, base=base):
@@ -130,24 +141,26 @@
         out_refs[o][...] = dot(matrix[o * span : (o + 1) * span, :], kept[...], ((1,), (0,))).astype(NARROW)
 
 
-def inner_slabs(first_factor, values, mode):
+def inner_slabs(first_factor, values, mode, merges):
     blocks, n, length = first_factor.shape
     channels = values.shape[1]
     group = 2 if blocks % 4 == 0 else 1
     count = count_of(n, mode)
     span = n // count * blocks
     half = VMEM((blocks // 2 * length, channels), NARROW)
-    *out, kept_a, kept_b = pl.pallas_call(
-        functools.partial(inner_kernel, mode, group),
+    total = blocks * n
+    *out, kept_a, kept_b, near, far = pl.pallas_call(
+        functools.partial(inner_kernel, mode, merges, group),
         in_specs=[pl.BlockSpec(memory_space=VMEM), pl.BlockSpec(memory_space=ANY)],
-        out_specs=[pl.BlockSpec(memory_space=VMEM)] * (count + 2),
-        out_shape=[jax.ShapeDtypeStruct((span, channels), NARROW)] * count + [half] * 2,
+        out_specs=[pl.BlockSpec(memory_space=VMEM)] * (count + 4),
+        out_shape=[jax.ShapeDtypeStruct((span, channels), NARROW)] * count + [half] * 2
+        + [jax.ShapeDtypeStruct((total, total), NARROW)] * 2,
         scratch_shapes=[VMEM((blocks * n, channels), NARROW), pltpu.SemaphoreType.DMA((blocks // group,))],
-        compiler_params=params(32),
+        compiler_params=params(20),
         cost_estimate=cost(2 * blocks * n * length * channels, 2 * blocks * length * channels),
         name="inner_slabs",
     )(first_factor, values)
-    return [o.reshape(n // count, blocks, channels) for o in out], [kept_a, kept_b]
+    return [o.reshape(n // count, blocks, channels) for o in out], [kept_a, kept_b], near, far
 
 
 def mix_kernel(n, arrive, leave, transpose, s_ref, *refs):
@@ -196,7 +209,7 @@
     return [out[p * leave_n : (p + 1) * leave_n] for p in range(leave[1])], out[-1]
 
 
-def grads_kernel(mode, slots, group, half, held, w_ref, *refs):
+def grads_kernel(mode, slots, group, half, held, w_ref, matrix_ref, *refs):
     n, length = w_ref.shape[1:]
     x_refs, refs = refs[:held], refs[held:]
     count = count_of(n, mode)
@@ -216,7 +229,10 @@
     for o in range(count):
         for b in range(every):
             slabs[(o * every + b) * part : (o * every + b + 1) * part, :] = slab_refs[o][b]
-    matrix = merge_matrix(lax.axis_index("seq"), part, n, major(n, mode))
+    if matrix_ref.shape[0] == slabs.shape[0]:
+        matrix = matrix_ref[...]
+    else:
+        matrix = merge_matrix(lax.axis_index("seq"), part, n, major(n, mode))
     back[...] = dot(matrix, slabs[...], ((1,), (0,))).astype(NARROW)
 
     each = steps // held
@@ -247,7 +263,7 @@
     last.wait()
 
 
-def grads(first_factor, kept_x, slabs, mode, half, earlier):
+def grads(first_factor, matrix, kept_x, slabs, mode, half, earlier):
     blocks, n, length = first_factor.shape
     channels = kept_x[0].shape[1]
     held, count = len(kept_x), len(slabs)
@@ -260,11 +276,11 @@
     ]
     return pl.pallas_call(
         functools.partial(grads_kernel, mode, slots, group, half, held),
-        in_specs=[pl.BlockSpec(memory_space=VMEM)] * (1 + held + count)
+        in_specs=[pl.BlockSpec(memory_space=VMEM)] * (2 + held + count)
         + ([] if half == 0 else [pl.BlockSpec(memory_space=ANY)] * 2),
         out_specs=[pl.BlockSpec(memory_space=ANY)] * 2,
         out_shape=shapes,
-        input_output_aliases={} if half == 0 else {1 + held + count: 0, 2 + held + count: 1},
+        input_output_aliases={} if half == 0 else {2 + held + count: 0, 3 + held + count: 1},
         scratch_shapes=[
             VMEM((part * n, channels), NARROW),
             VMEM((part * n, channels), NARROW),
@@ -276,43 +292,47 @@
         compiler_params=params(16),
         cost_estimate=cost(4 * part * n * length * channels, 2 * part * length * channels),
         name="grads",
-    )(first_factor, *kept_x, *slabs, *(earlier or ()))
-
-
-def gates_kernel(n, mode, rows, g_ref, d_ref, *refs):
-    count = count_of(n, mode)
-    slab_refs, (mixed_ref, grad_ref, matrix, slabs) = refs[:count], refs[count:]
-    @pl.when(pl.program_id(0) == 0)
-    def _():
-        matrix[...] = merge_matrix(lax.axis_index("seq"), rows, n, major(n, mode))
-
-    span = n // count * rows
+    )(first_factor, matrix, *kept_x, *slabs, *(earlier or ()))
+
+
+def gates_kernel(n, mode, pieces, matrix_ref, g_ref, d_ref, *refs):
+    count = count_of(n, mode)
+    slab_refs, (mixed_ref, grad_ref, slabs, mixed, grad, sem) = refs[:count], refs[count:]
+    span = slab_refs[0].shape[0]
     for o in range(count):
         slabs[o * span : (o + 1) * span, :] = slab_refs[o][...]
-    z = dot(matrix[...], slabs[...], ((1,), (0,)))
-    mixed_ref[...] = (g_ref[...].astype(WIDE) * z).astype(NARROW)
-    grad_ref[...] = (d_ref[...].astype(WIDE) * z).astype(NARROW)
-
-
-def gates(gate_in, cotangent, slabs, mode):
+    size = slabs.shape[0] // pieces
+    copies = []
+    for p in range(pieces):
+        here = slice(p * size, (p + 1) * size)
+        z = dot(matrix_ref[here, :], slabs[...], ((1,), (0,)))
+        mixed[here, :] = (g_ref[here, :].astype(WIDE) * z).astype(NARROW)
+        grad[here, :] = (d_ref[here, :].astype(WIDE) * z).astype(NARROW)
+        copies.append(pltpu.make_async_copy(mixed.at[here, :], mixed_ref.at[here, :], sem.at[0, p]))
+        copies.append(pltpu.make_async_copy(grad.at[here, :], grad_ref.at[here, :], sem.at[1, p]))
+        copies[-2].start()
+        copies[-1].start()
+    for copy in copies:
+        copy.wait()
+
+
+def gates(matrix, gate_in, cotangent, slabs, mode):
     rows, n, channels = gate_in.shape
     total = rows * n
-    chunks = 3 if channels % 384 == 0 else 1
-    wide = channels // chunks
     count = count_of(n, mode)
     span = n // count * rows
+    pieces = 2
     out = pl.pallas_call(
-        functools.partial(gates_kernel, n, mode, rows),
-        grid=(chunks,),
-        in_specs=[pl.BlockSpec((total, wide), lambda i: (0, i))] * 2
-        + [pl.BlockSpec((span, wide), lambda i: (0, i))] * count,
-        out_specs=[pl.BlockSpec((total, wide), lambda i: (0, i))] * 2,
+        functools.partial(gates_kernel, n, mode, pieces),
+        in_specs=[pl.BlockSpec(memory_space=VMEM)] * (3 + count),
+        out_specs=[pl.BlockSpec(memory_space=ANY)] * 2,
         out_shape=[jax.ShapeDtypeStruct((total, channels), NARROW)] * 2,
-        scratch_shapes=[VMEM((total, total), NARROW), VMEM((total, wide), NARROW)],
+        scratch_shapes=[VMEM((total, channels), NARROW)] * 3 + [pltpu.SemaphoreType.DMA((2, pieces))],
         compiler_params=params(10),
         cost_estimate=cost(2 * total * total * channels, 10 * total * channels),
         name="gates",
     )(
+        matrix,
         gate_in.reshape(total, channels),
         cotangent.reshape(total, channels),
         *[s.reshape(span, channels) for s in slabs],
@@ -349,7 +369,7 @@
     gated = gated_slabs(gate_in, cotangent, far)
     e = across(gated)
     (factor,) = after([first_factor], gated[0])
-    u, kept_x = inner_slabs(factor, values, far)
+    u, kept_x, merge_near, merge_far = inner_slabs(factor, values, far, (near, far))
     e = beside(regroup(after(e, u[0])))
     u = across(u)
     (f,), e_all = mix(second_factor, [e], n, (near, 1), (far, 1), True, "back")
@@ -358,15 +378,10 @@
     (z,), u_all = mix(second_factor, [u], n, (near, 1), (near, 1), False, "forth")
     z = across(regroup(beside(z)))
     f = beside(regroup(f))
-    out = None
-    part = gate_in.shape[0] // 2
-    for half in range(2):
-        slabs = [x[:, half * part : (half + 1) * part] for x in f]
-        out = grads(first_factor, [kept_x[half]], slabs, near, half, out)
-    values_grad, first_grad = out
-    second_grad = dot(*after([e_all, u_all], first_grad), ((1,), (1,))).astype(NARROW)[None]
+    values_grad, first_grad = grads(first_factor, merge_near, kept_x, f, near, 0, None)
+    second_grad = dot(e_all, u_all, ((1,), (1,))).astype(NARROW)[None]
     gate_in, cotangent = after([gate_in, cotangent], first_grad)
-    mixed, gate_grad = gates(gate_in, cotangent, z, far)
+    mixed, gate_grad = gates(merge_far, gate_in, cotangent, z, far)
     return mixed, values_grad, gate_grad, first_grad, second_grad
 
 

time: 98.2 us -> 96.5 us (0.983)
  Pallas kernels: 35 us -> 30.1 us
  waiting for transfers between devices: 25.8 us -> 27.9 us
  starting transfers between devices: 32.3 us -> 34.1 us
    pallas_call x3, Pallas kernels: 17.2 us -> 13.7 us  [the longest x1 9.29 us: inner_slabs(): pl.pallas_call(functools.partial(inner_kernel, mode, merges, group), in_s...]
    ppermute x24, waiting for transfers between devices: 25.8 us -> 27.9 us  [permutes(): lax.ppermute(slabs[k], 'seq', [(i, i ^ k * step) for i in range(n)])]
    ppermute x24, starting transfers between devices: 32.3 us -> 34.1 us  [permutes(): lax.ppermute(slabs[k], 'seq', [(i, i ^ k * step) for i in range(n)])]
    pallas_call x2 -> x1, Pallas kernels: 16.5 us -> 15 us  [grads(): pl.pallas_call(functools.partial(grads_kernel, mode, slots, group, half,...]
    unnamed x10, local copies, waits for them, and re-layouts: 0.03 us -> 1.06 us
  transfers between devices with their start and end apart: 24 -> 24, of which waited for: 8 -> 9; matrix products, arithmetic and copies ran while one was open for 3% -> 2% of each run, Pallas kernels for 30% -> 27%
where the time goes in v3:
time: 96.5 us; the launch traced here: 96.3 us
  starting transfers between devices  34.1 us (35%)
  Pallas kernels  30.1 us (31%)
  waiting for transfers between devices  27.9 us (29%)
  matrix products  1.39 us (1%)
  local copies, waits for them, and re-layouts  1.29 us (1%)
  between operations  1 us (1%)
    ppermute x24, starting transfers between devices, permutes(): lax.ppermute(slabs[k], 'seq', [(i, i ^ k * step) for i in range(n)])  34.1 us
    ppermute x24, waiting for transfers between devices, permutes(): lax.ppermute(slabs[k], 'seq', [(i, i ^ k * step) for i in range(n)])  27.9 us
    pallas_call x1, Pallas kernels, grads(): pl.pallas_call(functools.partial(grads_kernel, mode, slots, group, half,...  15 us
    pallas_call x1, Pallas kernels, inner_slabs(): pl.pallas_call(functools.partial(inner_kernel, mode, merges, group), in_s...  9.29 us
    pallas_call x1, Pallas kernels, gated_slabs(): pl.pallas_call(functools.partial(gated_kernel, n, mode, rows), in_specs=[...  2.76 us
  transfers between devices with their start and end apart: 24, of which 9 were waited for; matrix products, arithmetic and copies ran while one was open for 2% of the time, Pallas kernels for 27%

profile of v3, /device:TPU:11, one launch (start us, length us, event | category | flops | bytes accessed | tf_op | source)
XLA Modules:
  0.0 96.3 jit_solution(4041590089667945058)
XLA Ops:
  0.6 2.8 %gated_slabs.1 = (bf16[128,768]{1,0:T(8,128)(2,1)}, bf16[128,768]{1,0:T(8,128)(2,1)}, bf16[128,768]{1,0:T(8,128)(2,1)}, bf16[128,768]{1,0:T(8,128)(2,1)}) custom-call(bf16[512,768]{1,0:T(8,128)(2,1)} %bitcast.29, bf16[512,768]{1,0:T(8,128)(2,1)} %bitcast.31), custom_call_target="tpu_custom_call" | custom-call | flops 402653184 | bytes 2359296 | tf_op jit(solution)/shard_map/gated_slabs/pallas_call | solution.py:93
  3.6 2.3 %collective-permute-start.1 = (bf16[4,32,768]{2,1,0:T(8,128)(2,1)}, bf16[4,32,768]{2,1,0:T(8,128)(2,1)S(1)}, u32[]{:S(2)}, u32[]{:S(2)}) collective-permute-start(bf16[4,32,768]{2,1,0:T(8,128)(2,1)} %bitcast.44), channel_id=1, source_target_pairs={{0,8},{1,9},{2,10},{3,11},{4,12},{5,13},{6,14},{7,15},{8,0},{9,1},... | collective-permute-start | bytes 589832 | tf_op jit(solution)/shard_map/ppermute | solution.py:360
  6.1 1.0 %copy-done.2 = bf16[32,16,512]{2,1,0:T(8,128)(2,1)S(1)} copy-done((bf16[32,16,512]{2,1,0:T(8,128)(2,1)S(1)}, bf16[32,16,512]{2,1,0:T(8,128)(2,1)}, u32[]{:S(2)}) %copy-start.2) | copy-done | bytes 524312
  7.2 9.3 %inner_slabs.1 = (bf16[128,768]{1,0:T(8,128)(2,1)S(1)}, bf16[128,768]{1,0:T(8,128)(2,1)S(1)}, bf16[128,768]{1,0:T(8,128)(2,1)S(1)}, bf16[128,768]{1,0:T(8,128)(2...) custom-call(bf16[32,16,512]{2,1,0:T(8,128)(2,1)S(1)} %copy-done.2, ...), custom_call_target="tpu_custom_call" | custom-call | flops 402653184 | bytes 25165824 | tf_op jit(solution)/shard_map/inner_slabs/pallas_call | solution.py:152
  16.5 1.2 %collective-permute-start.12 = (bf16[4,32,768]{2,1,0:T(8,128)(2,1)S(1)}, bf16[4,32,768]{2,1,0:T(8,128)(2,1)S(1)}, u32[]{:S(2)}, u32[]{:S(2)}) collective-permute-start(bf16[4,32,768]{2,1,0:T(8,128)(2,1)S(1)} %bitcast.39), channel_id=1, source_target_pairs={{0,4},{1,5},{2,6},{3,7},{4,0},{5,1},{6,2},{7,3},{8,12},{9,13},{10,... | collective-permute-start | bytes 589832 | tf_op jit(solution)/shard_map/ppermute | solution.py:360
  17.7 2.2 %collective-permute-start.13 = (bf16[4,32,768]{2,1,0:T(8,128)(2,1)S(1)}, bf16[4,32,768]{2,1,0:T(8,128)(2,1)S(1)}, u32[]{:S(2)}, u32[]{:S(2)}) collective-permute-start(bf16[4,32,768]{2,1,0:T(8,128)(2,1)S(1)} %bitcast.38), channel_id=1, source_target_pairs={{0,8},{1,9},{2,10},{3,11},{4,12},{5,13},{6,14},{7,15},{8,0},{9,1},... | collective-permute-start | bytes 589832 | tf_op jit(solution)/shard_map/ppermute | solution.py:360
  20.1 2.9 %collective-permute-done.2 = bf16[4,32,768]{2,1,0:T(8,128)(2,1)S(1)} collective-permute-done((bf16[4,32,768]{2,1,0:T(8,128)(2,1)}, bf16[4,32,768]{2,1,0:T(8,128)(2,1)S(1)}, u32[]{:S(2)}, u32[]{:S(2)}) %collective-permute-start.2) | collective-permute-done | bytes 196640 | tf_op jit(solution)/shard_map/ppermute | solution.py:360
  23.2 11.7 %collective-permute-start.3 = (bf16[4,32,768]{2,1,0:T(8,128)(2,1)S(1)}, bf16[4,32,768]{2,1,0:T(8,128)(2,1)S(1)}, u32[]{:S(2)}, u32[]{:S(2)}) collective-permute-start(bf16[4,32,768]{2,1,0:T(8,128)(2,1)S(1)} %pad_maximum_fusion.1), channel_id=1, source_target_pairs={{0,1},{1,0},{2,3},{3,2},{4,5},{5,4},{6,7},{7,6},{8,9},{9,8},{10,11... | collective-permute-start | bytes 589832 | tf_op jit(solution)/shard_map/ppermute | solution.py:360
  34.9 0.3 collective-permute-start.4
  35.3 1.5 %collective-permute-start.5 = (bf16[4,32,768]{2,1,0:T(8,128)(2,1)S(1)}, bf16[4,32,768]{2,1,0:T(8,128)(2,1)S(1)}, u32[]{:S(2)}, u32[]{:S(2)}) collective-permute-start(bf16[4,32,768]{2,1,0:T(8,128)(2,1)S(1)} %pad_maximum_fusion.3), channel_id=1, source_target_pairs={{0,3},{1,2},{2,1},{3,0},{4,7},{5,6},{6,5},{7,4},{8,11},{9,10},{10,... | collective-permute-start | bytes 589832 | tf_op jit(solution)/shard_map/ppermute | solution.py:360
  36.8 3.1 %collective-permute-done.14 = bf16[4,32,768]{2,1,0:T(8,128)(2,1)S(1)} collective-permute-done((bf16[4,32,768]{2,1,0:T(8,128)(2,1)S(1)}, bf16[4,32,768]{2,1,0:T(8,128)(2,1)S(1)}, u32[]{:S(2)}, u32[]{:S(2)}) %collective-permute-start.14) | collective-permute-done | bytes 196640 | tf_op jit(solution)/shard_map/ppermute | solution.py:360
  40.0 1.9 %collective-permute-start.15 = (bf16[4,32,768]{2,1,0:T(8,128)(2,1)S(1)}, bf16[4,32,768]{2,1,0:T(8,128)(2,1)S(1)}, u32[]{:S(2)}, u32[]{:S(2)}) collective-permute-start(bf16[4,32,768]{2,1,0:T(8,128)(2,1)S(1)} %pad_maximum_fusion.9), channel_id=1, source_target_pairs={{0,1},{1,0},{2,3},{3,2},{4,5},{5,4},{6,7},{7,6},{8,9},{9,8},{10,11... | collective-permute-start | bytes 589832 | tf_op jit(solution)/shard_map/ppermute | solution.py:360
  41.9 0.3 collective-permute-start.16
  42.3 1.5 %collective-permute-start.17 = (bf16[4,32,768]{2,1,0:T(8,128)(2,1)S(1)}, bf16[4,32,768]{2,1,0:T(8,128)(2,1)S(1)}, u32[]{:S(2)}, u32[]{:S(2)}) collective-permute-start(bf16[4,32,768]{2,1,0:T(8,128)(2,1)S(1)} %pad_maximum_fusion.11), channel_id=1, source_target_pairs={{0,3},{1,2},{2,1},{3,0},{4,7},{5,6},{6,5},{7,4},{8,11},{9,10},{10,... | collective-permute-start | bytes 589832 | tf_op jit(solution)/shard_map/ppermute | solution.py:360
  43.8 2.5 %collective-permute-done.5.refs_3_ = bf16[4,32,768]{2,1,0:T(8,128)(2,1)S(1)} collective-permute-done((bf16[4,32,768]{2,1,0:T(8,128)(2,1)S(1)}, bf16[4,32,768]{2,1,0:T(8,128)(2,1)S(1)}, u32[]{:S(2)}, u32[]{:S(2)}) %collective-permute-start.5) | collective-permute-done | bytes 196640 | tf_op jit(solution)/shard_map/ppermute | solution.py:360
  46.2 0.7 back.1
  47.0 2.5 %collective-permute-start.7 = (bf16[4,32,768]{2,1,0:T(8,128)(2,1)S(1)}, bf16[4,32,768]{2,1,0:T(8,128)(2,1)S(1)}, u32[]{:S(2)}, u32[]{:S(2)}) collective-permute-start(bf16[4,32,768]{2,1,0:T(8,128)(2,1)S(1)} %get-tuple-element.53), channel_id=1, source_target_pairs={{0,8},{1,9},{2,10},{3,11},{4,12},{5,13},{6,14},{7,15},{8,0},{9,1},... | collective-permute-start | bytes 589832 | tf_op jit(solution)/shard_map/ppermute | solution.py:360
  49.9 4.3 %collective-permute-done.17.refs_3_ = bf16[4,32,768]{2,1,0:T(8,128)(2,1)S(1)} collective-permute-done((bf16[4,32,768]{2,1,0:T(8,128)(2,1)S(1)}, bf16[4,32,768]{2,1,0:T(8,128)(2,1)S(1)}, u32[]{:S(2)}, u32[]{:S(2)}) %collective-permute-start.17) | collective-permute-done | bytes 196640 | tf_op jit(solution)/shard_map/ppermute | solution.py:360
  54.3 0.7 forth.1
  55.0 0.3 collective-permute-start.18
  55.6 1.4 %fusion = bf16[1,512,512]{2,1,0:T(8,128)(2,1)} fusion(bf16[512,768]{1,0:T(8,128)(2,1)S(1)} %get-tuple-element.69, bf16[512,768]{1,0:T(8,128)(2,1)S(1)} %get-tuple-element.70), kind=kOutput, calls=%fused_computation.1 | convolution fusion | flops 402915328 | bytes 2097152 | tf_op jit(solution)/shard_map/dot_general | solution.py:61
  57.0 1.6 %collective-permute-start.20 = (bf16[4,32,768]{2,1,0:T(8,128)(2,1)S(1)}, bf16[4,32,768]{2,1,0:T(8,128)(2,1)S(1)}, u32[]{:S(2)}, u32[]{:S(2)}) collective-permute-start(bf16[4,32,768]{2,1,0:T(8,128)(2,1)S(1)} %get-tuple-element.65), channel_id=1, source_target_pairs={{0,3},{1,2},{2,1},{3,0},{4,7},{5,6},{6,5},{7,4},{8,11},{9,10},{10,... | collective-permute-start | bytes 589832 | tf_op jit(solution)/shard_map/ppermute | solution.py:360
  58.6 3.4 %collective-permute-done.7 = bf16[4,32,768]{2,1,0:T(8,128)(2,1)S(1)} collective-permute-done((bf16[4,32,768]{2,1,0:T(8,128)(2,1)S(1)}, bf16[4,32,768]{2,1,0:T(8,128)(2,1)S(1)}, u32[]{:S(2)}, u32[]{:S(2)}) %collective-permute-start.7) | collective-permute-done | bytes 196640 | tf_op jit(solution)/shard_map/ppermute | solution.py:360
  62.0 5.2 %collective-permute-done.8 = bf16[4,32,768]{2,1,0:T(8,128)(2,1)S(1)} collective-permute-done((bf16[4,32,768]{2,1,0:T(8,128)(2,1)S(1)}, bf16[4,32,768]{2,1,0:T(8,128)(2,1)S(1)}, u32[]{:S(2)}, u32[]{:S(2)}) %collective-permute-start.8) | collective-permute-done | bytes 196640 | tf_op jit(solution)/shard_map/ppermute | solution.py:360
  67.3 1.0 %collective-permute-start.9 = (bf16[4,32,768]{2,1,0:T(8,128)(2,1)S(1)}, bf16[4,32,768]{2,1,0:T(8,128)(2,1)S(1)}, u32[]{:S(2)}, u32[]{:S(2)}) collective-permute-start(bf16[4,32,768]{2,1,0:T(8,128)(2,1)S(1)} %pad_maximum_fusion.5), channel_id=1, source_target_pairs={{0,1},{1,0},{2,3},{3,2},{4,5},{5,4},{6,7},{7,6},{8,9},{9,8},{10,11... | collective-permute-start | bytes 589832 | tf_op jit(solution)/shard_map/ppermute | solution.py:360
  68.3 0.3 collective-permute-start.10
  68.7 1.5 %collective-permute-start.11 = (bf16[4,32,768]{2,1,0:T(8,128)(2,1)S(1)}, bf16[4,32,768]{2,1,0:T(8,128)(2,1)S(1)}, u32[]{:S(2)}, u32[]{:S(2)}) collective-permute-start(bf16[4,32,768]{2,1,0:T(8,128)(2,1)S(1)} %pad_maximum_fusion.7), channel_id=1, source_target_pairs={{0,3},{1,2},{2,1},{3,0},{4,7},{5,6},{6,5},{7,4},{8,11},{9,10},{10,... | collective-permute-start | bytes 589832 | tf_op jit(solution)/shard_map/ppermute | solution.py:360
  70.4 2.5 %collective-permute-start.22 = (bf16[4,32,768]{2,1,0:T(8,128)(2,1)S(1)}, bf16[4,32,768]{2,1,0:T(8,128)(2,1)S(1)}, u32[]{:S(2)}, u32[]{:S(2)}) collective-permute-start(bf16[4,32,768]{2,1,0:T(8,128)(2,1)S(1)} %pad_maximum_fusion.14), channel_id=1, source_target_pairs={{0,8},{1,9},{2,10},{3,11},{4,12},{5,13},{6,14},{7,15},{8,0},{9,1},... | collective-permute-start | bytes 589832 | tf_op jit(solution)/shard_map/ppermute | solution.py:360
  73.3 1.7 %collective-permute-done.10.refs_4_ = bf16[4,32,768]{2,1,0:T(8,128)(2,1)S(1)} collective-permute-done((bf16[4,32,768]{2,1,0:T(8,128)(2,1)S(1)}, bf16[4,32,768]{2,1,0:T(8,128)(2,1)S(1)}, u32[]{:S(2)}, u32[]{:S(2)}) %collective-permute-start.10) | collective-permute-done | bytes 196640 | tf_op jit(solution)/shard_map/ppermute | solution.py:360
  74.9 4.6 %collective-permute-done.11.refs_5_ = bf16[4,32,768]{2,1,0:T(8,128)(2,1)S(1)} collective-permute-done((bf16[4,32,768]{2,1,0:T(8,128)(2,1)S(1)}, bf16[4,32,768]{2,1,0:T(8,128)(2,1)S(1)}, u32[]{:S(2)}, u32[]{:S(2)}) %collective-permute-start.11) | collective-permute-done | bytes 196640 | tf_op jit(solution)/shard_map/ppermute | solution.py:360
  79.5 15.0 %grads.1 = (bf16[16384,768]{1,0:T(8,128)(2,1)}, bf16[32,16,512]{2,1,0:T(8,128)(2,1)}) custom-call(bf16[32,16,512]{2,1,0:T(8,128)(2,1)S(1)} %copy-done.2, bf16[512,512]{1,0:T(8,128)(2,1)S(1)} %get-tuple-element.41.matrix_ref, bf16[8192,768]{1,0:T(8,128)(2,1)S(1)} %get-tuple-element.42.refs_0_, bf16[8192,768]{1,0:T(8,128)(2,1)S(1)} %get-tuple-element.43.refs_1_, ...), custom_call_target="tpu_custom_call" | custom-call | flops 805306368 | bytes 25165824 | tf_op jit(solution)/shard_map/grads/pallas_call | solution.py:277
  94.6 1.6 %gates.1 = (bf16[512,768]{1,0:T(8,128)(2,1)}, bf16[512,768]{1,0:T(8,128)(2,1)}) custom-call(bf16[512,512]{1,0:T(8,128)(2,1)S(1)} %get-tuple-element.40.matrix_ref, bf16[512,768]{1,0:T(8,128)(2,1)S(1)} %bitcast.30, bf16[512,768]{1,0:T(8,128)(2,1)S(1)} %bitcast.32, bf16[128,768]{1,0:T(8,128)(2,1)S(1)} %bitcast.33, bf16[128,768]{1,0:T(8,128)(2,1)S(1)} %bitcast.34, ...), custom_call_target="tpu_custom_call" | custom-call | flops 402653184 | bytes 3932160 | tf_op jit(solution)/shard_map/gates/pallas_call | solution.py:325
  (63 shorter events, 2.5 us)
Async XLA Ops:
  0.6 45.6 %copy-start.3 = (bf16[1,512,512]{2,1,0:T(8,128)(2,1)S(1)}, bf16[1,512,512]{2,1,0:T(8,128)(2,1)}, u32[]{:S(2)}) copy-start(bf16[1,512,512]{2,1,0:T(8,128)(2,1)} %s_ref.3) | copy-start | bytes 1572868
  3.4 16.5 %collective-permute-start = (bf16[4,32,768]{2,1,0:T(8,128)(2,1)}, bf16[4,32,768]{2,1,0:T(8,128)(2,1)S(1)}, u32[]{:S(2)}, u32[]{:S(2)}) collective-permute-start(bf16[4,32,768]{2,1,0:T(8,128)(2,1)} %bitcast.45), channel_id=1, source_target_pairs={{0,4},{1,5},{2,6},{3,7},{4,0},{5,1},{6,2},{7,3},{8,12},{9,13},{10,... | collective-permute-start | bytes 589832 | tf_op jit(solution)/shard_map/ppermute | solution.py:360
  3.6 16.5 %collective-permute-start.1 = (bf16[4,32,768]{2,1,0:T(8,128)(2,1)}, bf16[4,32,768]{2,1,0:T(8,128)(2,1)S(1)}, u32[]{:S(2)}, u32[]{:S(2)}) collective-permute-start(bf16[4,32,768]{2,1,0:T(8,128)(2,1)} %bitcast.44), channel_id=1, source_target_pairs={{0,8},{1,9},{2,10},{3,11},{4,12},{5,13},{6,14},{7,15},{8,0},{9,1},... | collective-permute-start | bytes 589832 | tf_op jit(solution)/shard_map/ppermute | solution.py:360
  5.9 17.1 %collective-permute-start.2 = (bf16[4,32,768]{2,1,0:T(8,128)(2,1)}, bf16[4,32,768]{2,1,0:T(8,128)(2,1)S(1)}, u32[]{:S(2)}, u32[]{:S(2)}) collective-permute-start(bf16[4,32,768]{2,1,0:T(8,128)(2,1)} %bitcast.43), channel_id=1, source_target_pairs={{0,12},{1,13},{2,14},{3,15},{4,8},{5,9},{6,10},{7,11},{8,4},{9,5},... | collective-permute-start | bytes 589832 | tf_op jit(solution)/shard_map/ppermute | solution.py:360
  6.1 1.0 %copy-start.2 = (bf16[32,16,512]{2,1,0:T(8,128)(2,1)S(1)}, bf16[32,16,512]{2,1,0:T(8,128)(2,1)}, u32[]{:S(2)}) copy-start(bf16[32,16,512]{2,1,0:T(8,128)(2,1)} %w_ref.2) | copy-start | bytes 1572868
  7.2 15.9 %copy-start.4 = (bf16[128,768]{1,0:T(8,128)(2,1)S(1)}, bf16[128,768]{1,0:T(8,128)(2,1)}, u32[]{:S(2)}) copy-start(bf16[128,768]{1,0:T(8,128)(2,1)} %get-tuple-element.38) | copy-start | bytes 589828
  16.5 78.1 %copy-start = (bf16[32,16,768]{2,1,0:T(8,128)(2,1)S(1)}, bf16[32,16,768]{2,1,0:T(8,128)(2,1)}, u32[]{:S(2)}) copy-start(bf16[32,16,768]{2,1,0:T(8,128)(2,1)} %param.6) | copy-start | bytes 2359300
  16.5 78.1 %copy-start.1 = (bf16[32,16,768]{2,1,0:T(8,128)(2,1)S(1)}, bf16[32,16,768]{2,1,0:T(8,128)(2,1)}, u32[]{:S(2)}) copy-start(bf16[32,16,768]{2,1,0:T(8,128)(2,1)} %param.7) | copy-start | bytes 2359300
  16.5 18.8 %collective-permute-start.12 = (bf16[4,32,768]{2,1,0:T(8,128)(2,1)S(1)}, bf16[4,32,768]{2,1,0:T(8,128)(2,1)S(1)}, u32[]{:S(2)}, u32[]{:S(2)}) collective-permute-start(bf16[4,32,768]{2,1,0:T(8,128)(2,1)S(1)} %bitcast.39), channel_id=1, source_target_pairs={{0,4},{1,5},{2,6},{3,7},{4,0},{5,1},{6,2},{7,3},{8,12},{9,13},{10,... | collective-permute-start | bytes 589832 | tf_op jit(solution)/shard_map/ppermute | solution.py:360
  17.7 19.1 %collective-permute-start.13 = (bf16[4,32,768]{2,1,0:T(8,128)(2,1)S(1)}, bf16[4,32,768]{2,1,0:T(8,128)(2,1)S(1)}, u32[]{:S(2)}, u32[]{:S(2)}) collective-permute-start(bf16[4,32,768]{2,1,0:T(8,128)(2,1)S(1)} %bitcast.38), channel_id=1, source_target_pairs={{0,8},{1,9},{2,10},{3,11},{4,12},{5,13},{6,14},{7,15},{8,0},{9,1},... | collective-permute-start | bytes 589832 | tf_op jit(solution)/shard_map/ppermute | solution.py:360
  19.9 20.0 %collective-permute-start.14 = (bf16[4,32,768]{2,1,0:T(8,128)(2,1)S(1)}, bf16[4,32,768]{2,1,0:T(8,128)(2,1)S(1)}, u32[]{:S(2)}, u32[]{:S(2)}) collective-permute-start(bf16[4,32,768]{2,1,0:T(8,128)(2,1)S(1)} %bitcast.37), channel_id=1, source_target_pairs={{0,12},{1,13},{2,14},{3,15},{4,8},{5,9},{6,10},{7,11},{8,4},{9,5},... | collective-permute-start | bytes 589832 | tf_op jit(solution)/shard_map/ppermute | solution.py:360
  23.2 19.1 %collective-permute-start.3 = (bf16[4,32,768]{2,1,0:T(8,128)(2,1)S(1)}, bf16[4,32,768]{2,1,0:T(8,128)(2,1)S(1)}, u32[]{:S(2)}, u32[]{:S(2)}) collective-permute-start(bf16[4,32,768]{2,1,0:T(8,128)(2,1)S(1)} %pad_maximum_fusion.1), channel_id=1, source_target_pairs={{0,1},{1,0},{2,3},{3,2},{4,5},{5,4},{6,7},{7,6},{8,9},{9,8},{10,11... | collective-permute-start | bytes 589832 | tf_op jit(solution)/shard_map/ppermute | solution.py:360
  34.9 8.9 %collective-permute-start.4 = (bf16[4,32,768]{2,1,0:T(8,128)(2,1)S(1)}, bf16[4,32,768]{2,1,0:T(8,128)(2,1)S(1)}, u32[]{:S(2)}, u32[]{:S(2)}) collective-permute-start(bf16[4,32,768]{2,1,0:T(8,128)(2,1)S(1)} %pad_maximum_fusion.2), channel_id=1, source_target_pairs={{0,2},{1,3},{2,0},{3,1},{4,6},{5,7},{6,4},{7,5},{8,10},{9,11},{10,... | collective-permute-start | bytes 589832 | tf_op jit(solution)/shard_map/ppermute | solution.py:360
  35.3 10.9 %collective-permute-start.5 = (bf16[4,32,768]{2,1,0:T(8,128)(2,1)S(1)}, bf16[4,32,768]{2,1,0:T(8,128)(2,1)S(1)}, u32[]{:S(2)}, u32[]{:S(2)}) collective-permute-start(bf16[4,32,768]{2,1,0:T(8,128)(2,1)S(1)} %pad_maximum_fusion.3), channel_id=1, source_target_pairs={{0,3},{1,2},{2,1},{3,0},{4,7},{5,6},{6,5},{7,4},{8,11},{9,10},{10,... | collective-permute-start | bytes 589832 | tf_op jit(solution)/shard_map/ppermute | solution.py:360
  40.0 9.5 %collective-permute-start.15 = (bf16[4,32,768]{2,1,0:T(8,128)(2,1)S(1)}, bf16[4,32,768]{2,1,0:T(8,128)(2,1)S(1)}, u32[]{:S(2)}, u32[]{:S(2)}) collective-permute-start(bf16[4,32,768]{2,1,0:T(8,128)(2,1)S(1)} %pad_maximum_fusion.9), channel_id=1, source_target_pairs={{0,1},{1,0},{2,3},{3,2},{4,5},{5,4},{6,7},{7,6},{8,9},{9,8},{10,11... | collective-permute-start | bytes 589832 | tf_op jit(solution)/shard_map/ppermute | solution.py:360
  41.9 8.1 %collective-permute-start.16 = (bf16[4,32,768]{2,1,0:T(8,128)(2,1)S(1)}, bf16[4,32,768]{2,1,0:T(8,128)(2,1)S(1)}, u32[]{:S(2)}, u32[]{:S(2)}) collective-permute-start(bf16[4,32,768]{2,1,0:T(8,128)(2,1)S(1)} %pad_maximum_fusion.10), channel_id=1, source_target_pairs={{0,2},{1,3},{2,0},{3,1},{4,6},{5,7},{6,4},{7,5},{8,10},{9,11},{10,... | collective-permute-start | bytes 589832 | tf_op jit(solution)/shard_map/ppermute | solution.py:360
  42.3 12.0 %collective-permute-start.17 = (bf16[4,32,768]{2,1,0:T(8,128)(2,1)S(1)}, bf16[4,32,768]{2,1,0:T(8,128)(2,1)S(1)}, u32[]{:S(2)}, u32[]{:S(2)}) collective-permute-start(bf16[4,32,768]{2,1,0:T(8,128)(2,1)S(1)} %pad_maximum_fusion.11), channel_id=1, source_target_pairs={{0,3},{1,2},{2,1},{3,0},{4,7},{5,6},{6,5},{7,4},{8,11},{9,10},{10,... | collective-permute-start | bytes 589832 | tf_op jit(solution)/shard_map/ppermute | solution.py:360
  46.9 10.0 %collective-permute-start.6 = (bf16[4,32,768]{2,1,0:T(8,128)(2,1)S(1)}, bf16[4,32,768]{2,1,0:T(8,128)(2,1)S(1)}, u32[]{:S(2)}, u32[]{:S(2)}) collective-permute-start(bf16[4,32,768]{2,1,0:T(8,128)(2,1)S(1)} %get-tuple-element.52), channel_id=1, source_target_pairs={{0,4},{1,5},{2,6},{3,7},{4,0},{5,1},{6,2},{7,3},{8,12},{9,13},{10,... | collective-permute-start | bytes 589832 | tf_op jit(solution)/shard_map/ppermute | solution.py:360
  47.0 14.9 %collective-permute-start.7 = (bf16[4,32,768]{2,1,0:T(8,128)(2,1)S(1)}, bf16[4,32,768]{2,1,0:T(8,128)(2,1)S(1)}, u32[]{:S(2)}, u32[]{:S(2)}) collective-permute-start(bf16[4,32,768]{2,1,0:T(8,128)(2,1)S(1)} %get-tuple-element.53), channel_id=1, source_target_pairs={{0,8},{1,9},{2,10},{3,11},{4,12},{5,13},{6,14},{7,15},{8,0},{9,1},... | collective-permute-start | bytes 589832 | tf_op jit(solution)/shard_map/ppermute | solution.py:360
  49.5 17.7 %collective-permute-start.8 = (bf16[4,32,768]{2,1,0:T(8,128)(2,1)S(1)}, bf16[4,32,768]{2,1,0:T(8,128)(2,1)S(1)}, u32[]{:S(2)}, u32[]{:S(2)}) collective-permute-start(bf16[4,32,768]{2,1,0:T(8,128)(2,1)S(1)} %get-tuple-element.54), channel_id=1, source_target_pairs={{0,12},{1,13},{2,14},{3,15},{4,8},{5,9},{6,10},{7,11},{8,4},{9,5},... | collective-permute-start | bytes 589832 | tf_op jit(solution)/shard_map/ppermute | solution.py:360
  55.0 13.7 %collective-permute-start.18 = (bf16[4,32,768]{2,1,0:T(8,128)(2,1)S(1)}, bf16[4,32,768]{2,1,0:T(8,128)(2,1)S(1)}, u32[]{:S(2)}, u32[]{:S(2)}) collective-permute-start(bf16[4,32,768]{2,1,0:T(8,128)(2,1)S(1)} %get-tuple-element.63), channel_id=1, source_target_pairs={{0,1},{1,0},{2,3},{3,2},{4,5},{5,4},{6,7},{7,6},{8,9},{9,8},{10,11... | collective-permute-start | bytes 589832 | tf_op jit(solution)/shard_map/ppermute | solution.py:360
  55.3 14.9 %collective-permute-start.19 = (bf16[4,32,768]{2,1,0:T(8,128)(2,1)S(1)}, bf16[4,32,768]{2,1,0:T(8,128)(2,1)S(1)}, u32[]{:S(2)}, u32[]{:S(2)}) collective-permute-start(bf16[4,32,768]{2,1,0:T(8,128)(2,1)S(1)} %get-tuple-element.64), channel_id=1, source_target_pairs={{0,2},{1,3},{2,0},{3,1},{4,6},{5,7},{6,4},{7,5},{8,10},{9,11},{10,... | collective-permute-start | bytes 589832 | tf_op jit(solution)/shard_map/ppermute | solution.py:360
  57.0 13.2 %collective-permute-start.20 = (bf16[4,32,768]{2,1,0:T(8,128)(2,1)S(1)}, bf16[4,32,768]{2,1,0:T(8,128)(2,1)S(1)}, u32[]{:S(2)}, u32[]{:S(2)}) collective-permute-start(bf16[4,32,768]{2,1,0:T(8,128)(2,1)S(1)} %get-tuple-element.65), channel_id=1, source_target_pairs={{0,3},{1,2},{2,1},{3,0},{4,7},{5,6},{6,5},{7,4},{8,11},{9,10},{10,... | collective-permute-start | bytes 589832 | tf_op jit(solution)/shard_map/ppermute | solution.py:360
  67.3 5.7 %collective-permute-start.9 = (bf16[4,32,768]{2,1,0:T(8,128)(2,1)S(1)}, bf16[4,32,768]{2,1,0:T(8,128)(2,1)S(1)}, u32[]{:S(2)}, u32[]{:S(2)}) collective-permute-start(bf16[4,32,768]{2,1,0:T(8,128)(2,1)S(1)} %pad_maximum_fusion.5), channel_id=1, source_target_pairs={{0,1},{1,0},{2,3},{3,2},{4,5},{5,4},{6,7},{7,6},{8,9},{9,8},{10,11... | collective-permute-start | bytes 589832 | tf_op jit(solution)/shard_map/ppermute | solution.py:360
  68.3 6.6 %collective-permute-start.10 = (bf16[4,32,768]{2,1,0:T(8,128)(2,1)S(1)}, bf16[4,32,768]{2,1,0:T(8,128)(2,1)S(1)}, u32[]{:S(2)}, u32[]{:S(2)}) collective-permute-start(bf16[4,32,768]{2,1,0:T(8,128)(2,1)S(1)} %pad_maximum_fusion.6), channel_id=1, source_target_pairs={{0,2},{1,3},{2,0},{3,1},{4,6},{5,7},{6,4},{7,5},{8,10},{9,11},{10,... | collective-permute-start | bytes 589832 | tf_op jit(solution)/shard_map/ppermute | solution.py:360
  68.7 10.8 %collective-permute-start.11 = (bf16[4,32,768]{2,1,0:T(8,128)(2,1)S(1)}, bf16[4,32,768]{2,1,0:T(8,128)(2,1)S(1)}, u32[]{:S(2)}, u32[]{:S(2)}) collective-permute-start(bf16[4,32,768]{2,1,0:T(8,128)(2,1)S(1)} %pad_maximum_fusion.7), channel_id=1, source_target_pairs={{0,3},{1,2},{2,1},{3,0},{4,7},{5,6},{6,5},{7,4},{8,11},{9,10},{10,... | collective-permute-start | bytes 589832 | tf_op jit(solution)/shard_map/ppermute | solution.py:360
  70.3 24.3 %collective-permute-start.21 = (bf16[4,32,768]{2,1,0:T(8,128)(2,1)S(1)}, bf16[4,32,768]{2,1,0:T(8,128)(2,1)S(1)}, u32[]{:S(2)}, u32[]{:S(2)}) collective-permute-start(bf16[4,32,768]{2,1,0:T(8,128)(2,1)S(1)} %pad_maximum_fusion.13), channel_id=1, source_target_pairs={{0,4},{1,5},{2,6},{3,7},{4,0},{5,1},{6,2},{7,3},{8,12},{9,13},{10,... | collective-permute-start | bytes 589832 | tf_op jit(solution)/shard_map/ppermute | solution.py:360
  70.4 24.2 %collective-permute-start.22 = (bf16[4,32,768]{2,1,0:T(8,128)(2,1)S(1)}, bf16[4,32,768]{2,1,0:T(8,128)(2,1)S(1)}, u32[]{:S(2)}, u32[]{:S(2)}) collective-permute-start(bf16[4,32,768]{2,1,0:T(8,128)(2,1)S(1)} %pad_maximum_fusion.14), channel_id=1, source_target_pairs={{0,8},{1,9},{2,10},{3,11},{4,12},{5,13},{6,14},{7,15},{8,0},{9,1},... | collective-permute-start | bytes 589832 | tf_op jit(solution)/shard_map/ppermute | solution.py:360
  73.0 21.6 %collective-permute-start.23 = (bf16[4,32,768]{2,1,0:T(8,128)(2,1)S(1)}, bf16[4,32,768]{2,1,0:T(8,128)(2,1)S(1)}, u32[]{:S(2)}, u32[]{:S(2)}) collective-permute-start(bf16[4,32,768]{2,1,0:T(8,128)(2,1)S(1)} %pad_maximum_fusion.15), channel_id=1, source_target_pairs={{0,12},{1,13},{2,14},{3,15},{4,8},{5,9},{6,10},{7,11},{8,4},{9,5},... | collective-permute-start | bytes 589832 | tf_op jit(solution)/shard_map/ppermute | solution.py:360

commit v4 on v3

--- a/solution.py
+++ b/solution.py
@@ -47,9 +47,19 @@
     return inner if by_inner else n // inner
 
 
+ORDER = (0, 2, 3, 1)
+
+
+def partner(place):
+    if isinstance(place, int):
+        return ORDER[place]
+    return sum(jnp.where(place == i, k, 0) for i, k in enumerate(ORDER))
+
+
 def number(mode, group, member):
     by_inner, inner = mode
-    return member * inner + group if by_inner else group * inner + member
+    high, low = (member, group) if by_inner else (group, member)
+    return partner(high) * inner + partner(low)
 
 
 def major(n, mode):
@@ -355,9 +365,8 @@
 
     def permutes(slabs, step):
         got = list(slabs)
-        count = len(slabs)
-        for k in [2, 3, 1] if count == 4 else range(count - 1, 0, -1):
-            got[k] = lax.ppermute(slabs[k], "seq", [(i, i ^ (k * step)) for i in range(n)])
+        for i in range(1, len(slabs)):
+            got[i] = lax.ppermute(slabs[i], "seq", [(j, j ^ (ORDER[i] * step)) for j in range(n)])
         return got
 
     def across(slabs):

time: 96.5 us -> 91.6 us (0.949)
  starting transfers between devices: 34.1 us -> 22.8 us
  waiting for transfers between devices: 27.9 us -> 34.3 us
    ppermute x24, starting transfers between devices: 34.1 us -> 22.8 us  [permutes(): lax.ppermute(slabs[i], 'seq', [(j, j ^ ORDER[i] * step) for j in range(n)])]
    ppermute x24, waiting for transfers between devices: 27.9 us -> 34.3 us  [permutes(): lax.ppermute(slabs[i], 'seq', [(j, j ^ ORDER[i] * step) for j in range(n)])]
  transfers between devices with their start and end apart: 24 -> 24, of which waited for: 9 -> 11; matrix products, arithmetic and copies ran while one was open for 2% -> 2% of each run, Pallas kernels for 27% -> 28%
where the time goes in v4:
time: 91.6 us; the launch traced here: 91.4 us
  waiting for transfers between devices  34.3 us (37%)
  Pallas kernels  30.1 us (33%)
  starting transfers between devices  22.8 us (25%)
  matrix products  1.4 us (2%)
  local copies, waits for them, and re-layouts  1.29 us (1%)
  between operations  1.02 us (1%)
    ppermute x24, waiting for transfers between devices, permutes(): lax.ppermute(slabs[i], 'seq', [(j, j ^ ORDER[i] * step) for j in range(n)])  34.3 us
    ppermute x24, starting transfers between devices, permutes(): lax.ppermute(slabs[i], 'seq', [(j, j ^ ORDER[i] * step) for j in range(n)])  22.8 us
    pallas_call x1, Pallas kernels, grads(): pl.pallas_call(functools.partial(grads_kernel, mode, slots, group, half,...  15 us
    pallas_call x1, Pallas kernels, inner_slabs(): pl.pallas_call(functools.partial(inner_kernel, mode, merges, group), in_s...  9.29 us
    pallas_call x1, Pallas kernels, gated_slabs(): pl.pallas_call(functools.partial(gated_kernel, n, mode, rows), in_specs=[...  2.75 us
  transfers between devices with their start and end apart: 24, of which 11 were waited for; matrix products, arithmetic and copies ran while one was open for 2% of the time, Pallas kernels for 28%

profile of v4, /device:TPU:11, one launch (start us, length us, event | category | flops | bytes accessed | tf_op | source)
XLA Modules:
  0.0 91.4 jit_solution(4106713234014255045)
XLA Ops:
  0.6 2.7 %gated_slabs.1 = (bf16[128,768]{1,0:T(8,128)(2,1)}, bf16[128,768]{1,0:T(8,128)(2,1)}, bf16[128,768]{1,0:T(8,128)(2,1)}, bf16[128,768]{1,0:T(8,128)(2,1)}) custom-call(bf16[512,768]{1,0:T(8,128)(2,1)} %bitcast.29, bf16[512,768]{1,0:T(8,128)(2,1)} %bitcast.31), custom_call_target="tpu_custom_call" | custom-call | flops 402653184 | bytes 2359296 | tf_op jit(solution)/shard_map/gated_slabs/pallas_call | solution.py:103
  3.4 2.4 %collective-permute-start = (bf16[4,32,768]{2,1,0:T(8,128)(2,1)}, bf16[4,32,768]{2,1,0:T(8,128)(2,1)S(1)}, u32[]{:S(2)}, u32[]{:S(2)}) collective-permute-start(bf16[4,32,768]{2,1,0:T(8,128)(2,1)} %bitcast.45), channel_id=1, source_target_pairs={{0,8},{1,9},{2,10},{3,11},{4,12},{5,13},{6,14},{7,15},{8,0},{9,1},... | collective-permute-start | bytes 589832 | tf_op jit(solution)/shard_map/ppermute | solution.py:369
  5.8 1.3 %collective-permute-start.2 = (bf16[4,32,768]{2,1,0:T(8,128)(2,1)}, bf16[4,32,768]{2,1,0:T(8,128)(2,1)S(1)}, u32[]{:S(2)}, u32[]{:S(2)}) collective-permute-start(bf16[4,32,768]{2,1,0:T(8,128)(2,1)} %bitcast.43), channel_id=1, source_target_pairs={{0,4},{1,5},{2,6},{3,7},{4,0},{5,1},{6,2},{7,3},{8,12},{9,13},{10,... | collective-permute-start | bytes 589832 | tf_op jit(solution)/shard_map/ppermute | solution.py:369
  7.0 1.0 %copy-done.2 = bf16[32,16,512]{2,1,0:T(8,128)(2,1)S(1)} copy-done((bf16[32,16,512]{2,1,0:T(8,128)(2,1)S(1)}, bf16[32,16,512]{2,1,0:T(8,128)(2,1)}, u32[]{:S(2)}) %copy-start.2) | copy-done | bytes 524312
  8.1 9.3 %inner_slabs.1 = (bf16[128,768]{1,0:T(8,128)(2,1)S(1)}, bf16[128,768]{1,0:T(8,128)(2,1)S(1)}, bf16[128,768]{1,0:T(8,128)(2,1)S(1)}, bf16[128,768]{1,0:T(8,128)(2...) custom-call(bf16[32,16,512]{2,1,0:T(8,128)(2,1)S(1)} %copy-done.2, ...), custom_call_target="tpu_custom_call" | custom-call | flops 402653184 | bytes 25165824 | tf_op jit(solution)/shard_map/inner_slabs/pallas_call | solution.py:162
  17.4 1.5 %collective-permute-start.12 = (bf16[4,32,768]{2,1,0:T(8,128)(2,1)S(1)}, bf16[4,32,768]{2,1,0:T(8,128)(2,1)S(1)}, u32[]{:S(2)}, u32[]{:S(2)}) collective-permute-start(bf16[4,32,768]{2,1,0:T(8,128)(2,1)S(1)} %bitcast.39), channel_id=1, source_target_pairs={{0,8},{1,9},{2,10},{3,11},{4,12},{5,13},{6,14},{7,15},{8,0},{9,1},... | collective-permute-start | bytes 589832 | tf_op jit(solution)/shard_map/ppermute | solution.py:369
  19.1 2.0 %collective-permute-start.14 = (bf16[4,32,768]{2,1,0:T(8,128)(2,1)S(1)}, bf16[4,32,768]{2,1,0:T(8,128)(2,1)S(1)}, u32[]{:S(2)}, u32[]{:S(2)}) collective-permute-start(bf16[4,32,768]{2,1,0:T(8,128)(2,1)S(1)} %bitcast.37), channel_id=1, source_target_pairs={{0,4},{1,5},{2,6},{3,7},{4,0},{5,1},{6,2},{7,3},{8,12},{9,13},{10,... | collective-permute-start | bytes 589832 | tf_op jit(solution)/shard_map/ppermute | solution.py:369
  21.1 10.6 %collective-permute-done.1 = bf16[4,32,768]{2,1,0:T(8,128)(2,1)S(1)} collective-permute-done((bf16[4,32,768]{2,1,0:T(8,128)(2,1)}, bf16[4,32,768]{2,1,0:T(8,128)(2,1)S(1)}, u32[]{:S(2)}, u32[]{:S(2)}) %collective-permute-start.1) | collective-permute-done | bytes 196640 | tf_op jit(solution)/shard_map/ppermute | solution.py:369
  31.8 0.3 collective-permute-start.3
  32.2 2.8 %collective-permute-start.4 = (bf16[4,32,768]{2,1,0:T(8,128)(2,1)S(1)}, bf16[4,32,768]{2,1,0:T(8,128)(2,1)S(1)}, u32[]{:S(2)}, u32[]{:S(2)}) collective-permute-start(bf16[4,32,768]{2,1,0:T(8,128)(2,1)S(1)} %pad_maximum_fusion.2), channel_id=1, source_target_pairs={{0,3},{1,2},{2,1},{3,0},{4,7},{5,6},{6,5},{7,4},{8,11},{9,10},{10,... | collective-permute-start | bytes 589832 | tf_op jit(solution)/shard_map/ppermute | solution.py:369
  35.0 0.8 collective-permute-done.12
  35.8 0.6 collective-permute-start.5
  36.4 3.6 %collective-permute-done.13 = bf16[4,32,768]{2,1,0:T(8,128)(2,1)S(1)} collective-permute-done((bf16[4,32,768]{2,1,0:T(8,128)(2,1)S(1)}, bf16[4,32,768]{2,1,0:T(8,128)(2,1)S(1)}, u32[]{:S(2)}, u32[]{:S(2)}) %collective-permute-start.13) | collective-permute-done | bytes 196640 | tf_op jit(solution)/shard_map/ppermute | solution.py:369
  40.5 1.9 %collective-permute-start.16 = (bf16[4,32,768]{2,1,0:T(8,128)(2,1)S(1)}, bf16[4,32,768]{2,1,0:T(8,128)(2,1)S(1)}, u32[]{:S(2)}, u32[]{:S(2)}) collective-permute-start(bf16[4,32,768]{2,1,0:T(8,128)(2,1)S(1)} %pad_maximum_fusion.10), channel_id=1, source_target_pairs={{0,3},{1,2},{2,1},{3,0},{4,7},{5,6},{6,5},{7,4},{8,11},{9,10},{10,... | collective-permute-start | bytes 589832 | tf_op jit(solution)/shard_map/ppermute | solution.py:369
  42.8 0.7 back.1
  43.6 2.1 %collective-permute-start.7 = (bf16[4,32,768]{2,1,0:T(8,128)(2,1)S(1)}, bf16[4,32,768]{2,1,0:T(8,128)(2,1)S(1)}, u32[]{:S(2)}, u32[]{:S(2)}) collective-permute-start(bf16[4,32,768]{2,1,0:T(8,128)(2,1)S(1)} %get-tuple-element.53), channel_id=1, source_target_pairs={{0,12},{1,13},{2,14},{3,15},{4,8},{5,9},{6,10},{7,11},{8,4},{9,5},... | collective-permute-start | bytes 589832 | tf_op jit(solution)/shard_map/ppermute | solution.py:369
  45.7 0.7 collective-permute-done.15.refs_1_
  46.4 0.8 collective-permute-start.8
  47.2 4.2 %collective-permute-done.16.refs_2_ = bf16[4,32,768]{2,1,0:T(8,128)(2,1)S(1)} collective-permute-done((bf16[4,32,768]{2,1,0:T(8,128)(2,1)S(1)}, bf16[4,32,768]{2,1,0:T(8,128)(2,1)S(1)}, u32[]{:S(2)}, u32[]{:S(2)}) %collective-permute-start.16) | collective-permute-done | bytes 196640 | tf_op jit(solution)/shard_map/ppermute | solution.py:369
  51.5 0.7 forth.1
  52.2 0.3 collective-permute-start.18
  52.5 0.9 %collective-permute-start.19 = (bf16[4,32,768]{2,1,0:T(8,128)(2,1)S(1)}, bf16[4,32,768]{2,1,0:T(8,128)(2,1)S(1)}, u32[]{:S(2)}, u32[]{:S(2)}) collective-permute-start(bf16[4,32,768]{2,1,0:T(8,128)(2,1)S(1)} %get-tuple-element.64), channel_id=1, source_target_pairs={{0,3},{1,2},{2,1},{3,0},{4,7},{5,6},{6,5},{7,4},{8,11},{9,10},{10,... | collective-permute-start | bytes 589832 | tf_op jit(solution)/shard_map/ppermute | solution.py:369
  53.4 1.4 %fusion = bf16[1,512,512]{2,1,0:T(8,128)(2,1)} fusion(bf16[512,768]{1,0:T(8,128)(2,1)S(1)} %get-tuple-element.69, bf16[512,768]{1,0:T(8,128)(2,1)S(1)} %get-tuple-element.70), kind=kOutput, calls=%fused_computation.1 | convolution fusion | flops 402915328 | bytes 2097152 | tf_op jit(solution)/shard_map/dot_general | solution.py:71
  54.8 0.9 collective-permute-done.6
  55.7 1.8 %collective-permute-start.20 = (bf16[4,32,768]{2,1,0:T(8,128)(2,1)S(1)}, bf16[4,32,768]{2,1,0:T(8,128)(2,1)S(1)}, u32[]{:S(2)}, u32[]{:S(2)}) collective-permute-start(bf16[4,32,768]{2,1,0:T(8,128)(2,1)S(1)} %get-tuple-element.65), channel_id=1, source_target_pairs={{0,1},{1,0},{2,3},{3,2},{4,5},{5,4},{6,7},{7,6},{8,9},{9,8},{10,11... | collective-permute-start | bytes 589832 | tf_op jit(solution)/shard_map/ppermute | solution.py:369
  57.5 5.9 %collective-permute-done.7 = bf16[4,32,768]{2,1,0:T(8,128)(2,1)S(1)} collective-permute-done((bf16[4,32,768]{2,1,0:T(8,128)(2,1)S(1)}, bf16[4,32,768]{2,1,0:T(8,128)(2,1)S(1)}, u32[]{:S(2)}, u32[]{:S(2)}) %collective-permute-start.7) | collective-permute-done | bytes 196640 | tf_op jit(solution)/shard_map/ppermute | solution.py:369
  63.8 2.2 %collective-permute-start.10 = (bf16[4,32,768]{2,1,0:T(8,128)(2,1)S(1)}, bf16[4,32,768]{2,1,0:T(8,128)(2,1)S(1)}, u32[]{:S(2)}, u32[]{:S(2)}) collective-permute-start(bf16[4,32,768]{2,1,0:T(8,128)(2,1)S(1)} %pad_maximum_fusion.6), channel_id=1, source_target_pairs={{0,3},{1,2},{2,1},{3,0},{4,7},{5,6},{6,5},{7,4},{8,11},{9,10},{10,... | collective-permute-start | bytes 589832 | tf_op jit(solution)/shard_map/ppermute | solution.py:369
  66.5 2.7 %collective-permute-done.9.refs_3_ = bf16[4,32,768]{2,1,0:T(8,128)(2,1)S(1)} collective-permute-done((bf16[4,32,768]{2,1,0:T(8,128)(2,1)S(1)}, bf16[4,32,768]{2,1,0:T(8,128)(2,1)S(1)}, u32[]{:S(2)}, u32[]{:S(2)}) %collective-permute-start.9) | collective-permute-done | bytes 196640 | tf_op jit(solution)/shard_map/ppermute | solution.py:369
  69.2 0.9 collective-permute-start.23
  70.2 4.5 %collective-permute-done.10.refs_4_ = bf16[4,32,768]{2,1,0:T(8,128)(2,1)S(1)} collective-permute-done((bf16[4,32,768]{2,1,0:T(8,128)(2,1)S(1)}, bf16[4,32,768]{2,1,0:T(8,128)(2,1)S(1)}, u32[]{:S(2)}, u32[]{:S(2)}) %collective-permute-start.10) | collective-permute-done | bytes 196640 | tf_op jit(solution)/shard_map/ppermute | solution.py:369
  74.7 15.0 %grads.1 = (bf16[16384,768]{1,0:T(8,128)(2,1)}, bf16[32,16,512]{2,1,0:T(8,128)(2,1)}) custom-call(bf16[32,16,512]{2,1,0:T(8,128)(2,1)S(1)} %copy-done.2, bf16[512,512]{1,0:T(8,128)(2,1)S(1)} %get-tuple-element.41.matrix_ref, bf16[8192,768]{1,0:T(8,128)(2,1)S(1)} %get-tuple-element.42.refs_0_, bf16[8192,768]{1,0:T(8,128)(2,1)S(1)} %get-tuple-element.43.refs_1_, ...), custom_call_target="tpu_custom_call" | custom-call | flops 805306368 | bytes 25165824 | tf_op jit(solution)/shard_map/grads/pallas_call | solution.py:287
  89.8 1.6 %gates.1 = (bf16[512,768]{1,0:T(8,128)(2,1)}, bf16[512,768]{1,0:T(8,128)(2,1)}) custom-call(bf16[512,512]{1,0:T(8,128)(2,1)S(1)} %get-tuple-element.40.matrix_ref, bf16[512,768]{1,0:T(8,128)(2,1)S(1)} %bitcast.30, bf16[512,768]{1,0:T(8,128)(2,1)S(1)} %bitcast.32, bf16[128,768]{1,0:T(8,128)(2,1)S(1)} %bitcast.33, bf16[128,768]{1,0:T(8,128)(2,1)S(1)} %bitcast.34, ...), custom_call_target="tpu_custom_call" | custom-call | flops 402653184 | bytes 3932160 | tf_op jit(solution)/shard_map/gates/pallas_call | solution.py:335
  (63 shorter events, 2.1 us)
Async XLA Ops:
  0.6 42.2 %copy-start.3 = (bf16[1,512,512]{2,1,0:T(8,128)(2,1)S(1)}, bf16[1,512,512]{2,1,0:T(8,128)(2,1)}, u32[]{:S(2)}) copy-start(bf16[1,512,512]{2,1,0:T(8,128)(2,1)} %s_ref.3) | copy-start | bytes 1572868
  3.4 15.7 %collective-permute-start = (bf16[4,32,768]{2,1,0:T(8,128)(2,1)}, bf16[4,32,768]{2,1,0:T(8,128)(2,1)S(1)}, u32[]{:S(2)}, u32[]{:S(2)}) collective-permute-start(bf16[4,32,768]{2,1,0:T(8,128)(2,1)} %bitcast.45), channel_id=1, source_target_pairs={{0,8},{1,9},{2,10},{3,11},{4,12},{5,13},{6,14},{7,15},{8,0},{9,1},... | collective-permute-start | bytes 589832 | tf_op jit(solution)/shard_map/ppermute | solution.py:369
  5.8 25.9 %collective-permute-start.1 = (bf16[4,32,768]{2,1,0:T(8,128)(2,1)}, bf16[4,32,768]{2,1,0:T(8,128)(2,1)S(1)}, u32[]{:S(2)}, u32[]{:S(2)}) collective-permute-start(bf16[4,32,768]{2,1,0:T(8,128)(2,1)} %bitcast.44), channel_id=1, source_target_pairs={{0,12},{1,13},{2,14},{3,15},{4,8},{5,9},{6,10},{7,11},{8,4},{9,5},... | collective-permute-start | bytes 589832 | tf_op jit(solution)/shard_map/ppermute | solution.py:369
  5.8 25.9 %collective-permute-start.2 = (bf16[4,32,768]{2,1,0:T(8,128)(2,1)}, bf16[4,32,768]{2,1,0:T(8,128)(2,1)S(1)}, u32[]{:S(2)}, u32[]{:S(2)}) collective-permute-start(bf16[4,32,768]{2,1,0:T(8,128)(2,1)} %bitcast.43), channel_id=1, source_target_pairs={{0,4},{1,5},{2,6},{3,7},{4,0},{5,1},{6,2},{7,3},{8,12},{9,13},{10,... | collective-permute-start | bytes 589832 | tf_op jit(solution)/shard_map/ppermute | solution.py:369
  7.0 1.0 %copy-start.2 = (bf16[32,16,512]{2,1,0:T(8,128)(2,1)S(1)}, bf16[32,16,512]{2,1,0:T(8,128)(2,1)}, u32[]{:S(2)}) copy-start(bf16[32,16,512]{2,1,0:T(8,128)(2,1)} %w_ref.2) | copy-start | bytes 1572868
  8.1 23.6 %copy-start.4 = (bf16[128,768]{1,0:T(8,128)(2,1)S(1)}, bf16[128,768]{1,0:T(8,128)(2,1)}, u32[]{:S(2)}) copy-start(bf16[128,768]{1,0:T(8,128)(2,1)} %get-tuple-element.38) | copy-start | bytes 589828
  17.4 72.4 %copy-start = (bf16[32,16,768]{2,1,0:T(8,128)(2,1)S(1)}, bf16[32,16,768]{2,1,0:T(8,128)(2,1)}, u32[]{:S(2)}) copy-start(bf16[32,16,768]{2,1,0:T(8,128)(2,1)} %param.6) | copy-start | bytes 2359300
  17.4 72.4 %copy-start.1 = (bf16[32,16,768]{2,1,0:T(8,128)(2,1)S(1)}, bf16[32,16,768]{2,1,0:T(8,128)(2,1)}, u32[]{:S(2)}) copy-start(bf16[32,16,768]{2,1,0:T(8,128)(2,1)} %param.7) | copy-start | bytes 2359300
  17.4 18.4 %collective-permute-start.12 = (bf16[4,32,768]{2,1,0:T(8,128)(2,1)S(1)}, bf16[4,32,768]{2,1,0:T(8,128)(2,1)S(1)}, u32[]{:S(2)}, u32[]{:S(2)}) collective-permute-start(bf16[4,32,768]{2,1,0:T(8,128)(2,1)S(1)} %bitcast.39), channel_id=1, source_target_pairs={{0,8},{1,9},{2,10},{3,11},{4,12},{5,13},{6,14},{7,15},{8,0},{9,1},... | collective-permute-start | bytes 589832 | tf_op jit(solution)/shard_map/ppermute | solution.py:369
  18.9 21.2 %collective-permute-start.13 = (bf16[4,32,768]{2,1,0:T(8,128)(2,1)S(1)}, bf16[4,32,768]{2,1,0:T(8,128)(2,1)S(1)}, u32[]{:S(2)}, u32[]{:S(2)}) collective-permute-start(bf16[4,32,768]{2,1,0:T(8,128)(2,1)S(1)} %bitcast.38), channel_id=1, source_target_pairs={{0,12},{1,13},{2,14},{3,15},{4,8},{5,9},{6,10},{7,11},{8,4},{9,5},... | collective-permute-start | bytes 589832 | tf_op jit(solution)/shard_map/ppermute | solution.py:369
  19.1 21.0 %collective-permute-start.14 = (bf16[4,32,768]{2,1,0:T(8,128)(2,1)S(1)}, bf16[4,32,768]{2,1,0:T(8,128)(2,1)S(1)}, u32[]{:S(2)}, u32[]{:S(2)}) collective-permute-start(bf16[4,32,768]{2,1,0:T(8,128)(2,1)S(1)} %bitcast.37), channel_id=1, source_target_pairs={{0,4},{1,5},{2,6},{3,7},{4,0},{5,1},{6,2},{7,3},{8,12},{9,13},{10,... | collective-permute-start | bytes 589832 | tf_op jit(solution)/shard_map/ppermute | solution.py:369
  31.8 10.7 %collective-permute-start.3 = (bf16[4,32,768]{2,1,0:T(8,128)(2,1)S(1)}, bf16[4,32,768]{2,1,0:T(8,128)(2,1)S(1)}, u32[]{:S(2)}, u32[]{:S(2)}) collective-permute-start(bf16[4,32,768]{2,1,0:T(8,128)(2,1)S(1)} %pad_maximum_fusion.1), channel_id=1, source_target_pairs={{0,2},{1,3},{2,0},{3,1},{4,6},{5,7},{6,4},{7,5},{8,10},{9,11},{10,... | collective-permute-start | bytes 589832 | tf_op jit(solution)/shard_map/ppermute | solution.py:369
  32.2 10.6 %collective-permute-start.4 = (bf16[4,32,768]{2,1,0:T(8,128)(2,1)S(1)}, bf16[4,32,768]{2,1,0:T(8,128)(2,1)S(1)}, u32[]{:S(2)}, u32[]{:S(2)}) collective-permute-start(bf16[4,32,768]{2,1,0:T(8,128)(2,1)S(1)} %pad_maximum_fusion.2), channel_id=1, source_target_pairs={{0,3},{1,2},{2,1},{3,0},{4,7},{5,6},{6,5},{7,4},{8,11},{9,10},{10,... | collective-permute-start | bytes 589832 | tf_op jit(solution)/shard_map/ppermute | solution.py:369
  35.8 7.0 %collective-permute-start.5 = (bf16[4,32,768]{2,1,0:T(8,128)(2,1)S(1)}, bf16[4,32,768]{2,1,0:T(8,128)(2,1)S(1)}, u32[]{:S(2)}, u32[]{:S(2)}) collective-permute-start(bf16[4,32,768]{2,1,0:T(8,128)(2,1)S(1)} %pad_maximum_fusion.3), channel_id=1, source_target_pairs={{0,1},{1,0},{2,3},{3,2},{4,5},{5,4},{6,7},{7,6},{8,9},{9,8},{10,11... | collective-permute-start | bytes 589832 | tf_op jit(solution)/shard_map/ppermute | solution.py:369
  40.1 6.3 %collective-permute-start.15 = (bf16[4,32,768]{2,1,0:T(8,128)(2,1)S(1)}, bf16[4,32,768]{2,1,0:T(8,128)(2,1)S(1)}, u32[]{:S(2)}, u32[]{:S(2)}) collective-permute-start(bf16[4,32,768]{2,1,0:T(8,128)(2,1)S(1)} %pad_maximum_fusion.9), channel_id=1, source_target_pairs={{0,2},{1,3},{2,0},{3,1},{4,6},{5,7},{6,4},{7,5},{8,10},{9,11},{10,... | collective-permute-start | bytes 589832 | tf_op jit(solution)/shard_map/ppermute | solution.py:369
  40.5 11.0 %collective-permute-start.16 = (bf16[4,32,768]{2,1,0:T(8,128)(2,1)S(1)}, bf16[4,32,768]{2,1,0:T(8,128)(2,1)S(1)}, u32[]{:S(2)}, u32[]{:S(2)}) collective-permute-start(bf16[4,32,768]{2,1,0:T(8,128)(2,1)S(1)} %pad_maximum_fusion.10), channel_id=1, source_target_pairs={{0,3},{1,2},{2,1},{3,0},{4,7},{5,6},{6,5},{7,4},{8,11},{9,10},{10,... | collective-permute-start | bytes 589832 | tf_op jit(solution)/shard_map/ppermute | solution.py:369
  42.5 8.9 %collective-permute-start.17 = (bf16[4,32,768]{2,1,0:T(8,128)(2,1)S(1)}, bf16[4,32,768]{2,1,0:T(8,128)(2,1)S(1)}, u32[]{:S(2)}, u32[]{:S(2)}) collective-permute-start(bf16[4,32,768]{2,1,0:T(8,128)(2,1)S(1)} %pad_maximum_fusion.11), channel_id=1, source_target_pairs={{0,1},{1,0},{2,3},{3,2},{4,5},{5,4},{6,7},{7,6},{8,9},{9,8},{10,11... | collective-permute-start | bytes 589832 | tf_op jit(solution)/shard_map/ppermute | solution.py:369
  43.5 12.2 %collective-permute-start.6 = (bf16[4,32,768]{2,1,0:T(8,128)(2,1)S(1)}, bf16[4,32,768]{2,1,0:T(8,128)(2,1)S(1)}, u32[]{:S(2)}, u32[]{:S(2)}) collective-permute-start(bf16[4,32,768]{2,1,0:T(8,128)(2,1)S(1)} %get-tuple-element.52), channel_id=1, source_target_pairs={{0,8},{1,9},{2,10},{3,11},{4,12},{5,13},{6,14},{7,15},{8,0},{9,1},... | collective-permute-start | bytes 589832 | tf_op jit(solution)/shard_map/ppermute | solution.py:369
  43.6 19.8 %collective-permute-start.7 = (bf16[4,32,768]{2,1,0:T(8,128)(2,1)S(1)}, bf16[4,32,768]{2,1,0:T(8,128)(2,1)S(1)}, u32[]{:S(2)}, u32[]{:S(2)}) collective-permute-start(bf16[4,32,768]{2,1,0:T(8,128)(2,1)S(1)} %get-tuple-element.53), channel_id=1, source_target_pairs={{0,12},{1,13},{2,14},{3,15},{4,8},{5,9},{6,10},{7,11},{8,4},{9,5},... | collective-permute-start | bytes 589832 | tf_op jit(solution)/shard_map/ppermute | solution.py:369
  46.4 17.0 %collective-permute-start.8 = (bf16[4,32,768]{2,1,0:T(8,128)(2,1)S(1)}, bf16[4,32,768]{2,1,0:T(8,128)(2,1)S(1)}, u32[]{:S(2)}, u32[]{:S(2)}) collective-permute-start(bf16[4,32,768]{2,1,0:T(8,128)(2,1)S(1)} %get-tuple-element.54), channel_id=1, source_target_pairs={{0,4},{1,5},{2,6},{3,7},{4,0},{5,1},{6,2},{7,3},{8,12},{9,13},{10,... | collective-permute-start | bytes 589832 | tf_op jit(solution)/shard_map/ppermute | solution.py:369
  52.2 13.9 %collective-permute-start.18 = (bf16[4,32,768]{2,1,0:T(8,128)(2,1)S(1)}, bf16[4,32,768]{2,1,0:T(8,128)(2,1)S(1)}, u32[]{:S(2)}, u32[]{:S(2)}) collective-permute-start(bf16[4,32,768]{2,1,0:T(8,128)(2,1)S(1)} %get-tuple-element.63), channel_id=1, source_target_pairs={{0,2},{1,3},{2,0},{3,1},{4,6},{5,7},{6,4},{7,5},{8,10},{9,11},{10,... | collective-permute-start | bytes 589832 | tf_op jit(solution)/shard_map/ppermute | solution.py:369
  52.5 13.7 %collective-permute-start.19 = (bf16[4,32,768]{2,1,0:T(8,128)(2,1)S(1)}, bf16[4,32,768]{2,1,0:T(8,128)(2,1)S(1)}, u32[]{:S(2)}, u32[]{:S(2)}) collective-permute-start(bf16[4,32,768]{2,1,0:T(8,128)(2,1)S(1)} %get-tuple-element.64), channel_id=1, source_target_pairs={{0,3},{1,2},{2,1},{3,0},{4,7},{5,6},{6,5},{7,4},{8,11},{9,10},{10,... | collective-permute-start | bytes 589832 | tf_op jit(solution)/shard_map/ppermute | solution.py:369
  55.7 10.5 %collective-permute-start.20 = (bf16[4,32,768]{2,1,0:T(8,128)(2,1)S(1)}, bf16[4,32,768]{2,1,0:T(8,128)(2,1)S(1)}, u32[]{:S(2)}, u32[]{:S(2)}) collective-permute-start(bf16[4,32,768]{2,1,0:T(8,128)(2,1)S(1)} %get-tuple-element.65), channel_id=1, source_target_pairs={{0,1},{1,0},{2,3},{3,2},{4,5},{5,4},{6,7},{7,6},{8,9},{9,8},{10,11... | collective-permute-start | bytes 589832 | tf_op jit(solution)/shard_map/ppermute | solution.py:369
  63.5 5.7 %collective-permute-start.9 = (bf16[4,32,768]{2,1,0:T(8,128)(2,1)S(1)}, bf16[4,32,768]{2,1,0:T(8,128)(2,1)S(1)}, u32[]{:S(2)}, u32[]{:S(2)}) collective-permute-start(bf16[4,32,768]{2,1,0:T(8,128)(2,1)S(1)} %pad_maximum_fusion.5), channel_id=1, source_target_pairs={{0,2},{1,3},{2,0},{3,1},{4,6},{5,7},{6,4},{7,5},{8,10},{9,11},{10,... | collective-permute-start | bytes 589832 | tf_op jit(solution)/shard_map/ppermute | solution.py:369
  63.8 10.9 %collective-permute-start.10 = (bf16[4,32,768]{2,1,0:T(8,128)(2,1)S(1)}, bf16[4,32,768]{2,1,0:T(8,128)(2,1)S(1)}, u32[]{:S(2)}, u32[]{:S(2)}) collective-permute-start(bf16[4,32,768]{2,1,0:T(8,128)(2,1)S(1)} %pad_maximum_fusion.6), channel_id=1, source_target_pairs={{0,3},{1,2},{2,1},{3,0},{4,7},{5,6},{6,5},{7,4},{8,11},{9,10},{10,... | collective-permute-start | bytes 589832 | tf_op jit(solution)/shard_map/ppermute | solution.py:369
  66.1 8.6 %collective-permute-start.11 = (bf16[4,32,768]{2,1,0:T(8,128)(2,1)S(1)}, bf16[4,32,768]{2,1,0:T(8,128)(2,1)S(1)}, u32[]{:S(2)}, u32[]{:S(2)}) collective-permute-start(bf16[4,32,768]{2,1,0:T(8,128)(2,1)S(1)} %pad_maximum_fusion.7), channel_id=1, source_target_pairs={{0,1},{1,0},{2,3},{3,2},{4,5},{5,4},{6,7},{7,6},{8,9},{9,8},{10,11... | collective-permute-start | bytes 589832 | tf_op jit(solution)/shard_map/ppermute | solution.py:369
  66.3 23.4 %collective-permute-start.21 = (bf16[4,32,768]{2,1,0:T(8,128)(2,1)S(1)}, bf16[4,32,768]{2,1,0:T(8,128)(2,1)S(1)}, u32[]{:S(2)}, u32[]{:S(2)}) collective-permute-start(bf16[4,32,768]{2,1,0:T(8,128)(2,1)S(1)} %pad_maximum_fusion.13), channel_id=1, source_target_pairs={{0,8},{1,9},{2,10},{3,11},{4,12},{5,13},{6,14},{7,15},{8,0},{9,1},... | collective-permute-start | bytes 589832 | tf_op jit(solution)/shard_map/ppermute | solution.py:369
  66.4 23.3 %collective-permute-start.22 = (bf16[4,32,768]{2,1,0:T(8,128)(2,1)S(1)}, bf16[4,32,768]{2,1,0:T(8,128)(2,1)S(1)}, u32[]{:S(2)}, u32[]{:S(2)}) collective-permute-start(bf16[4,32,768]{2,1,0:T(8,128)(2,1)S(1)} %pad_maximum_fusion.14), channel_id=1, source_target_pairs={{0,12},{1,13},{2,14},{3,15},{4,8},{5,9},{6,10},{7,11},{8,4},{9,5},... | collective-permute-start | bytes 589832 | tf_op jit(solution)/shard_map/ppermute | solution.py:369
  69.2 20.5 %collective-permute-start.23 = (bf16[4,32,768]{2,1,0:T(8,128)(2,1)S(1)}, bf16[4,32,768]{2,1,0:T(8,128)(2,1)S(1)}, u32[]{:S(2)}, u32[]{:S(2)}) collective-permute-start(bf16[4,32,768]{2,1,0:T(8,128)(2,1)S(1)} %pad_maximum_fusion.15), channel_id=1, source_target_pairs={{0,4},{1,5},{2,6},{3,7},{4,0},{5,1},{6,2},{7,3},{8,12},{9,13},{10,... | collective-permute-start | bytes 589832 | tf_op jit(solution)/shard_map/ppermute | solution.py:369

commit v5 on v4

--- a/solution.py
+++ b/solution.py
@@ -247,7 +247,7 @@
 
     each = steps // held
 
-    def step(x_ref, start, i, carry):
+    def step(x_ref, start, early, i, carry):
         s = lax.rem(i, slots)
 
         @pl.when(i >= slots)
@@ -261,11 +261,25 @@
             out_buf[s, g * length : (g + 1) * length, :] = dot(w, f, ((0,), (0,))).astype(NARROW)
             x = x_ref[pl.ds(pl.multiple_of((block - start * group) * length, length), length), :]
             fg_buf[block] = dot(f, x, ((1,), (1,))).astype(NARROW)
-        put(i, s).start()
+            if early and (g + 1) * 2 == group:
+                piece(i, s, 0).start()
+        if early:
+            piece(i, s, 1).start()
+        else:
+            put(i, s).start()
         return carry
 
+    def piece(i, s, p):
+        size = rows // 2
+        there = pl.ds(pl.multiple_of(base * length + i * rows + p * size, size), size)
+        return pltpu.make_async_copy(out_buf.at[s, pl.ds(p * size, size), :], vg_ref.at[there, :], out_sem.at[s])
+
     for h in range(held):
-        lax.fori_loop(h * each, (h + 1) * each, functools.partial(step, x_refs[h], h * each), 0)
+        end = (h + 1) * each
+        peeled = 1 if h == held - 1 and group % 2 == 0 else 0
+        lax.fori_loop(h * each, end - peeled, functools.partial(step, x_refs[h], h * each, False), 0)
+        if peeled:
+            lax.fori_loop(end - 1, end, functools.partial(step, x_refs[h], h * each, True), 0)
     last = pltpu.make_async_copy(fg_buf, fg_ref.at[pl.ds(base, part)], fg_sem)
     last.start()
     for i in range(steps - slots, steps):

time: 91.6 us -> 91.2 us (level)
  no operation moved by 1% of the time
where the time goes in v5:
time: 91.2 us; the launch traced here: 91 us
  waiting for transfers between devices  34.3 us (38%)
  Pallas kernels  29.6 us (32%)
  starting transfers between devices  22.8 us (25%)
  matrix products  1.4 us (2%)
  local copies, waits for them, and re-layouts  1.29 us (1%)
  between operations  1.02 us (1%)
    ppermute x24, waiting for transfers between devices, permutes(): lax.ppermute(slabs[i], 'seq', [(j, j ^ ORDER[i] * step) for j in range(n)])  34.3 us
    ppermute x24, starting transfers between devices, permutes(): lax.ppermute(slabs[i], 'seq', [(j, j ^ ORDER[i] * step) for j in range(n)])  22.8 us
    pallas_call x1, Pallas kernels, grads(): pl.pallas_call(functools.partial(grads_kernel, mode, slots, group, half,...  14.5 us
    pallas_call x1, Pallas kernels, inner_slabs(): pl.pallas_call(functools.partial(inner_kernel, mode, merges, group), in_s...  9.29 us
    pallas_call x1, Pallas kernels, gated_slabs(): pl.pallas_call(functools.partial(gated_kernel, n, mode, rows), in_specs=[...  2.75 us
  transfers between devices with their start and end apart: 24, of which 11 were waited for; matrix products, arithmetic and copies ran while one was open for 2% of the time, Pallas kernels for 28%

profile of v5, /device:TPU:11, one launch (start us, length us, event | category | flops | bytes accessed | tf_op | source)
XLA Modules:
  0.0 91.0 jit_solution(9563518763700860933)
XLA Ops:
  0.6 2.7 %gated_slabs.1 = (bf16[128,768]{1,0:T(8,128)(2,1)}, bf16[128,768]{1,0:T(8,128)(2,1)}, bf16[128,768]{1,0:T(8,128)(2,1)}, bf16[128,768]{1,0:T(8,128)(2,1)}) custom-call(bf16[512,768]{1,0:T(8,128)(2,1)} %bitcast.29, bf16[512,768]{1,0:T(8,128)(2,1)} %bitcast.31), custom_call_target="tpu_custom_call" | custom-call | flops 402653184 | bytes 2359296 | tf_op jit(solution)/shard_map/gated_slabs/pallas_call | solution.py:103
  3.4 2.4 %collective-permute-start = (bf16[4,32,768]{2,1,0:T(8,128)(2,1)}, bf16[4,32,768]{2,1,0:T(8,128)(2,1)S(1)}, u32[]{:S(2)}, u32[]{:S(2)}) collective-permute-start(bf16[4,32,768]{2,1,0:T(8,128)(2,1)} %bitcast.45), channel_id=1, source_target_pairs={{0,8},{1,9},{2,10},{3,11},{4,12},{5,13},{6,14},{7,15},{8,0},{9,1},... | collective-permute-start | bytes 589832 | tf_op jit(solution)/shard_map/ppermute | solution.py:383
  5.8 1.3 %collective-permute-start.2 = (bf16[4,32,768]{2,1,0:T(8,128)(2,1)}, bf16[4,32,768]{2,1,0:T(8,128)(2,1)S(1)}, u32[]{:S(2)}, u32[]{:S(2)}) collective-permute-start(bf16[4,32,768]{2,1,0:T(8,128)(2,1)} %bitcast.43), channel_id=1, source_target_pairs={{0,4},{1,5},{2,6},{3,7},{4,0},{5,1},{6,2},{7,3},{8,12},{9,13},{10,... | collective-permute-start | bytes 589832 | tf_op jit(solution)/shard_map/ppermute | solution.py:383
  7.0 1.0 %copy-done.2 = bf16[32,16,512]{2,1,0:T(8,128)(2,1)S(1)} copy-done((bf16[32,16,512]{2,1,0:T(8,128)(2,1)S(1)}, bf16[32,16,512]{2,1,0:T(8,128)(2,1)}, u32[]{:S(2)}) %copy-start.2) | copy-done | bytes 524312
  8.1 9.3 %inner_slabs.1 = (bf16[128,768]{1,0:T(8,128)(2,1)S(1)}, bf16[128,768]{1,0:T(8,128)(2,1)S(1)}, bf16[128,768]{1,0:T(8,128)(2,1)S(1)}, bf16[128,768]{1,0:T(8,128)(2...) custom-call(bf16[32,16,512]{2,1,0:T(8,128)(2,1)S(1)} %copy-done.2, ...), custom_call_target="tpu_custom_call" | custom-call | flops 402653184 | bytes 25165824 | tf_op jit(solution)/shard_map/inner_slabs/pallas_call | solution.py:162
  17.4 1.5 %collective-permute-start.12 = (bf16[4,32,768]{2,1,0:T(8,128)(2,1)S(1)}, bf16[4,32,768]{2,1,0:T(8,128)(2,1)S(1)}, u32[]{:S(2)}, u32[]{:S(2)}) collective-permute-start(bf16[4,32,768]{2,1,0:T(8,128)(2,1)S(1)} %bitcast.39), channel_id=1, source_target_pairs={{0,8},{1,9},{2,10},{3,11},{4,12},{5,13},{6,14},{7,15},{8,0},{9,1},... | collective-permute-start | bytes 589832 | tf_op jit(solution)/shard_map/ppermute | solution.py:383
  19.1 2.0 %collective-permute-start.14 = (bf16[4,32,768]{2,1,0:T(8,128)(2,1)S(1)}, bf16[4,32,768]{2,1,0:T(8,128)(2,1)S(1)}, u32[]{:S(2)}, u32[]{:S(2)}) collective-permute-start(bf16[4,32,768]{2,1,0:T(8,128)(2,1)S(1)} %bitcast.37), channel_id=1, source_target_pairs={{0,4},{1,5},{2,6},{3,7},{4,0},{5,1},{6,2},{7,3},{8,12},{9,13},{10,... | collective-permute-start | bytes 589832 | tf_op jit(solution)/shard_map/ppermute | solution.py:383
  21.1 10.6 %collective-permute-done.1 = bf16[4,32,768]{2,1,0:T(8,128)(2,1)S(1)} collective-permute-done((bf16[4,32,768]{2,1,0:T(8,128)(2,1)}, bf16[4,32,768]{2,1,0:T(8,128)(2,1)S(1)}, u32[]{:S(2)}, u32[]{:S(2)}) %collective-permute-start.1) | collective-permute-done | bytes 196640 | tf_op jit(solution)/shard_map/ppermute | solution.py:383
  31.8 0.3 collective-permute-start.3
  32.2 2.8 %collective-permute-start.4 = (bf16[4,32,768]{2,1,0:T(8,128)(2,1)S(1)}, bf16[4,32,768]{2,1,0:T(8,128)(2,1)S(1)}, u32[]{:S(2)}, u32[]{:S(2)}) collective-permute-start(bf16[4,32,768]{2,1,0:T(8,128)(2,1)S(1)} %pad_maximum_fusion.2), channel_id=1, source_target_pairs={{0,3},{1,2},{2,1},{3,0},{4,7},{5,6},{6,5},{7,4},{8,11},{9,10},{10,... | collective-permute-start | bytes 589832 | tf_op jit(solution)/shard_map/ppermute | solution.py:383
  35.0 0.8 collective-permute-done.12
  35.8 0.6 collective-permute-start.5
  36.4 3.6 %collective-permute-done.13 = bf16[4,32,768]{2,1,0:T(8,128)(2,1)S(1)} collective-permute-done((bf16[4,32,768]{2,1,0:T(8,128)(2,1)S(1)}, bf16[4,32,768]{2,1,0:T(8,128)(2,1)S(1)}, u32[]{:S(2)}, u32[]{:S(2)}) %collective-permute-start.13) | collective-permute-done | bytes 196640 | tf_op jit(solution)/shard_map/ppermute | solution.py:383
  40.5 1.9 %collective-permute-start.16 = (bf16[4,32,768]{2,1,0:T(8,128)(2,1)S(1)}, bf16[4,32,768]{2,1,0:T(8,128)(2,1)S(1)}, u32[]{:S(2)}, u32[]{:S(2)}) collective-permute-start(bf16[4,32,768]{2,1,0:T(8,128)(2,1)S(1)} %pad_maximum_fusion.10), channel_id=1, source_target_pairs={{0,3},{1,2},{2,1},{3,0},{4,7},{5,6},{6,5},{7,4},{8,11},{9,10},{10,... | collective-permute-start | bytes 589832 | tf_op jit(solution)/shard_map/ppermute | solution.py:383
  42.8 0.7 back.1
  43.6 2.1 %collective-permute-start.7 = (bf16[4,32,768]{2,1,0:T(8,128)(2,1)S(1)}, bf16[4,32,768]{2,1,0:T(8,128)(2,1)S(1)}, u32[]{:S(2)}, u32[]{:S(2)}) collective-permute-start(bf16[4,32,768]{2,1,0:T(8,128)(2,1)S(1)} %get-tuple-element.53), channel_id=1, source_target_pairs={{0,12},{1,13},{2,14},{3,15},{4,8},{5,9},{6,10},{7,11},{8,4},{9,5},... | collective-permute-start | bytes 589832 | tf_op jit(solution)/shard_map/ppermute | solution.py:383
  45.7 0.7 collective-permute-done.15.refs_1_
  46.4 0.8 collective-permute-start.8
  47.2 4.2 %collective-permute-done.16.refs_2_ = bf16[4,32,768]{2,1,0:T(8,128)(2,1)S(1)} collective-permute-done((bf16[4,32,768]{2,1,0:T(8,128)(2,1)S(1)}, bf16[4,32,768]{2,1,0:T(8,128)(2,1)S(1)}, u32[]{:S(2)}, u32[]{:S(2)}) %collective-permute-start.16) | collective-permute-done | bytes 196640 | tf_op jit(solution)/shard_map/ppermute | solution.py:383
  51.5 0.7 forth.1
  52.2 0.3 collective-permute-start.18
  52.5 0.9 %collective-permute-start.19 = (bf16[4,32,768]{2,1,0:T(8,128)(2,1)S(1)}, bf16[4,32,768]{2,1,0:T(8,128)(2,1)S(1)}, u32[]{:S(2)}, u32[]{:S(2)}) collective-permute-start(bf16[4,32,768]{2,1,0:T(8,128)(2,1)S(1)} %get-tuple-element.64), channel_id=1, source_target_pairs={{0,3},{1,2},{2,1},{3,0},{4,7},{5,6},{6,5},{7,4},{8,11},{9,10},{10,... | collective-permute-start | bytes 589832 | tf_op jit(solution)/shard_map/ppermute | solution.py:383
  53.4 1.4 %fusion = bf16[1,512,512]{2,1,0:T(8,128)(2,1)} fusion(bf16[512,768]{1,0:T(8,128)(2,1)S(1)} %get-tuple-element.69, bf16[512,768]{1,0:T(8,128)(2,1)S(1)} %get-tuple-element.70), kind=kOutput, calls=%fused_computation.1 | convolution fusion | flops 402915328 | bytes 2097152 | tf_op jit(solution)/shard_map/dot_general | solution.py:71
  54.8 0.9 collective-permute-done.6
  55.7 1.8 %collective-permute-start.20 = (bf16[4,32,768]{2,1,0:T(8,128)(2,1)S(1)}, bf16[4,32,768]{2,1,0:T(8,128)(2,1)S(1)}, u32[]{:S(2)}, u32[]{:S(2)}) collective-permute-start(bf16[4,32,768]{2,1,0:T(8,128)(2,1)S(1)} %get-tuple-element.65), channel_id=1, source_target_pairs={{0,1},{1,0},{2,3},{3,2},{4,5},{5,4},{6,7},{7,6},{8,9},{9,8},{10,11... | collective-permute-start | bytes 589832 | tf_op jit(solution)/shard_map/ppermute | solution.py:383
  57.5 5.9 %collective-permute-done.7 = bf16[4,32,768]{2,1,0:T(8,128)(2,1)S(1)} collective-permute-done((bf16[4,32,768]{2,1,0:T(8,128)(2,1)S(1)}, bf16[4,32,768]{2,1,0:T(8,128)(2,1)S(1)}, u32[]{:S(2)}, u32[]{:S(2)}) %collective-permute-start.7) | collective-permute-done | bytes 196640 | tf_op jit(solution)/shard_map/ppermute | solution.py:383
  63.8 2.2 %collective-permute-start.10 = (bf16[4,32,768]{2,1,0:T(8,128)(2,1)S(1)}, bf16[4,32,768]{2,1,0:T(8,128)(2,1)S(1)}, u32[]{:S(2)}, u32[]{:S(2)}) collective-permute-start(bf16[4,32,768]{2,1,0:T(8,128)(2,1)S(1)} %pad_maximum_fusion.6), channel_id=1, source_target_pairs={{0,3},{1,2},{2,1},{3,0},{4,7},{5,6},{6,5},{7,4},{8,11},{9,10},{10,... | collective-permute-start | bytes 589832 | tf_op jit(solution)/shard_map/ppermute | solution.py:383
  66.5 2.7 %collective-permute-done.9.refs_3_ = bf16[4,32,768]{2,1,0:T(8,128)(2,1)S(1)} collective-permute-done((bf16[4,32,768]{2,1,0:T(8,128)(2,1)S(1)}, bf16[4,32,768]{2,1,0:T(8,128)(2,1)S(1)}, u32[]{:S(2)}, u32[]{:S(2)}) %collective-permute-start.9) | collective-permute-done | bytes 196640 | tf_op jit(solution)/shard_map/ppermute | solution.py:383
  69.2 0.9 collective-permute-start.23
  70.2 4.5 %collective-permute-done.10.refs_4_ = bf16[4,32,768]{2,1,0:T(8,128)(2,1)S(1)} collective-permute-done((bf16[4,32,768]{2,1,0:T(8,128)(2,1)S(1)}, bf16[4,32,768]{2,1,0:T(8,128)(2,1)S(1)}, u32[]{:S(2)}, u32[]{:S(2)}) %collective-permute-start.10) | collective-permute-done | bytes 196640 | tf_op jit(solution)/shard_map/ppermute | solution.py:383
  74.7 14.5 %grads.1 = (bf16[16384,768]{1,0:T(8,128)(2,1)}, bf16[32,16,512]{2,1,0:T(8,128)(2,1)}) custom-call(bf16[32,16,512]{2,1,0:T(8,128)(2,1)S(1)} %copy-done.2, bf16[512,512]{1,0:T(8,128)(2,1)S(1)} %get-tuple-element.41.matrix_ref, bf16[8192,768]{1,0:T(8,128)(2,1)S(1)} %get-tuple-element.42.refs_0_, bf16[8192,768]{1,0:T(8,128)(2,1)S(1)} %get-tuple-element.43.refs_1_, ...), custom_call_target="tpu_custom_call" | custom-call | flops 805306368 | bytes 25165824 | tf_op jit(solution)/shard_map/grads/pallas_call | solution.py:301
  89.3 1.6 %gates.1 = (bf16[512,768]{1,0:T(8,128)(2,1)}, bf16[512,768]{1,0:T(8,128)(2,1)}) custom-call(bf16[512,512]{1,0:T(8,128)(2,1)S(1)} %get-tuple-element.40.matrix_ref, bf16[512,768]{1,0:T(8,128)(2,1)S(1)} %bitcast.30, bf16[512,768]{1,0:T(8,128)(2,1)S(1)} %bitcast.32, bf16[128,768]{1,0:T(8,128)(2,1)S(1)} %bitcast.33, bf16[128,768]{1,0:T(8,128)(2,1)S(1)} %bitcast.34, ...), custom_call_target="tpu_custom_call" | custom-call | flops 402653184 | bytes 3932160 | tf_op jit(solution)/shard_map/gates/pallas_call | solution.py:349
  (63 shorter events, 2.1 us)
Async XLA Ops:
  0.6 42.2 %copy-start.3 = (bf16[1,512,512]{2,1,0:T(8,128)(2,1)S(1)}, bf16[1,512,512]{2,1,0:T(8,128)(2,1)}, u32[]{:S(2)}) copy-start(bf16[1,512,512]{2,1,0:T(8,128)(2,1)} %s_ref.3) | copy-start | bytes 1572868
  3.4 15.7 %collective-permute-start = (bf16[4,32,768]{2,1,0:T(8,128)(2,1)}, bf16[4,32,768]{2,1,0:T(8,128)(2,1)S(1)}, u32[]{:S(2)}, u32[]{:S(2)}) collective-permute-start(bf16[4,32,768]{2,1,0:T(8,128)(2,1)} %bitcast.45), channel_id=1, source_target_pairs={{0,8},{1,9},{2,10},{3,11},{4,12},{5,13},{6,14},{7,15},{8,0},{9,1},... | collective-permute-start | bytes 589832 | tf_op jit(solution)/shard_map/ppermute | solution.py:383
  5.8 25.9 %collective-permute-start.1 = (bf16[4,32,768]{2,1,0:T(8,128)(2,1)}, bf16[4,32,768]{2,1,0:T(8,128)(2,1)S(1)}, u32[]{:S(2)}, u32[]{:S(2)}) collective-permute-start(bf16[4,32,768]{2,1,0:T(8,128)(2,1)} %bitcast.44), channel_id=1, source_target_pairs={{0,12},{1,13},{2,14},{3,15},{4,8},{5,9},{6,10},{7,11},{8,4},{9,5},... | collective-permute-start | bytes 589832 | tf_op jit(solution)/shard_map/ppermute | solution.py:383
  5.8 25.9 %collective-permute-start.2 = (bf16[4,32,768]{2,1,0:T(8,128)(2,1)}, bf16[4,32,768]{2,1,0:T(8,128)(2,1)S(1)}, u32[]{:S(2)}, u32[]{:S(2)}) collective-permute-start(bf16[4,32,768]{2,1,0:T(8,128)(2,1)} %bitcast.43), channel_id=1, source_target_pairs={{0,4},{1,5},{2,6},{3,7},{4,0},{5,1},{6,2},{7,3},{8,12},{9,13},{10,... | collective-permute-start | bytes 589832 | tf_op jit(solution)/shard_map/ppermute | solution.py:383
  7.0 1.0 %copy-start.2 = (bf16[32,16,512]{2,1,0:T(8,128)(2,1)S(1)}, bf16[32,16,512]{2,1,0:T(8,128)(2,1)}, u32[]{:S(2)}) copy-start(bf16[32,16,512]{2,1,0:T(8,128)(2,1)} %w_ref.2) | copy-start | bytes 1572868
  8.1 23.6 %copy-start.4 = (bf16[128,768]{1,0:T(8,128)(2,1)S(1)}, bf16[128,768]{1,0:T(8,128)(2,1)}, u32[]{:S(2)}) copy-start(bf16[128,768]{1,0:T(8,128)(2,1)} %get-tuple-element.38) | copy-start | bytes 589828
  17.4 71.9 %copy-start = (bf16[32,16,768]{2,1,0:T(8,128)(2,1)S(1)}, bf16[32,16,768]{2,1,0:T(8,128)(2,1)}, u32[]{:S(2)}) copy-start(bf16[32,16,768]{2,1,0:T(8,128)(2,1)} %param.6) | copy-start | bytes 2359300
  17.4 71.9 %copy-start.1 = (bf16[32,16,768]{2,1,0:T(8,128)(2,1)S(1)}, bf16[32,16,768]{2,1,0:T(8,128)(2,1)}, u32[]{:S(2)}) copy-start(bf16[32,16,768]{2,1,0:T(8,128)(2,1)} %param.7) | copy-start | bytes 2359300
  17.4 18.4 %collective-permute-start.12 = (bf16[4,32,768]{2,1,0:T(8,128)(2,1)S(1)}, bf16[4,32,768]{2,1,0:T(8,128)(2,1)S(1)}, u32[]{:S(2)}, u32[]{:S(2)}) collective-permute-start(bf16[4,32,768]{2,1,0:T(8,128)(2,1)S(1)} %bitcast.39), channel_id=1, source_target_pairs={{0,8},{1,9},{2,10},{3,11},{4,12},{5,13},{6,14},{7,15},{8,0},{9,1},... | collective-permute-start | bytes 589832 | tf_op jit(solution)/shard_map/ppermute | solution.py:383
  18.9 21.2 %collective-permute-start.13 = (bf16[4,32,768]{2,1,0:T(8,128)(2,1)S(1)}, bf16[4,32,768]{2,1,0:T(8,128)(2,1)S(1)}, u32[]{:S(2)}, u32[]{:S(2)}) collective-permute-start(bf16[4,32,768]{2,1,0:T(8,128)(2,1)S(1)} %bitcast.38), channel_id=1, source_target_pairs={{0,12},{1,13},{2,14},{3,15},{4,8},{5,9},{6,10},{7,11},{8,4},{9,5},... | collective-permute-start | bytes 589832 | tf_op jit(solution)/shard_map/ppermute | solution.py:383
  19.1 21.0 %collective-permute-start.14 = (bf16[4,32,768]{2,1,0:T(8,128)(2,1)S(1)}, bf16[4,32,768]{2,1,0:T(8,128)(2,1)S(1)}, u32[]{:S(2)}, u32[]{:S(2)}) collective-permute-start(bf16[4,32,768]{2,1,0:T(8,128)(2,1)S(1)} %bitcast.37), channel_id=1, source_target_pairs={{0,4},{1,5},{2,6},{3,7},{4,0},{5,1},{6,2},{7,3},{8,12},{9,13},{10,... | collective-permute-start | bytes 589832 | tf_op jit(solution)/shard_map/ppermute | solution.py:383
  31.8 10.7 %collective-permute-start.3 = (bf16[4,32,768]{2,1,0:T(8,128)(2,1)S(1)}, bf16[4,32,768]{2,1,0:T(8,128)(2,1)S(1)}, u32[]{:S(2)}, u32[]{:S(2)}) collective-permute-start(bf16[4,32,768]{2,1,0:T(8,128)(2,1)S(1)} %pad_maximum_fusion.1), channel_id=1, source_target_pairs={{0,2},{1,3},{2,0},{3,1},{4,6},{5,7},{6,4},{7,5},{8,10},{9,11},{10,... | collective-permute-start | bytes 589832 | tf_op jit(solution)/shard_map/ppermute | solution.py:383
  32.2 10.6 %collective-permute-start.4 = (bf16[4,32,768]{2,1,0:T(8,128)(2,1)S(1)}, bf16[4,32,768]{2,1,0:T(8,128)(2,1)S(1)}, u32[]{:S(2)}, u32[]{:S(2)}) collective-permute-start(bf16[4,32,768]{2,1,0:T(8,128)(2,1)S(1)} %pad_maximum_fusion.2), channel_id=1, source_target_pairs={{0,3},{1,2},{2,1},{3,0},{4,7},{5,6},{6,5},{7,4},{8,11},{9,10},{10,... | collective-permute-start | bytes 589832 | tf_op jit(solution)/shard_map/ppermute | solution.py:383
  35.8 7.0 %collective-permute-start.5 = (bf16[4,32,768]{2,1,0:T(8,128)(2,1)S(1)}, bf16[4,32,768]{2,1,0:T(8,128)(2,1)S(1)}, u32[]{:S(2)}, u32[]{:S(2)}) collective-permute-start(bf16[4,32,768]{2,1,0:T(8,128)(2,1)S(1)} %pad_maximum_fusion.3), channel_id=1, source_target_pairs={{0,1},{1,0},{2,3},{3,2},{4,5},{5,4},{6,7},{7,6},{8,9},{9,8},{10,11... | collective-permute-start | bytes 589832 | tf_op jit(solution)/shard_map/ppermute | solution.py:383
  40.1 6.3 %collective-permute-start.15 = (bf16[4,32,768]{2,1,0:T(8,128)(2,1)S(1)}, bf16[4,32,768]{2,1,0:T(8,128)(2,1)S(1)}, u32[]{:S(2)}, u32[]{:S(2)}) collective-permute-start(bf16[4,32,768]{2,1,0:T(8,128)(2,1)S(1)} %pad_maximum_fusion.9), channel_id=1, source_target_pairs={{0,2},{1,3},{2,0},{3,1},{4,6},{5,7},{6,4},{7,5},{8,10},{9,11},{10,... | collective-permute-start | bytes 589832 | tf_op jit(solution)/shard_map/ppermute | solution.py:383
  40.5 11.0 %collective-permute-start.16 = (bf16[4,32,768]{2,1,0:T(8,128)(2,1)S(1)}, bf16[4,32,768]{2,1,0:T(8,128)(2,1)S(1)}, u32[]{:S(2)}, u32[]{:S(2)}) collective-permute-start(bf16[4,32,768]{2,1,0:T(8,128)(2,1)S(1)} %pad_maximum_fusion.10), channel_id=1, source_target_pairs={{0,3},{1,2},{2,1},{3,0},{4,7},{5,6},{6,5},{7,4},{8,11},{9,10},{10,... | collective-permute-start | bytes 589832 | tf_op jit(solution)/shard_map/ppermute | solution.py:383
  42.5 8.9 %collective-permute-start.17 = (bf16[4,32,768]{2,1,0:T(8,128)(2,1)S(1)}, bf16[4,32,768]{2,1,0:T(8,128)(2,1)S(1)}, u32[]{:S(2)}, u32[]{:S(2)}) collective-permute-start(bf16[4,32,768]{2,1,0:T(8,128)(2,1)S(1)} %pad_maximum_fusion.11), channel_id=1, source_target_pairs={{0,1},{1,0},{2,3},{3,2},{4,5},{5,4},{6,7},{7,6},{8,9},{9,8},{10,11... | collective-permute-start | bytes 589832 | tf_op jit(solution)/shard_map/ppermute | solution.py:383
  43.5 12.2 %collective-permute-start.6 = (bf16[4,32,768]{2,1,0:T(8,128)(2,1)S(1)}, bf16[4,32,768]{2,1,0:T(8,128)(2,1)S(1)}, u32[]{:S(2)}, u32[]{:S(2)}) collective-permute-start(bf16[4,32,768]{2,1,0:T(8,128)(2,1)S(1)} %get-tuple-element.52), channel_id=1, source_target_pairs={{0,8},{1,9},{2,10},{3,11},{4,12},{5,13},{6,14},{7,15},{8,0},{9,1},... | collective-permute-start | bytes 589832 | tf_op jit(solution)/shard_map/ppermute | solution.py:383
  43.6 19.8 %collective-permute-start.7 = (bf16[4,32,768]{2,1,0:T(8,128)(2,1)S(1)}, bf16[4,32,768]{2,1,0:T(8,128)(2,1)S(1)}, u32[]{:S(2)}, u32[]{:S(2)}) collective-permute-start(bf16[4,32,768]{2,1,0:T(8,128)(2,1)S(1)} %get-tuple-element.53), channel_id=1, source_target_pairs={{0,12},{1,13},{2,14},{3,15},{4,8},{5,9},{6,10},{7,11},{8,4},{9,5},... | collective-permute-start | bytes 589832 | tf_op jit(solution)/shard_map/ppermute | solution.py:383
  46.4 17.0 %collective-permute-start.8 = (bf16[4,32,768]{2,1,0:T(8,128)(2,1)S(1)}, bf16[4,32,768]{2,1,0:T(8,128)(2,1)S(1)}, u32[]{:S(2)}, u32[]{:S(2)}) collective-permute-start(bf16[4,32,768]{2,1,0:T(8,128)(2,1)S(1)} %get-tuple-element.54), channel_id=1, source_target_pairs={{0,4},{1,5},{2,6},{3,7},{4,0},{5,1},{6,2},{7,3},{8,12},{9,13},{10,... | collective-permute-start | bytes 589832 | tf_op jit(solution)/shard_map/ppermute | solution.py:383
  52.2 13.9 %collective-permute-start.18 = (bf16[4,32,768]{2,1,0:T(8,128)(2,1)S(1)}, bf16[4,32,768]{2,1,0:T(8,128)(2,1)S(1)}, u32[]{:S(2)}, u32[]{:S(2)}) collective-permute-start(bf16[4,32,768]{2,1,0:T(8,128)(2,1)S(1)} %get-tuple-element.63), channel_id=1, source_target_pairs={{0,2},{1,3},{2,0},{3,1},{4,6},{5,7},{6,4},{7,5},{8,10},{9,11},{10,... | collective-permute-start | bytes 589832 | tf_op jit(solution)/shard_map/ppermute | solution.py:383
  52.5 13.7 %collective-permute-start.19 = (bf16[4,32,768]{2,1,0:T(8,128)(2,1)S(1)}, bf16[4,32,768]{2,1,0:T(8,128)(2,1)S(1)}, u32[]{:S(2)}, u32[]{:S(2)}) collective-permute-start(bf16[4,32,768]{2,1,0:T(8,128)(2,1)S(1)} %get-tuple-element.64), channel_id=1, source_target_pairs={{0,3},{1,2},{2,1},{3,0},{4,7},{5,6},{6,5},{7,4},{8,11},{9,10},{10,... | collective-permute-start | bytes 589832 | tf_op jit(solution)/shard_map/ppermute | solution.py:383
  55.7 10.5 %collective-permute-start.20 = (bf16[4,32,768]{2,1,0:T(8,128)(2,1)S(1)}, bf16[4,32,768]{2,1,0:T(8,128)(2,1)S(1)}, u32[]{:S(2)}, u32[]{:S(2)}) collective-permute-start(bf16[4,32,768]{2,1,0:T(8,128)(2,1)S(1)} %get-tuple-element.65), channel_id=1, source_target_pairs={{0,1},{1,0},{2,3},{3,2},{4,5},{5,4},{6,7},{7,6},{8,9},{9,8},{10,11... | collective-permute-start | bytes 589832 | tf_op jit(solution)/shard_map/ppermute | solution.py:383
  63.5 5.7 %collective-permute-start.9 = (bf16[4,32,768]{2,1,0:T(8,128)(2,1)S(1)}, bf16[4,32,768]{2,1,0:T(8,128)(2,1)S(1)}, u32[]{:S(2)}, u32[]{:S(2)}) collective-permute-start(bf16[4,32,768]{2,1,0:T(8,128)(2,1)S(1)} %pad_maximum_fusion.5), channel_id=1, source_target_pairs={{0,2},{1,3},{2,0},{3,1},{4,6},{5,7},{6,4},{7,5},{8,10},{9,11},{10,... | collective-permute-start | bytes 589832 | tf_op jit(solution)/shard_map/ppermute | solution.py:383
  63.8 10.9 %collective-permute-start.10 = (bf16[4,32,768]{2,1,0:T(8,128)(2,1)S(1)}, bf16[4,32,768]{2,1,0:T(8,128)(2,1)S(1)}, u32[]{:S(2)}, u32[]{:S(2)}) collective-permute-start(bf16[4,32,768]{2,1,0:T(8,128)(2,1)S(1)} %pad_maximum_fusion.6), channel_id=1, source_target_pairs={{0,3},{1,2},{2,1},{3,0},{4,7},{5,6},{6,5},{7,4},{8,11},{9,10},{10,... | collective-permute-start | bytes 589832 | tf_op jit(solution)/shard_map/ppermute | solution.py:383
  66.1 8.6 %collective-permute-start.11 = (bf16[4,32,768]{2,1,0:T(8,128)(2,1)S(1)}, bf16[4,32,768]{2,1,0:T(8,128)(2,1)S(1)}, u32[]{:S(2)}, u32[]{:S(2)}) collective-permute-start(bf16[4,32,768]{2,1,0:T(8,128)(2,1)S(1)} %pad_maximum_fusion.7), channel_id=1, source_target_pairs={{0,1},{1,0},{2,3},{3,2},{4,5},{5,4},{6,7},{7,6},{8,9},{9,8},{10,11... | collective-permute-start | bytes 589832 | tf_op jit(solution)/shard_map/ppermute | solution.py:383
  66.3 23.0 %collective-permute-start.21 = (bf16[4,32,768]{2,1,0:T(8,128)(2,1)S(1)}, bf16[4,32,768]{2,1,0:T(8,128)(2,1)S(1)}, u32[]{:S(2)}, u32[]{:S(2)}) collective-permute-start(bf16[4,32,768]{2,1,0:T(8,128)(2,1)S(1)} %pad_maximum_fusion.13), channel_id=1, source_target_pairs={{0,8},{1,9},{2,10},{3,11},{4,12},{5,13},{6,14},{7,15},{8,0},{9,1},... | collective-permute-start | bytes 589832 | tf_op jit(solution)/shard_map/ppermute | solution.py:383
  66.4 22.9 %collective-permute-start.22 = (bf16[4,32,768]{2,1,0:T(8,128)(2,1)S(1)}, bf16[4,32,768]{2,1,0:T(8,128)(2,1)S(1)}, u32[]{:S(2)}, u32[]{:S(2)}) collective-permute-start(bf16[4,32,768]{2,1,0:T(8,128)(2,1)S(1)} %pad_maximum_fusion.14), channel_id=1, source_target_pairs={{0,12},{1,13},{2,14},{3,15},{4,8},{5,9},{6,10},{7,11},{8,4},{9,5},... | collective-permute-start | bytes 589832 | tf_op jit(solution)/shard_map/ppermute | solution.py:383
  69.2 20.0 %collective-permute-start.23 = (bf16[4,32,768]{2,1,0:T(8,128)(2,1)S(1)}, bf16[4,32,768]{2,1,0:T(8,128)(2,1)S(1)}, u32[]{:S(2)}, u32[]{:S(2)}) collective-permute-start(bf16[4,32,768]{2,1,0:T(8,128)(2,1)S(1)} %pad_maximum_fusion.15), channel_id=1, source_target_pairs={{0,4},{1,5},{2,6},{3,7},{4,0},{5,1},{6,2},{7,3},{8,12},{9,13},{10,... | collective-permute-start | bytes 589832 | tf_op jit(solution)/shard_map/ppermute | solution.py:383
